TPU v7x, 32 devices: a whole 2x2x4 slice. The times are simulated.
32 devices in a mesh: seq: 16 (over z, y, x), head: 2 (over core).
Axes of the slice: x: 2, y: 2, z: 4, core: 2. Of those that a mesh axis runs over, the one named last changes fastest.
Arguments:
- tokens: bfloat16 [4096, 2048], P('seq'), may hold values from -6 to 6
- cotangent: bfloat16 [4096, 2048], P('seq'), may hold values from -6 to 6
- g1: bfloat16 [2048], P('seq'), may hold values from 0.5 to 1.5
- w_q: bfloat16 [2048, 1024], P('seq', 'head'), may hold values from -0.125 to 0.125
- w_k: bfloat16 [2048, 256], P('seq', 'head'), may hold values from -0.125 to 0.125
- w_v: bfloat16 [2048, 256], P('seq', 'head'), may hold values from -0.125 to 0.125
- w_o: bfloat16 [1024, 2048], P('head', 'seq'), may hold values from -3 to 3
- w_z: bfloat16 [2048, 3072], P('seq', 'head'), may hold values from -0.125 to 0.125
- w_x: bfloat16 [2048, 3072], P('seq', 'head'), may hold values from -0.125 to 0.125
- w_bc: bfloat16 [2048, 512], P('seq'), may hold values from -0.125 to 0.125
- w_dt: bfloat16 [2048, 48], P('seq', 'head'), may hold values from -0.125 to 0.125
- conv_bc: bfloat16 [4, 512], P(None, 'seq'), may hold values from -3 to 3
- conv_bc_bias: bfloat16 [512], P('seq'), may hold values from -3 to 3
- w_out: bfloat16 [3072, 2048], P('head', 'seq'), may hold values from -0.013671875 to 0.013671875
- g2: bfloat16 [2048], P('seq'), may hold values from 0.5 to 1.5
- w_gate: bfloat16 [2048, 4096], P('seq', 'head'), may hold values from -0.125 to 0.125
- w_up: bfloat16 [2048, 4096], P('seq', 'head'), may hold values from -0.125 to 0.125
- w_down: bfloat16 [4096, 2048], P('head', 'seq'), may hold values from -0.09375 to 0.09375
- conv_x: bfloat16 [4, 3072], P(None, 'head'), may hold values from -3 to 3
- conv_x_bias: bfloat16 [3072], P('head'), may hold values from -3 to 3
- dt_bias: bfloat16 [48], P('head'), may hold values from -8 to -3
- a_log: bfloat16 [48], P('head'), may hold values from -2 to 2
- d_skip: bfloat16 [48], P('head'), may hold values from 0.5 to 1.5
Outputs:
- output: bfloat16 [4096, 2048], P('seq')
- grad_tokens: float32 [4096, 2048], P('seq')
- grad_g1: float32 [2048], P('seq')
- grad_w_q: float32 [2048, 1024], P('seq', 'head')
- grad_w_k: float32 [2048, 256], P('seq', 'head')
- grad_w_v: float32 [2048, 256], P('seq', 'head')
- grad_w_o: float32 [1024, 2048], P('head', 'seq')
- grad_w_z: float32 [2048, 3072], P('seq', 'head')
- grad_w_x: float32 [2048, 3072], P('seq', 'head')
- grad_w_bc: float32 [2048, 512], P('seq')
- grad_w_dt: float32 [2048, 48], P('seq', 'head')
- grad_conv_bc: float32 [4, 512], P(None, 'seq')
- grad_conv_bc_bias: float32 [512], P('seq')
- grad_w_out: float32 [3072, 2048], P('head', 'seq')
- grad_g2: float32 [2048], P('seq')
- grad_w_gate: float32 [2048, 4096], P('seq', 'head')
- grad_w_up: float32 [2048, 4096], P('seq', 'head')
- grad_w_down: float32 [4096, 2048], P('head', 'seq')
- grad_conv_x: float32 [4, 3072], P(None, 'head')
- grad_conv_x_bias: float32 [3072], P('head')
- grad_dt_bias: float32 [48], P('head')
- grad_a_log: float32 [48], P('head')
- grad_d_skip: float32 [48], P('head')
All inputs are finite; a program needn't handle non-finite values.
Results may differ from a plain program's by a relative error of at most 0.017.
Values may be sent and summed in bfloat16 or wider, within the bound.
No kernel may reach another device: no remote copies, remote signals or barrier semaphores. Data moves between devices by JAX's collectives and lax.ppermute only.
A program may use at most 320 MiB of HBM per device.

v0:
```python
import math

import jax
import jax.numpy as jnp
from jax import lax
from jax.sharding import PartitionSpec as P

HEAD_DIM = 128
STATE = 256
CONV = 4


EPS = 1e-05
ROPE_BASE = 100000000000.0
MASKED = -1e30
HIGHEST = lax.Precision.HIGHEST


def passed_along(block, axis, distance):
    devices = range(lax.axis_size(axis))
    route = [(i - distance, i) for i in devices if i - distance in devices]
    return lax.ppermute(block, axis, route)


def entering(part, axis, combine, identity):
    place = lax.axis_index(axis)
    gathered = jax.tree.map(lambda a: lax.all_gather(a, axis), part)
    state = jax.tree.map(lambda a, e: jnp.zeros_like(a) + jnp.asarray(e, a.dtype), part, identity)

    def one(turn, state):
        return combine(
            state, jax.tree.map(lambda a: lax.dynamic_index_in_dim(a, turn, 0, False), gathered)
        )

    return lax.fori_loop(0, place, one, state)


def cut_along(x, dim, peers):
    before, after = (x.shape[:dim], x.shape[dim + 1 :])
    return jnp.moveaxis(x.reshape(*before, peers, -1, *after), dim, 0)


def sum_at_owner(x, axis, dim):
    peers = lax.axis_size(axis)
    parts = lax.all_to_all(cut_along(x, dim, peers), axis, 0, 0, tiled=True)
    return jnp.sum(parts.astype(jnp.float32), axis=0)


def side_by_side(arrays, axis, dim, along):
    ends, at = ([], 0)
    for a in arrays[:-1]:
        at += a.shape[along]
        ends.append(at)
    both = jnp.concatenate(arrays, axis=along)
    return tuple(jnp.split(sum_at_owner(both, axis, dim), ends, axis=along))


def entering_2(x, axis, combine, identity):
    peers, mine = (lax.axis_size(axis), lax.axis_index(axis))
    everything = jax.tree.map(
        lambda part, kind: lax.all_gather(part.astype(kind), axis),
        x,
        jax.tree.map(lambda a: jnp.bfloat16 if a.dtype == jnp.float32 else a.dtype, x),
    )
    start = jax.tree.map(
        lambda part, zero: jnp.broadcast_to(jnp.asarray(zero, part.dtype), part.shape), x, identity
    )

    def turn(k, before):
        at = peers - 1 - k
        reached = at > mine
        new = combine(
            before, jax.tree.map(lambda part, own: part[at].astype(own.dtype), everything, x)
        )
        return jax.tree.map(lambda a, b: jnp.where(reached, a, b), new, before)

    return lax.fori_loop(0, peers, turn, start)


def matmul_low(left, right):
    return jnp.dot(left, right, preferred_element_type=jnp.float32)


def matmul_left(left, right):
    return lax.dot_general(
        left, right, (((0,), (0,)), ((), ())), preferred_element_type=jnp.float32
    )


def matmul_right(left, right):
    return lax.dot_general(
        left, right, (((1,), (1,)), ((), ())), preferred_element_type=jnp.float32
    )


def matmul_high(left, right):
    return jnp.dot(left, right, precision=HIGHEST)


def normalize(values, gain):
    factor = lax.rsqrt(jnp.mean(values * values, -1, keepdims=True) + EPS)
    unit = values * factor
    return (unit * gain, unit, factor)


def norm_back(grad_out, unit, factor, gain):
    grad_unit = grad_out * gain[None, :]
    grad_in = factor * (grad_unit - unit * jnp.mean(grad_unit * unit, -1, keepdims=True))
    return (grad_in, jnp.sum(grad_out * unit, 0))


def rotate(values, positions, sign):
    half = values.shape[-1] // 2
    freqs = ROPE_BASE ** (-jnp.arange(half, dtype=jnp.float32) / half)
    angle = sign * positions.astype(jnp.float32)[:, None] * freqs[None, :]
    cosine = jnp.cos(angle)[:, None, :]
    sine = jnp.sin(angle)[:, None, :]
    first = values[..., :half]
    second = values[..., half:]
    return jnp.concatenate([first * cosine - second * sine, second * cosine + first * sine], -1)


def edge_conv(inputs, edge, weight, bias):
    length = inputs.shape[0]
    padded = jnp.concatenate([edge, inputs], 0)
    total = bias[None, :]
    for tap in range(CONV):
        total = total + weight[tap][None, :] * padded[tap : tap + length]
    return total


def prepare(
    x_proj,
    bc_proj,
    dt_proj,
    x_edge,
    bc_edge,
    conv_x,
    conv_x_bias,
    conv_bc,
    conv_bc_bias,
    dt_bias,
    a_log,
):
    length = x_proj.shape[0]
    xc = jax.nn.silu(edge_conv(x_proj, x_edge, conv_x, conv_x_bias))
    bc = jax.nn.silu(edge_conv(bc_proj, bc_edge, conv_bc, conv_bc_bias))
    dt = jax.nn.softplus(dt_proj + dt_bias[None, :])
    logs = -dt * jnp.exp(a_log)[None, :]
    return (xc.reshape(length, dt.shape[1], -1), bc[:, :STATE], bc[:, STATE:], dt, logs)


def span_state(xc, bmat, dt, logs):
    cum = jnp.cumsum(logs, 0)
    tail = jnp.exp(cum[-1][None, :] - cum) * dt
    local = jnp.einsum("sh,shp,sn->hpn", tail, xc, bmat, precision=HIGHEST)
    return (local, jnp.exp(cum[-1]))


def span_output(xc, bmat, cmat, dt, logs, state_in, d_skip):
    length = xc.shape[0]
    cum = jnp.cumsum(logs, 0)
    diff = cum[:, None, :] - cum[None, :, :]
    order = jnp.arange(length)
    causal = (order[:, None] >= order[None, :])[:, :, None]
    decay = jnp.exp(jnp.where(causal, diff, MASKED))
    inner = matmul_high(cmat, bmat.T)
    mixing = decay * inner[:, :, None] * dt[None, :, :]
    within = jnp.einsum("tsh,shp->thp", mixing, xc, precision=HIGHEST)
    carried = jnp.exp(cum)[:, :, None] * jnp.einsum(
        "tn,hpn->thp", cmat, state_in, precision=HIGHEST
    )
    return within + carried + d_skip[None, :, None] * xc


def gated_output(xc, bmat, cmat, dt, logs, z_proj, state_in, d_skip):
    outputs = span_output(xc, bmat, cmat, dt, logs, state_in, d_skip)
    return outputs.reshape(xc.shape[0], -1) * jax.nn.silu(z_proj)


def chain(earlier, later):
    return (later[1][:, None, None] * earlier[0] + later[0], earlier[1] * later[1])


def key_blocks(all_keys, all_values):
    total = all_keys.shape[0]
    block = math.gcd(total, 1024)
    count = total // block
    return (all_keys.reshape(count, block, -1), all_values.reshape(count, block, -1), block, count)


def masked_scores(queries, query_pos, key_block, index, block):
    key_pos = index * block + jnp.arange(block)
    scores = matmul_right(queries, key_block) * HEAD_DIM ** (-0.5)
    return jnp.where(key_pos[None, :] <= query_pos[:, None], scores, MASKED)


def attend_forward(queries, query_pos, all_keys, all_values):
    keyed, valued, block, count = key_blocks(all_keys, all_values)
    height = queries.shape[0]

    def stats_step(carry, item):
        top, mass = carry
        key_block, index = item
        scores = masked_scores(queries, query_pos, key_block, index, block)
        new_top = jnp.maximum(top, jnp.max(scores, 1))
        mass = mass * jnp.exp(top - new_top) + jnp.sum(jnp.exp(scores - new_top[:, None]), 1)
        return ((new_top, mass), None)

    start = (jnp.full((height,), MASKED, jnp.float32), jnp.zeros((height,), jnp.float32))
    (top, mass), _ = lax.scan(stats_step, start, (keyed, jnp.arange(count)))
    lse = top + jnp.log(mass)

    def value_step(accum, item):
        key_block, value_block, index = item
        probs = jnp.exp(masked_scores(queries, query_pos, key_block, index, block) - lse[:, None])
        return (accum + matmul_low(probs.astype(jnp.bfloat16), value_block), None)

    accum, _ = lax.scan(
        value_step,
        jnp.zeros((height, queries.shape[1]), jnp.float32),
        (keyed, valued, jnp.arange(count)),
    )
    return (accum, lse)


def attend_backward(queries, query_pos, all_keys, all_values, grad_flat, lse, delta):
    keyed, valued, block, count = key_blocks(all_keys, all_values)

    def grad_step(grad_query, item):
        key_block, value_block, index = item
        probs = jnp.exp(masked_scores(queries, query_pos, key_block, index, block) - lse[:, None])
        grad_probs = matmul_right(grad_flat, value_block)
        grad_scores = (probs * (grad_probs - delta[:, None])).astype(jnp.bfloat16)
        grad_query = grad_query + matmul_low(grad_scores, key_block)
        key_part = matmul_left(grad_scores, queries) * HEAD_DIM ** (-0.5)
        value_part = matmul_left(probs.astype(jnp.bfloat16), grad_flat)
        return (grad_query, (key_part, value_part))

    start = jnp.zeros(queries.shape, jnp.float32)
    grad_query, (key_parts, value_parts) = lax.scan(
        grad_step, start, (keyed, valued, jnp.arange(count))
    )
    return (
        grad_query * HEAD_DIM ** (-0.5),
        key_parts.reshape(-1, queries.shape[1]),
        value_parts.reshape(-1, queries.shape[1]),
    )


def reduce_mlp(gain_grad, gate_grad, up_grad, down_grad):
    return (
        lax.psum_scatter(gain_grad, "seq", scatter_dimension=0, tiled=True),
        lax.psum_scatter(gate_grad, "seq", scatter_dimension=0, tiled=True),
        lax.psum_scatter(up_grad, "seq", scatter_dimension=0, tiled=True),
        lax.psum_scatter(down_grad, "seq", scatter_dimension=1, tiled=True),
    )


def per_device(
    tokens,
    cotangent,
    g1,
    w_q,
    w_k,
    w_v,
    w_o,
    w_z,
    w_x,
    w_bc,
    w_dt,
    conv_bc,
    conv_bc_bias,
    w_out,
    g2,
    w_gate,
    w_up,
    w_down,
    conv_x,
    conv_x_bias,
    dt_bias,
    a_log,
    d_skip,
):
    f32 = jnp.float32
    b16 = jnp.bfloat16
    (
        full_g1,
        full_q,
        full_k,
        full_v,
        full_o,
        full_z,
        full_x,
        full_bc,
        full_dt,
        full_cbc,
        full_cbcb,
        full_out,
        full_g2,
        full_gate,
        full_up,
        full_down,
    ) = (
        lax.all_gather(g1, "seq", axis=0, tiled=True),
        lax.all_gather(w_q, "seq", axis=0, tiled=True),
        lax.all_gather(w_k, "seq", axis=0, tiled=True),
        lax.all_gather(w_v, "seq", axis=0, tiled=True),
        lax.all_gather(w_o, "seq", axis=1, tiled=True),
        lax.all_gather(w_z, "seq", axis=0, tiled=True),
        lax.all_gather(w_x, "seq", axis=0, tiled=True),
        lax.all_gather(w_bc, "seq", axis=0, tiled=True),
        lax.all_gather(w_dt, "seq", axis=0, tiled=True),
        lax.all_gather(conv_bc, "seq", axis=1, tiled=True),
        lax.all_gather(conv_bc_bias, "seq", axis=0, tiled=True),
        lax.all_gather(w_out, "seq", axis=1, tiled=True),
        lax.all_gather(g2, "seq", axis=0, tiled=True),
        lax.all_gather(w_gate, "seq", axis=0, tiled=True),
        lax.all_gather(w_up, "seq", axis=0, tiled=True),
        lax.all_gather(w_down, "seq", axis=1, tiled=True),
    )
    tokens32 = tokens.astype(f32)
    length = tokens32.shape[0]
    positions = lax.axis_index("seq") * length + jnp.arange(length)
    gain1 = full_g1.astype(f32)
    gain2 = full_g2.astype(f32)
    normed1, unit1, factor1 = normalize(tokens32, gain1)
    n1 = normed1.astype(b16)
    q_proj = matmul_low(n1, full_q)
    k_proj = matmul_low(n1, full_k)
    value_rows = matmul_low(n1, full_v).astype(b16)
    local_heads = q_proj.shape[1] // HEAD_DIM
    queries = rotate(q_proj.reshape(length, local_heads, HEAD_DIM), positions, 1.0).astype(b16)
    query_flat = queries.transpose(1, 0, 2).reshape(-1, HEAD_DIM)
    query_pos = jnp.tile(positions, local_heads)
    key_rows = (
        rotate(k_proj.reshape(length, 1, HEAD_DIM), positions, 1.0)
        .reshape(length, HEAD_DIM)
        .astype(b16)
    )
    all_keys, all_values = (
        lax.all_gather(key_rows, "seq", axis=0, tiled=True),
        lax.all_gather(value_rows, "seq", axis=0, tiled=True),
    )
    accum, lse = attend_forward(query_flat, query_pos, all_keys, all_values)
    attended = (
        accum.reshape(local_heads, length, HEAD_DIM)
        .transpose(1, 0, 2)
        .reshape(length, -1)
        .astype(b16)
    )
    z_proj = matmul_low(n1, full_z)
    x_proj = matmul_low(n1, full_x)
    bc_proj = matmul_low(n1, full_bc)
    dt_proj = matmul_low(n1, full_dt)
    width = CONV - 1
    x_edge, bc_edge = passed_along((x_proj[length - width :], bc_proj[length - width :]), "seq", 1)
    conv_x32 = conv_x.astype(f32)
    conv_xb32 = conv_x_bias.astype(f32)
    conv_bc32 = full_cbc.astype(f32)
    conv_bcb32 = full_cbcb.astype(f32)
    dt_bias32 = dt_bias.astype(f32)
    a_log32 = a_log.astype(f32)
    d_skip32 = d_skip.astype(f32)
    xc, bmat, cmat, steps, logs = prepare(
        x_proj,
        bc_proj,
        dt_proj,
        x_edge,
        bc_edge,
        conv_x32,
        conv_xb32,
        conv_bc32,
        conv_bcb32,
        dt_bias32,
        a_log32,
    )
    local_state, decay_total = span_state(xc, bmat, steps, logs)
    state_in, _ = entering(
        (local_state, decay_total),
        "seq",
        chain,
        (jnp.zeros_like(local_state), jnp.ones_like(decay_total)),
    )
    gated = gated_output(xc, bmat, cmat, steps, logs, z_proj, state_in, d_skip32).astype(b16)
    mixer_part = matmul_low(attended, full_o) + matmul_low(gated, full_out)
    mixed = lax.psum(mixer_part.astype(jnp.bfloat16), "head").astype(jnp.float32)
    hidden = tokens32 + mixed
    normed2, unit2, factor2 = normalize(hidden, gain2)
    n2 = normed2.astype(b16)
    gate = matmul_low(n2, full_gate)
    up = matmul_low(n2, full_up)
    sigma = jax.nn.sigmoid(gate)
    act = (gate * sigma * up).astype(b16)
    mlp_part = matmul_low(act, full_down)
    feed = lax.psum(mlp_part.astype(jnp.bfloat16), "head").astype(jnp.float32)
    output = (hidden + feed).astype(b16)
    grad_act = matmul_right(cotangent, full_down)
    grad_gate = (grad_act * up * sigma * (1.0 + gate * (1.0 - sigma))).astype(b16)
    grad_up = (grad_act * gate * sigma).astype(b16)
    grad_wdown = matmul_left(act, cotangent)
    grad_wgate = matmul_left(n2, grad_gate)
    grad_wup = matmul_left(n2, grad_up)
    partial2 = matmul_right(grad_gate, full_gate) + matmul_right(grad_up, full_up)
    grad_n2 = lax.psum(partial2.astype(jnp.bfloat16), "head").astype(jnp.float32)
    grad_norm2, grad_g2 = norm_back(grad_n2, unit2, factor2, gain2)
    grad_hidden = cotangent.astype(f32) + grad_norm2
    grad_mixed = grad_hidden.astype(b16)
    grad_wo = matmul_left(attended, grad_mixed)
    grad_wout = matmul_left(gated, grad_mixed)
    grad_attended = matmul_right(grad_mixed, full_o).astype(b16)
    grad_gated = matmul_right(grad_mixed, full_out).astype(b16).astype(f32)
    grad_flat = (
        grad_attended.reshape(length, local_heads, HEAD_DIM)
        .transpose(1, 0, 2)
        .reshape(-1, HEAD_DIM)
    )
    delta = jnp.sum(grad_flat.astype(f32) * accum, 1)
    grad_query, key_grads, value_grads = attend_backward(
        query_flat, query_pos, all_keys, all_values, grad_flat, lse, delta
    )
    my_key_grad, my_value_grad = side_by_side(
        (key_grads.astype(jnp.bfloat16), value_grads.astype(jnp.bfloat16)), "seq", 0, 1
    )
    grad_qproj = (
        rotate(
            grad_query.reshape(local_heads, length, HEAD_DIM).transpose(1, 0, 2), positions, -1.0
        )
        .reshape(length, -1)
        .astype(b16)
    )
    grad_kproj = (
        rotate(my_key_grad.reshape(length, 1, HEAD_DIM), positions, -1.0)
        .reshape(length, HEAD_DIM)
        .astype(b16)
    )
    grad_vproj = my_value_grad.astype(b16)
    grad_wq = matmul_left(n1, grad_qproj)
    grad_wk = matmul_left(n1, grad_kproj)
    grad_wv = matmul_left(n1, grad_vproj)
    _, output_back = jax.vjp(gated_output, xc, bmat, cmat, steps, logs, z_proj, state_in, d_skip32)
    grad_xc, grad_bmat, grad_cmat, grad_steps, grad_logs, grad_zproj, grad_state_in, grad_dskip = (
        output_back(grad_gated)
    )
    carried, _ = entering_2(
        (grad_state_in, decay_total),
        "seq",
        chain,
        (jnp.zeros_like(grad_state_in), jnp.ones_like(decay_total)),
    )
    grad_decay = jnp.sum(carried * state_in, (1, 2))
    _, state_back = jax.vjp(span_state, xc, bmat, steps, logs)
    more_xc, more_bmat, more_steps, more_logs = state_back((carried, grad_decay))
    _, prepare_back = jax.vjp(
        prepare,
        x_proj,
        bc_proj,
        dt_proj,
        x_edge,
        bc_edge,
        conv_x32,
        conv_xb32,
        conv_bc32,
        conv_bcb32,
        dt_bias32,
        a_log32,
    )
    (
        grad_xproj,
        grad_bcproj,
        grad_dtproj,
        grad_xedge,
        grad_bcedge,
        grad_convx,
        grad_convxb,
        grad_cbc,
        grad_cbcb,
        grad_dtbias,
        grad_alog,
    ) = prepare_back(
        (
            grad_xc + more_xc,
            grad_bmat + more_bmat,
            grad_cmat,
            grad_steps + more_steps,
            grad_logs + more_logs,
        )
    )
    from_next_x, from_next_bc = passed_along((grad_xedge, grad_bcedge), "seq", -1)
    grad_xproj = jnp.concatenate(
        [grad_xproj[: length - width], grad_xproj[length - width :] + from_next_x], 0
    )
    grad_bcproj = jnp.concatenate(
        [grad_bcproj[: length - width], grad_bcproj[length - width :] + from_next_bc], 0
    )
    grad_xproj_low = grad_xproj.astype(b16)
    grad_zproj_low = grad_zproj.astype(b16)
    grad_dtproj_low = grad_dtproj.astype(b16)
    partial1 = (
        matmul_right(grad_qproj, full_q)
        + matmul_right(grad_kproj, full_k)
        + matmul_right(grad_vproj, full_v)
    )
    partial1 = (
        partial1
        + matmul_right(grad_zproj_low, full_z)
        + matmul_right(grad_xproj_low, full_x)
        + matmul_right(grad_dtproj_low, full_dt)
    )
    grad_n1_part, grad_bc_total, grad_cbc_total, grad_cbcb_total = (
        lax.psum(partial1.astype(jnp.bfloat16), "head").astype(jnp.float32),
        lax.psum(grad_bcproj.astype(jnp.bfloat16), "head").astype(jnp.float32),
        lax.psum(grad_cbc.astype(jnp.bfloat16), "head").astype(jnp.float32),
        lax.psum(grad_cbcb.astype(jnp.bfloat16), "head").astype(jnp.float32),
    )
    grad_bc_low = grad_bc_total.astype(b16)
    grad_n1 = grad_n1_part + matmul_right(grad_bc_low, full_bc)
    grad_norm1, grad_g1 = norm_back(grad_n1, unit1, factor1, gain1)
    grad_tokens = grad_hidden + grad_norm1
    grad_wz = matmul_left(n1, grad_zproj_low)
    grad_wx = matmul_left(n1, grad_xproj_low)
    grad_wbc = matmul_left(n1, grad_bc_low)
    grad_wdt = matmul_left(n1, grad_dtproj_low)
    (
        sum_g1,
        sum_wq,
        sum_wk,
        sum_wv,
        sum_wo,
        sum_wz,
        sum_wx,
        sum_wbc,
        sum_wdt,
        sum_cbc,
        sum_cbcb,
        sum_wout,
    ) = (
        lax.psum_scatter(grad_g1, "seq", scatter_dimension=0, tiled=True),
        lax.psum_scatter(grad_wq, "seq", scatter_dimension=0, tiled=True),
        lax.psum_scatter(grad_wk, "seq", scatter_dimension=0, tiled=True),
        lax.psum_scatter(grad_wv, "seq", scatter_dimension=0, tiled=True),
        lax.psum_scatter(grad_wo, "seq", scatter_dimension=1, tiled=True),
        lax.psum_scatter(grad_wz, "seq", scatter_dimension=0, tiled=True),
        lax.psum_scatter(grad_wx, "seq", scatter_dimension=0, tiled=True),
        lax.psum_scatter(grad_wbc, "seq", scatter_dimension=0, tiled=True),
        lax.psum_scatter(grad_wdt, "seq", scatter_dimension=0, tiled=True),
        lax.psum_scatter(grad_cbc_total, "seq", scatter_dimension=1, tiled=True),
        lax.psum_scatter(grad_cbcb_total, "seq", scatter_dimension=0, tiled=True),
        lax.psum_scatter(grad_wout, "seq", scatter_dimension=1, tiled=True),
    )
    mlp_summed = reduce_mlp(grad_g2, grad_wgate, grad_wup, grad_wdown)
    sum_g2, sum_wgate, sum_wup, sum_wdown = mlp_summed
    sum_convx, sum_convxb, sum_dtbias, sum_alog, sum_dskip = lax.psum(
        (grad_convx, grad_convxb, grad_dtbias, grad_alog, grad_dskip), "seq"
    )
    return (
        output,
        grad_tokens,
        sum_g1,
        sum_wq,
        sum_wk,
        sum_wv,
        sum_wo,
        sum_wz,
        sum_wx,
        sum_wbc,
        sum_wdt,
        sum_cbc,
        sum_cbcb,
        sum_wout,
        sum_g2,
        sum_wgate,
        sum_wup,
        sum_wdown,
        sum_convx,
        sum_convxb,
        sum_dtbias,
        sum_alog,
        sum_dskip,
    )


def solution(mesh):
    placed = (
        P("seq", None),
        P("seq", None),
        P("seq"),
        P("seq", "head"),
        P("seq", "head"),
        P("seq", "head"),
        P("head", "seq"),
        P("seq", "head"),
        P("seq", "head"),
        P("seq", None),
        P("seq", "head"),
        P(None, "seq"),
        P("seq"),
        P("head", "seq"),
        P("seq"),
        P("seq", "head"),
        P("seq", "head"),
        P("head", "seq"),
        P(None, "head"),
        P("head"),
        P("head"),
        P("head"),
        P("head"),
    )
    return jax.shard_map(
        per_device,
        mesh=mesh,
        in_specs=placed,
        out_specs=(
            P("seq", None),
            P("seq", None),
            P("seq"),
            P("seq", "head"),
            P("seq", "head"),
            P("seq", "head"),
            P("head", "seq"),
            P("seq", "head"),
            P("seq", "head"),
            P("seq", None),
            P("seq", "head"),
            P(None, "seq"),
            P("seq"),
            P("head", "seq"),
            P("seq"),
            P("seq", "head"),
            P("seq", "head"),
            P("head", "seq"),
            P(None, "head"),
            P("head"),
            P("head"),
            P("head"),
            P("head"),
        ),
        check_vma=False,
    )
```

profile of v0, /device:TPU:0, one launch (start us, length us, event | category | flops | bytes accessed | tf_op | source)
XLA Modules:
  0.0 3986.7 jit_solution(1382476672001063667)
XLA Ops:
  8.7 42.4 %all-gather.3 = bf16[16,1,128]{2,1,0:T(2,128)(2,1)S(1)} all-gather(bf16[1,1,128]{2,1,0:T(2,128)(2,1)} %bitcast.519), channel_id=1, replica_groups=mesh['seq'=16,'head'=2] {'seq'}, dimensions={0}, use_global_device_ids=true | all-gather | bytes 4352 | tf_op jit(solution)/shard_map/all_gather | solution.py:305
  52.8 40.7 %all_gather.75 = bf16[2048,128]{1,0:T(8,128)(2,1)S(1)} all-gather(bf16[128,128]{1,0:T(8,128)(2,1)} %param.37), channel_id=1, replica_groups=mesh['seq'=16,'head'=2] {'seq'}, dimensions={0}, use_global_device_ids=true | all-gather | bytes 557056 | tf_op jit(solution)/shard_map/all_gather | solution.py:307
  96.5 43.4 %all_gather.78 = bf16[2048,128]{1,0:T(8,128)(2,1)S(1)} all-gather(bf16[128,128]{1,0:T(8,128)(2,1)S(1)} %copy-done.125), channel_id=1, replica_groups=mesh['seq'=16,'head'=2] {'seq'}, dimensions={0}, use_global_device_ids=true | all-gather | bytes 557056 | tf_op jit(solution)/shard_map/all_gather | solution.py:308
  142.0 37.1 all_gather.82
  181.1 37.5 all-gather.4
  220.3 36.9 all-reduce.20
  283.7 38.0 all-gather.5
  378.1 250.8 %all-gather.44.cloned.1.call-done = f32[384,64,256]{2,1,0:T(8,128)} async-done(((f32[24,64,256]{2,1,0:T(8,128)}), f32[384,64,256]{2,1,0:T(8,128)}) %all-gather.44.cloned.1.call-update) | async-done | bytes 25165840 | tf_op jit(solution)/shard_map/all_gather | solution.py:27
  641.9 82.2 %all-gather.32.cloned.1.call-done = bf16[2048,1536]{1,0:T(8,128)(2,1)} async-done(((bf16[128,1536]{1,0:T(8,128)(2,1)}), bf16[2048,1536]{1,0:T(8,128)(2,1)}) %all-gather.32.cloned.1.call-update) | async-done | bytes 6291472 | tf_op jit(solution)/shard_map/all_gather | solution.py:310
  730.2 110.5 %all-gather.34.cloned.1.call-done = bf16[1536,2048]{1,0:T(8,128)(2,1)} async-done(((bf16[1536,128]{1,0:T(8,128)(2,1)}), bf16[1536,2048]{1,0:T(8,128)(2,1)}) %all-gather.34.cloned.1.call-update) | async-done | bytes 6291472 | tf_op jit(solution)/shard_map/all_gather | solution.py:316
  846.8 58.0 %all-gather.26.cloned.1.call-done = bf16[512,2048]{1,0:T(8,128)(2,1)} async-done(((bf16[512,128]{1,0:T(8,128)(2,1)}), bf16[512,2048]{1,0:T(8,128)(2,1)}) %all-gather.26.cloned.1.call-update) | async-done | bytes 2097168 | tf_op jit(solution)/shard_map/all_gather | solution.py:309
  910.9 37.8 all-gather.6
  952.0 92.0 %all-gather.36.cloned.1.call-done = bf16[2048,2048]{1,0:T(8,128)(2,1)} async-done(((bf16[128,2048]{1,0:T(8,128)(2,1)}), bf16[2048,2048]{1,0:T(8,128)(2,1)}) %all-gather.36.cloned.1.call-update) | async-done | bytes 8388624 | tf_op jit(solution)/shard_map/all_gather | solution.py:318
  1051.3 106.7 %all-gather.38.cloned.1.call-done = bf16[2048,2048]{1,0:T(8,128)(2,1)} async-done(((bf16[128,2048]{1,0:T(8,128)(2,1)}), bf16[2048,2048]{1,0:T(8,128)(2,1)}) %all-gather.38.cloned.1.call-update) | async-done | bytes 8388624 | tf_op jit(solution)/shard_map/all_gather | solution.py:319
  1165.4 136.3 %all-gather.40.cloned.1.call-done = bf16[2048,2048]{1,0:T(8,128)(2,1)} async-done(((bf16[2048,128]{1,0:T(8,128)(2,1)}), bf16[2048,2048]{1,0:T(8,128)(2,1)}) %all-gather.40.cloned.1.call-update) | async-done | bytes 8388624 | tf_op jit(solution)/shard_map/all_gather | solution.py:320
  1356.3 41.0 %all-gather.7 = bf16[16,1,24]{2,1,0:T(2,128)(2,1)S(1)} all-gather(bf16[1,1,24]{2,1,0:T(2,128)(2,1)S(1)} %bitcast.515), channel_id=1, replica_groups=mesh['seq'=16,'head'=2] {'seq'}, dimensions={0}, use_global_device_ids=true | all-gather | bytes 816 | tf_op jit(solution)/shard_map/all_gather | solution.py:61
  1403.7 51.4 %while.70 = (s32[]{:T(128)}, f32[1024,128]{1,0:T(8,128)}, bf16[4,1024,128]{2,1,0:T(8,128)(2,1)}, bf16[4,1024,128]{2,1,0:T(8,128)(2,1)}, s32[4]{0:T(128)S(1)}, /*...) while((s32[]{:T(128)}, f32[1024,128]{1,0:T(8,128)}, ...), condition=%wide.region_18.19_spmd.clone, body=%wide.region_17.18_spmd.clone.sunk | while | flops 1355154432 | bytes 58507040 | solution.py:241
  1501.9 31.9 all-to-all-done
  1551.8 48.9 %while.71 = (s32[]{:T(128)}, f32[24,64,256]{2,1,0:T(8,128)}, s32[]{:T(128)}, bf16[16,24]{1,0:T(8,128)(2,1)S(1)}, bf16[16,24,64,256]{3,2,1,0:T(8,128)(2,1)}, /*index=5*/s32[]{:T(128)}, s32[]{:T(128)}, s32[]{:T(128)}, s32[]{:T(128)}) while((s32[]{:T(128)}, f32[24,64,256]{2,1,0:T(8,128)}, s32[]{:T(128)}, ...), condition=%wide.region_21.22_spmd.clone, body=%wide.region_20.21_spmd.clone.sunk | while | flops 1966112 | bytes 3932567 | solution.py:77
  1724.9 40.1 %reduce-scatter.40.cloned.1.call-done = f32[32,4]{1,0:T(8,128)} async-done(((f32[512,4]{1,0:T(8,128)}), f32[32,4]{1,0:T(8,128)}) %reduce-scatter.40.cloned.1.call-update) | async-done | bytes 528
  1770.6 72.3 %all-reduce.24 = (f32[2048]{0:T(1024)S(1)}, f32[512]{0:T(512)S(1)}, f32[2048]{0:T(1024)S(1)}, f32[4,1536]{1,0:T(4,128)}, f32[1536]{0:T(1024)}, /*index=5*/f32[24]{0:T(128)}, f32[24]{0:T(128)}, f32[24]{0:T(128)}) all-reduce(f32[2048]{0:T(1024)S(1)} %get-tuple-element.639, ...), channel_id=5, replica_groups=mesh['seq'=16,'head'=2] {'seq'}, use_global_device_ids=true, to_apply=%region_37.38.clone | all-reduce | flops 12360 | bytes 97856
  1850.2 68.6 %reduce-scatter.20.cloned.1.call-done = f32[128,128]{1,0:T(8,128)} async-done(((f32[2048,128]{1,0:T(8,128)}), f32[128,128]{1,0:T(8,128)}) %reduce-scatter.20.cloned.1.call-update) | async-done | bytes 65552 | tf_op jit(solution)/shard_map/reduce_scatter | solution.py:541
  1918.8 94.4 %reduce-scatter.16.cloned.1.call-done = f32[128,512]{1,0:T(8,128)} async-done(((f32[2048,512]{1,0:T(8,128)}), f32[128,512]{1,0:T(8,128)}) %reduce-scatter.16.cloned.1.call-update) | async-done | bytes 262160 | tf_op jit(solution)/shard_map/reduce_scatter | solution.py:539
  2013.2 97.5 %reduce-scatter.22.cloned.1.call-done = f32[512,128]{1,0:T(8,128)} async-done(((f32[512,2048]{1,0:T(8,128)}), f32[512,128]{1,0:T(8,128)}) %reduce-scatter.22.cloned.1.call-update) | async-done | bytes 262160 | tf_op jit(solution)/shard_map/reduce_scatter | solution.py:542
  2110.7 78.6 %reduce-scatter.30.cloned.1.call-done = f32[128,24]{0,1:T(8,128)} async-done(((f32[2048,24]{0,1:T(8,128)}), f32[128,24]{0,1:T(8,128)}) %reduce-scatter.30.cloned.1.call-update) | async-done | bytes 12304 | tf_op jit(solution)/shard_map/reduce_scatter | solution.py:546
  2189.3 207.6 %reduce-scatter.32.cloned.1.call-done = f32[1536,128]{1,0:T(8,128)} async-done(((f32[1536,2048]{1,0:T(8,128)}), f32[1536,128]{1,0:T(8,128)}) %reduce-scatter.32.cloned.1.call-update) | async-done | bytes 786448 | tf_op jit(solution)/shard_map/reduce_scatter | solution.py:549
  2396.9 209.8 %reduce-scatter.24.cloned.1.call-done = f32[128,1536]{1,0:T(8,128)} async-done(((f32[2048,1536]{1,0:T(8,128)}), f32[128,1536]{1,0:T(8,128)}) %reduce-scatter.24.cloned.1.call-update) | async-done | bytes 786448 | tf_op jit(solution)/shard_map/reduce_scatter | solution.py:543
  2606.6 349.0 %reduce-scatter.34.cloned.1.call-done = f32[128,2048]{1,0:T(8,128)} async-done(((f32[2048,2048]{1,0:T(8,128)}), f32[128,2048]{1,0:T(8,128)}) %reduce-scatter.34.cloned.1.call-update) | async-done | bytes 1048592 | tf_op jit(solution)/shard_map/reduce_scatter | solution.py:254
  2955.6 354.8 %reduce-scatter.36.cloned.1.call-done = f32[128,2048]{1,0:T(8,128)} async-done(((f32[2048,2048]{1,0:T(8,128)}), f32[128,2048]{1,0:T(8,128)}) %reduce-scatter.36.cloned.1.call-update) | async-done | bytes 1048592 | tf_op jit(solution)/shard_map/reduce_scatter | solution.py:255
  3310.5 354.9 %reduce-scatter.38.cloned.1.call-done = f32[2048,128]{1,0:T(8,128)} async-done(((f32[2048,2048]{1,0:T(8,128)}), f32[2048,128]{1,0:T(8,128)}) %reduce-scatter.38.cloned.1.call-update) | async-done | bytes 1048592 | tf_op jit(solution)/shard_map/reduce_scatter | solution.py:256
  3665.4 103.8 %reduce-scatter.28.cloned.1.call-done = f32[128,512]{1,0:T(8,128)} async-done(((f32[2048,512]{1,0:T(8,128)}), f32[128,512]{1,0:T(8,128)}) %reduce-scatter.28.cloned.1.call-update) | async-done | bytes 262160 | tf_op jit(solution)/shard_map/reduce_scatter | solution.py:545
  3769.1 210.9 %reduce-scatter.26.cloned.1.call-done = f32[128,1536]{1,0:T(8,128)} async-done(((f32[2048,1536]{1,0:T(8,128)}), f32[128,1536]{1,0:T(8,128)}) %reduce-scatter.26.cloned.1.call-update) | async-done | bytes 786448 | tf_op jit(solution)/shard_map/reduce_scatter | solution.py:544
  (741 shorter events, 539.7 us)
Async XLA Ops:
  7.2 250.2 %all-gather.30.cloned.1.call-start = ((), (), s32[]{:S(2)}) async-start(), calls=%async_computation.18 | async-start | bytes 2228224 | tf_op jit(solution)/shard_map/all_gather | solution.py:312
  7.9 255.8 %all-gather.28.cloned.1.call-start = ((), (), s32[]{:S(2)}) async-start(), calls=%async_computation.17 | async-start | bytes 6684672 | tf_op jit(solution)/shard_map/all_gather | solution.py:311
  8.7 313.0 %all-gather.42.cloned.1.call-start = ((), (), s32[]{:S(2)}) async-start(), calls=%async_computation.38 | async-start | bytes 1114112 | tf_op jit(solution)/shard_map/all_gather | solution.py:342
  95.9 227.4 %all-gather.22.cloned.1.call-start = ((), (), s32[]{:S(2)}) async-start(), calls=%async_computation.14 | async-start | bytes 2228224 | tf_op jit(solution)/shard_map/all_gather | solution.py:306
  96.5 261.8 %all-gather.24.cloned.1.call-start = ((), (), s32[]{:S(2)}) async-start(), calls=%async_computation.15 | async-start | bytes 1114112 | tf_op jit(solution)/shard_map/all_gather | solution.py:343
  141.9 487.0 %all-gather.44.cloned.1.call-start = ((), (), s32[]{:S(2)}) async-start(), calls=%async_computation.39 | async-start | bytes 26738688 | tf_op jit(solution)/shard_map/all_gather | solution.py:27
  259.8 10.7 collective-permute-start.1
  279.1 445.0 %all-gather.32.cloned.1.call-start = ((), (), s32[]{:S(2)}) async-start(), calls=%async_computation.19 | async-start | bytes 6684672 | tf_op jit(solution)/shard_map/all_gather | solution.py:310
  279.9 560.8 %all-gather.34.cloned.1.call-start = ((), (), s32[]{:S(2)}) async-start(), calls=%async_computation.20 | async-start | bytes 6684672 | tf_op jit(solution)/shard_map/all_gather | solution.py:316
  280.6 624.2 %all-gather.26.cloned.1.call-start = ((), (), s32[]{:S(2)}) async-start(), calls=%async_computation.16 | async-start | bytes 2228224 | tf_op jit(solution)/shard_map/all_gather | solution.py:309
  281.4 667.4 %all-reduce.31.cloned.1.call-start = ((), (), s32[]{:S(2)}) async-start(), calls=%async_computation.21 | async-start | bytes 2097152 | tf_op jit(solution)/shard_map/psum | solution.py:387
  908.8 135.2 %all-gather.36.cloned.1.call-start = ((), (), s32[]{:S(2)}) async-start(), calls=%async_computation.22 | async-start | bytes 8912896 | tf_op jit(solution)/shard_map/all_gather | solution.py:318
  909.5 248.5 %all-gather.38.cloned.1.call-start = ((), (), s32[]{:S(2)}) async-start(), calls=%async_computation.23 | async-start | bytes 8912896 | tf_op jit(solution)/shard_map/all_gather | solution.py:319
  910.1 391.5 %all-gather.40.cloned.1.call-start = ((), (), s32[]{:S(2)}) async-start(), calls=%async_computation.24 | async-start | bytes 8912896 | tf_op jit(solution)/shard_map/all_gather | solution.py:320
  910.9 427.7 %all-reduce.33.cloned.1.call-start = ((), (), s32[]{:S(2)}) async-start(), calls=%async_computation.25 | async-start | bytes 2097152 | tf_op jit(solution)/shard_map/psum | solution.py:405
  1320.7 231.1 %all-gather.46.cloned.1.call-start = ((), (), s32[]{:S(2)}) async-start(), calls=%async_computation.40 | async-start | bytes 13369344 | tf_op jit(solution)/shard_map/all_gather | solution.py:61
  1458.3 75.5 %all-to-all-start = ((bf16[16,256,256]{2,1,0:T(8,128)(2,1)}), bf16[16,256,256]{2,1,0:T(8,128)(2,1)}, u32[]{:S(2)}, u32[]{:S(2)}) async-start(bf16[16,256,256]{2,1,0:T(8,128)(2,1)} %pad_maximum_fusion), calls=%async_computation | async-start | bytes 4194304 | tf_op jit(solution)/shard_map/all_to_all | solution.py:45
  1462.8 248.8 %all-reduce.35.cloned.1.call-start = ((), (), s32[]{:S(2)}) async-start(), calls=%async_computation.42 | async-start | bytes 4718592 | tf_op jit(solution)/shard_map/psum | solution.py:396
  1625.8 18.5 collective-permute-start.2
  1652.1 112.9 %reduce-scatter.40.cloned.1.call-start = ((), (), s32[]{:S(2)}) async-start(), calls=%async_computation.41 | async-start | bytes 278528
  1655.6 194.6 %reduce-scatter.18.cloned.1.call-start = ((), (), s32[]{:S(2)}) async-start(), calls=%async_computation.27 | async-start | bytes 1114112 | tf_op jit(solution)/shard_map/reduce_scatter | solution.py:540
  1657.2 261.6 %reduce-scatter.20.cloned.1.call-start = ((), (), s32[]{:S(2)}) async-start(), calls=%async_computation.28 | async-start | bytes 1114112 | tf_op jit(solution)/shard_map/reduce_scatter | solution.py:541
  1658.9 354.2 %reduce-scatter.16.cloned.1.call-start = ((), (), s32[]{:S(2)}) async-start(), calls=%async_computation.26 | async-start | bytes 4456448 | tf_op jit(solution)/shard_map/reduce_scatter | solution.py:539
  1661.9 448.8 %reduce-scatter.22.cloned.1.call-start = ((), (), s32[]{:S(2)}) async-start(), calls=%async_computation.29 | async-start | bytes 4456448 | tf_op jit(solution)/shard_map/reduce_scatter | solution.py:542
  1666.0 523.3 %reduce-scatter.30.cloned.1.call-start = ((), (), s32[]{:S(2)}) async-start(), calls=%async_computation.33 | async-start | bytes 208896 | tf_op jit(solution)/shard_map/reduce_scatter | solution.py:546
  1667.8 729.1 %reduce-scatter.32.cloned.1.call-start = ((), (), s32[]{:S(2)}) async-start(), calls=%async_computation.34 | async-start | bytes 13369344 | tf_op jit(solution)/shard_map/reduce_scatter | solution.py:549
  1674.4 932.2 %reduce-scatter.24.cloned.1.call-start = ((), (), s32[]{:S(2)}) async-start(), calls=%async_computation.30 | async-start | bytes 13369344 | tf_op jit(solution)/shard_map/reduce_scatter | solution.py:543
  1682.5 1273.2 %reduce-scatter.34.cloned.1.call-start = ((), (), s32[]{:S(2)}) async-start(), calls=%async_computation.35 | async-start | bytes 17825792 | tf_op jit(solution)/shard_map/reduce_scatter | solution.py:254
  1692.5 1618.0 %reduce-scatter.36.cloned.1.call-start = ((), (), s32[]{:S(2)}) async-start(), calls=%async_computation.36 | async-start | bytes 17825792 | tf_op jit(solution)/shard_map/reduce_scatter | solution.py:255
  1701.8 1963.5 %reduce-scatter.38.cloned.1.call-start = ((), (), s32[]{:S(2)}) async-start(), calls=%async_computation.37 | async-start | bytes 17825792 | tf_op jit(solution)/shard_map/reduce_scatter | solution.py:256
  1711.6 2057.5 %reduce-scatter.28.cloned.1.call-start = ((), (), s32[]{:S(2)}) async-start(), calls=%async_computation.32 | async-start | bytes 4456448 | tf_op jit(solution)/shard_map/reduce_scatter | solution.py:545
  1715.4 2264.6 %reduce-scatter.26.cloned.1.call-start = ((), (), s32[]{:S(2)}) async-start(), calls=%async_computation.31 | async-start | bytes 13369344 | tf_op jit(solution)/shard_map/reduce_scatter | solution.py:544
  (183 other events, 9180.7 us)
Sparse Core Ops, SparseCore 0:
  10.8 65.2 all-gather.29
  78.9 99.1 all-gather.27
  181.4 53.9 all-gather.41
  238.0 60.6 all-gather.21
  301.9 53.7 all-gather.23
  358.9 269.9 all-gather.43
  631.7 92.3 all-gather.31
  726.8 113.8 all-gather.33
  843.4 61.4 all-gather.25
  908.9 17.7 all-reduce.30
  929.9 114.0 all-gather.35
  1047.0 111.0 all-gather.37
  1161.1 140.5 all-gather.39
  1320.8 17.7 all-reduce.32
  1356.2 195.5 all-gather.45
  1652.2 33.2 all-reduce.34
  1687.7 77.3 reduce-scatter.39
  1767.7 74.0 reduce-scatter.17
  1844.7 74.0 reduce-scatter.19
  1921.5 91.5 reduce-scatter.15
  2016.0 94.6 reduce-scatter.21
  2113.5 75.7 reduce-scatter.29
  2196.5 200.3 reduce-scatter.31
  2403.0 203.6 reduce-scatter.23
  2609.6 345.9 reduce-scatter.33
  2958.5 351.9 reduce-scatter.35
  3313.3 352.0 reduce-scatter.37
  3668.3 100.7 reduce-scatter.27
  3776.3 203.6 reduce-scatter.25
where the time goes:
time: 4000 us; the launch traced here: 3990 us
  waiting for transfers between devices  3070 us (77%)
  blocking collectives  430 us (11%)
  matrix products  274 us (7%)
  other arithmetic  115 us (3%)
  local copies, waits for them, and re-layouts  52.8 us (1%)
    reduce_scatter x1, waiting for transfers between devices, reduce_mlp(): lax.psum_scatter(down_grad, 'seq', scatter_dimension=1, tiled=True)  355 us
    reduce_scatter x1, waiting for transfers between devices, reduce_mlp(): lax.psum_scatter(up_grad, 'seq', scatter_dimension=0, tiled=True)  355 us
    reduce_scatter x1, waiting for transfers between devices, reduce_mlp(): lax.psum_scatter(gate_grad, 'seq', scatter_dimension=0, tiled=True)  349 us
    all_gather x1, waiting for transfers between devices, entering(): gathered = jax.tree.map(lambda a: lax.all_gather(a, axis), part)  251 us
    reduce_scatter x1, waiting for transfers between devices, per_device(): lax.psum_scatter(grad_wx, 'seq', scatter_dimension=0, tiled=True)  211 us
    reduce_scatter x1, waiting for transfers between devices, per_device(): lax.psum_scatter(grad_wz, 'seq', scatter_dimension=0, tiled=True)  210 us
    reduce_scatter x1, waiting for transfers between devices, per_device(): lax.psum_scatter(grad_wout, 'seq', scatter_dimension=1, tiled=True)  208 us
    all_gather x1, waiting for transfers between devices, per_device(): lax.all_gather(w_down, 'seq', axis=1, tiled=True)  136 us
  transfers between devices with their start and end apart: 34, of which 24 were waited for; matrix products, arithmetic and copies ran while one was open for 8% of the time, Pallas kernels for 0%

commit v1 on v0

v1 whole, which is shorter than its diff:
```python
import math

import jax
import jax.numpy as jnp
from jax import lax
from jax.sharding import Mesh, PartitionSpec as P

HEAD_DIM = 128
STATE = 256
CONV = 4
EPS = 1e-05
ROPE_BASE = 100000000000.0
MASKED = -1e30
HIGHEST = lax.Precision.HIGHEST
F32 = jnp.float32
B16 = jnp.bfloat16


def after(x, *earlier):
    return lax.optimization_barrier((x, earlier))[0]


def swap_cores(x):
    return lax.ppermute(x, "head", [(0, 1), (1, 0)])


def trade_near(x):
    return lax.all_to_all(x, "near", 0, 0, tiled=True)


def gather_near(x):
    return trade_near(jnp.broadcast_to(x, (lax.axis_size("near"), *x.shape)))


def both_halves(mine, other, dim):
    first = lax.axis_index("head") == 0
    return jnp.concatenate([jnp.where(first, mine, other), jnp.where(first, other, mine)], dim)


def gather_tokens(x):
    half = x.shape[1] // 2
    mine = lax.dynamic_slice_in_dim(x, lax.axis_index("head") * half, half, 1)
    rows = gather_near(mine).reshape(-1, half)
    return both_halves(rows, swap_cores(rows), 1)


def scatter_tokens(partial):
    near = lax.axis_size("near")
    half = partial.shape[1] // 2
    core = lax.axis_index("head")
    give = lax.dynamic_slice_in_dim(partial, (1 - core) * half, half, 1).astype(B16)
    keep = lax.dynamic_slice_in_dim(partial, core * half, half, 1)
    mine = (keep + swap_cores(give).astype(F32)).astype(B16)
    parts = trade_near(mine.reshape(near, -1, half))
    total = jnp.sum(parts.astype(F32), 0)
    return both_halves(total, swap_cores(total), 1)


def ring_route(axis):
    count = lax.axis_size(axis)
    return [(i, (i + 1) % count) for i in range(count)]


def ring_gather(x):
    count, place = lax.axis_size("group"), lax.axis_index("group")
    held = jnp.zeros((count, *x.shape), x.dtype)
    held = lax.dynamic_update_index_in_dim(held, x, place, 0)
    for turn in range(1, count):
        x = lax.ppermute(x, "group", ring_route("group"))
        held = lax.dynamic_update_index_in_dim(held, x, (place - turn) % count, 0)
    return held


def ring_sum(parts):
    count, place = lax.axis_size("group"), lax.axis_index("group")

    def part(turn):
        return lax.dynamic_index_in_dim(parts, (place - 1 - turn) % count, 0, False)

    moving = part(0)
    for turn in range(1, count):
        moving = lax.ppermute(moving, "group", ring_route("group"))
        moving = moving.astype(F32) + part(turn).astype(F32)
        if turn < count - 1:
            moving = moving.astype(B16)
    return moving


def step_group(x, distance):
    count = lax.axis_size("group")
    route = [(i, i + distance) for i in range(count) if 0 <= i + distance < count]
    return lax.ppermute(x, "group", route)


def dot(left, right, dims=((1,), (0,))):
    return lax.dot_general(left, right, (dims, ((), ())), preferred_element_type=F32)


def dot_nt(left, right):
    return dot(left, right, ((1,), (1,)))


def dot_tn(left, right):
    return dot(left, right, ((0,), (0,)))


def exact(spec, *operands):
    return jnp.einsum(spec, *operands, precision=HIGHEST)


def normalize(values, gain):
    factor = lax.rsqrt(jnp.mean(values * values, -1, keepdims=True) + EPS)
    unit = values * factor
    return unit * gain, unit, factor


def norm_back(grad_out, unit, factor, gain):
    grad_unit = grad_out * gain[None, :]
    grad_in = factor * (grad_unit - unit * jnp.mean(grad_unit * unit, -1, keepdims=True))
    return grad_in, jnp.sum(grad_out * unit, 0)


def rope_angles(positions, first, count, half):
    index = first + jnp.arange(count, dtype=F32)
    freqs = ROPE_BASE ** (-index / half)
    return positions.astype(F32), freqs


def rotate_pair(first, second, cosine, sine):
    return first * cosine - second * sine, second * cosine + first * sine


def conv(inputs, edge, weight, bias, dim):
    length = inputs.shape[dim]
    padded = jnp.concatenate([edge, inputs], dim)
    total = bias
    for tap in range(CONV):
        total = total + weight[tap] * lax.slice_in_dim(padded, tap, tap + length, axis=dim)
    return total


def conv_back(grad, grad_edge, inputs, edge, weight, dim):
    length = inputs.shape[dim]
    padded = jnp.concatenate([edge, inputs], dim)
    late = jnp.concatenate([grad, grad_edge], dim)
    total = 0.0
    taps = []
    for tap in range(CONV):
        back = CONV - 1 - tap
        total = total + weight[tap] * lax.slice_in_dim(late, back, back + length, axis=dim)
        taps.append(jnp.sum(grad * lax.slice_in_dim(padded, tap, tap + length, axis=dim), dim))
    return total, jnp.stack(taps), jnp.sum(grad, dim)


def silu_slope(v):
    s = jax.nn.sigmoid(v)
    return s * (1.0 + v * (1.0 - s))


def attention_scores(queries, keys_t, first):
    scores = dot(queries, keys_t) * HEAD_DIM**-0.5
    rows = first + lax.broadcasted_iota(jnp.int32, scores.shape, 0)
    return jnp.where(lax.broadcasted_iota(jnp.int32, scores.shape, 1) <= rows, scores, MASKED)


def attend(queries, keys_t, values_t, first):
    scores = attention_scores(queries, keys_t, first)
    top = jnp.max(scores, 1, keepdims=True)
    probs = jnp.exp(scores - top)
    mass = jnp.sum(probs, 1, keepdims=True)
    out = dot_nt((probs / mass).astype(B16), values_t)
    return out, top + jnp.log(mass)


def attend_back(queries, keys_t, values_t, first, grad, lse, delta):
    probs = jnp.exp(attention_scores(queries, keys_t, first) - lse)
    grad_probs = dot(grad, values_t)
    grad_scores = (probs * (grad_probs - delta)).astype(B16)
    grad_q = dot_nt(grad_scores, keys_t) * HEAD_DIM**-0.5
    grad_kt = dot_tn(queries, grad_scores) * HEAD_DIM**-0.5
    grad_vt = dot_tn(grad, probs.astype(B16))
    return grad_q, grad_kt, grad_vt


def decay_matrix(cum):
    length = cum.shape[-1]
    order = jnp.arange(length)
    causal = order[:, None] >= order[None, :]
    return jnp.exp(jnp.where(causal, cum[..., :, None] - cum[..., None, :], MASKED))


def scan_forward(scaled, bmat, cmat, cum):
    decay = decay_matrix(cum)
    inner = exact("ctn,csn->cts", cmat, bmat)
    within = exact("chts,cshp->cthp", decay * inner[:, None], scaled)
    tail = jnp.exp(cum[..., -1:] - cum)
    added = exact("cshp,csn->chpn", scaled * tail.transpose(0, 2, 1)[..., None], bmat)
    state = jnp.zeros_like(added[0])
    states = []
    for c in range(added.shape[0]):
        states.append(state)
        state = jnp.exp(cum[c, :, -1])[:, None, None] * state + added[c]
    states = jnp.stack(states)
    carried = exact("ctn,chpn->cthp", cmat, states) * jnp.exp(cum).transpose(0, 2, 1)[..., None]
    return within + carried, states, state


def scan_backward(scaled, bmat, cmat, cum, states, state_out, grad, grad_state):
    decay = decay_matrix(cum)
    inner = exact("ctn,csn->cts", cmat, bmat)
    tail = jnp.exp(cum[..., -1:] - cum).transpose(0, 2, 1)[..., None]
    faded = grad * jnp.exp(cum).transpose(0, 2, 1)[..., None]
    grad_scaled = exact("chts,cthp->cshp", decay * inner[:, None], grad)
    grad_inner = jnp.sum(exact("cthp,cshp->chts", grad, scaled) * decay, 1)
    read = exact("cthp,ctn->chpn", faded, cmat)
    count = grad.shape[0]
    grad_states = [None] * count
    grad_last = [None] * count
    following = [*(states[c] for c in range(1, count)), state_out]
    for c in reversed(range(count)):
        grad_states[c] = grad_state
        grad_last[c] = jnp.sum(following[c] * grad_state, (1, 2))
        grad_state = jnp.exp(cum[c, :, -1])[:, None, None] * grad_state + read[c]
    grad_states = jnp.stack(grad_states)
    grad_scaled = grad_scaled + tail * exact("csn,chpn->cshp", bmat, grad_states)
    grad_c = exact("cts,csn->ctn", grad_inner, bmat) + exact("cthp,chpn->ctn", faded, states)
    grad_b = exact("cts,ctn->csn", grad_inner, cmat) + exact(
        "cshp,chpn->csn", scaled * tail, grad_states
    )
    return grad_scaled, grad_b, grad_c, jnp.stack(grad_last)


def per_device(
    tokens,
    cotangent,
    g1,
    w_q,
    w_k,
    w_v,
    w_o,
    w_z,
    w_x,
    w_bc,
    w_dt,
    conv_bc,
    conv_bc_bias,
    w_out,
    g2,
    w_gate,
    w_up,
    w_down,
    conv_x,
    conv_x_bias,
    dt_bias,
    a_log,
    d_skip,
):
    near, groups = lax.axis_size("near"), lax.axis_size("group")
    here, group, core = (lax.axis_index(a) for a in ("near", "group", "head"))
    rows, width = tokens.shape
    span = near * rows
    piece = w_q.shape[0]
    first_position = group * span

    def columns(w):
        return w.reshape(w.shape[0], near, -1).transpose(1, 0, 2)

    def share(x, dim):
        size = x.shape[dim] // near
        return lax.dynamic_slice_in_dim(x, here * size, size, dim)

    smalls = jnp.concatenate([g1, g2, conv_bc.reshape(-1), conv_bc_bias])
    devices = near * groups
    smalls = lax.all_to_all(
        jnp.broadcast_to(smalls, (devices, smalls.shape[0])), ("group", "near"), 0, 0, tiled=True
    ).astype(F32)
    gain1 = smalls[:, :piece].reshape(-1)
    gain2 = smalls[:, piece : 2 * piece].reshape(-1)
    taps_bc = smalls[:, 2 * piece : -conv_bc_bias.shape[0]].reshape(devices, CONV, -1)
    taps_bc = taps_bc.transpose(1, 0, 2).reshape(CONV, 2, near, -1)
    taps_bc = taps_bc[:, core, here][:, :, None]
    bias_bc = smalls[:, -conv_bc_bias.shape[0] :].reshape(2, near, -1)[core, here][:, None]

    key_cols = HEAD_DIM // near
    half_cols = key_cols // 2
    state_cols = STATE // near
    k_cols = w_k.reshape(piece, 2, near, half_cols).transpose(2, 0, 1, 3)
    w_bc_mine = lax.dynamic_slice_in_dim(w_bc, core * STATE, STATE, 1)
    small_cols = [k_cols.reshape(near, piece, key_cols), columns(w_v), columns(w_bc_mine)]
    pack1 = trade_near(jnp.concatenate([columns(w_q), *small_cols, columns(w_x)], 2))
    dt_heads = w_dt.shape[1] // near
    pack_dt = jnp.pad(w_dt.T.reshape(near, dt_heads, piece), ((0, 0), (0, -dt_heads % 8), (0, 0)))
    pack_dt = trade_near(pack_dt).transpose(1, 0, 2).reshape(-1, near * piece)
    all_tokens = gather_tokens(tokens)
    full1 = ring_gather(pack1.reshape(near * piece, -1))
    full_dt = ring_gather(pack_dt)
    pack2 = trade_near(after(columns(w_z), pack1)).reshape(near * piece, -1)
    full_z = ring_gather(after(pack2, full1))
    pack3 = jnp.concatenate([w_o.reshape(near, -1, piece), w_out.reshape(near, -1, piece)], 1)
    pack3 = trade_near(after(pack3, pack2))
    full3 = ring_gather(after(pack3, full_z))
    pack4 = trade_near(after(jnp.concatenate([columns(w_gate), columns(w_up)], 2), pack3))
    full4 = ring_gather(after(pack4.reshape(near * piece, -1), full3))
    pack5 = trade_near(after(w_down.reshape(near, -1, piece), pack4))
    full5 = ring_gather(after(pack5, full4))
    all_cotangent = gather_tokens(after(cotangent, pack5))

    wq_cols = w_q.shape[1] // near
    full1 = full1.reshape(width, -1)
    full_q, full_kvbc, full_x = jnp.split(full1, [wq_cols, wq_cols + 2 * key_cols + state_cols], 1)
    full_dt = full_dt.transpose(1, 0, 2).reshape(-1, width)[:dt_heads]
    full_z = full_z.reshape(width, -1)
    full3 = full3.transpose(2, 0, 1, 3).reshape(-1, width)
    o_rows = w_o.shape[0] // near
    full_o, full_out = full3[:o_rows], full3[o_rows:]
    full4 = full4.reshape(width, -1)
    ff = full4.shape[1] // 2
    full_gate, full_up = full4[:, :ff], full4[:, ff:]
    full_down = full5.transpose(2, 0, 1, 3).reshape(-1, width)

    n1 = normalize(all_tokens.astype(F32), gain1)[0].astype(B16)
    positions = (first_position + jnp.arange(span)).astype(F32)
    half = HEAD_DIM // 2
    freqs = ROPE_BASE ** (-jnp.arange(half, dtype=F32) / half)
    angle = positions[:, None] * freqs[None, :]
    cos_q, sin_q = jnp.cos(angle), jnp.sin(angle)
    cos_k, sin_k = (share(x, 1).T for x in (cos_q, sin_q))

    q_proj = dot(n1, full_q)
    queries = jnp.concatenate(rotate_pair(q_proj[:, :half], q_proj[:, half:], cos_q, sin_q), 1)
    queries = queries.astype(B16)
    kvbc = dot(full_kvbc, n1, ((0,), (1,)))
    k_first, k_second = rotate_pair(kvbc[:half_cols], kvbc[half_cols:key_cols], cos_k, sin_k)
    kv = jnp.concatenate([k_first, k_second, kvbc[key_cols : 2 * key_cols]], 0).astype(B16)
    kv = gather_near(ring_gather(kv))
    keys_t = kv[:, :, :key_cols].reshape(near, groups, 2, half_cols, span)
    keys_t = keys_t.transpose(2, 0, 3, 1, 4).reshape(HEAD_DIM, -1)
    values_t = kv[:, :, key_cols:].transpose(0, 2, 1, 3).reshape(HEAD_DIM, -1)

    bc_proj = kvbc[2 * key_cols :]
    bc_edge = step_group(bc_proj[:, span - CONV + 1 :], 1)
    bc_pre = conv(bc_proj, bc_edge, taps_bc, bias_bc, 1)
    bc_mine = gather_near(jax.nn.silu(bc_pre).astype(B16)).reshape(STATE, span)
    bc_other = swap_cores(bc_mine)
    bc_both = both_halves(bc_mine, bc_other, 0).astype(F32)
    bmat = bc_both[:STATE].reshape(STATE, near, rows).transpose(1, 2, 0)
    cmat = bc_both[STATE:].reshape(STATE, near, rows).transpose(1, 2, 0)

    x_proj = dot(n1, full_x)
    x_edge = step_group(x_proj[span - CONV + 1 :], 1)
    taps_x = share(conv_x, 1).astype(F32)[:, None, :]
    bias_x = share(conv_x_bias, 0).astype(F32)[None, :]
    x_pre = conv(x_proj, x_edge, taps_x, bias_x, 0)
    xc = jax.nn.silu(x_pre)
    inner_cols = xc.shape[1]
    channels = inner_cols // dt_heads
    dt_pre = dot_nt(full_dt, n1) + share(dt_bias, 0).astype(F32)[:, None]
    dt = jax.nn.softplus(dt_pre)
    decay_rate = jnp.exp(share(a_log, 0).astype(F32))[:, None]
    logs = -dt * decay_rate
    skip = share(d_skip, 0).astype(F32)
    chunked = logs.reshape(dt_heads, near, rows).transpose(1, 0, 2)
    triangle = jnp.tril(jnp.ones((rows, rows), F32))
    cum = exact("chs,ts->cht", chunked, triangle)
    xh = xc.reshape(near, rows, dt_heads, channels)
    dt_col = dt.reshape(dt_heads, near, rows).transpose(1, 2, 0)[..., None]
    scaled = xh * dt_col

    outputs, states, state_out = scan_forward(scaled, bmat, cmat, cum)
    chunk_total = cum[..., -1]
    before = jnp.cumsum(chunk_total, 0) - chunk_total
    group_total = jnp.sum(chunk_total, 0)
    all_states = ring_gather(state_out.astype(B16))
    all_totals = ring_gather(jnp.pad(group_total, (0, -dt_heads % 8)))[:, :dt_heads]

    attended32, lse = attend(queries, keys_t, values_t, first_position)
    attended = attended32.astype(B16)

    entering = jnp.zeros_like(state_out)
    for turn in range(groups - 1):
        passed = jnp.exp(all_totals[turn])[:, None, None] * entering + all_states[turn].astype(F32)
        entering = jnp.where(turn < group, passed, entering)
    fade = jnp.exp(cum + before[..., None]).transpose(0, 2, 1)[..., None]
    outputs = outputs + fade * exact("ctn,hpn->cthp", cmat, entering)
    states = states + jnp.exp(before)[:, :, None, None] * entering
    state_out = state_out + jnp.exp(group_total)[:, None, None] * entering
    y = outputs + skip[:, None] * xh
    z_proj = dot(n1, full_z)
    gated = (y.reshape(span, -1) * jax.nn.silu(z_proj)).astype(B16)

    mixed = scatter_tokens(dot(attended, full_o) + dot(gated, full_out))
    hidden = tokens.astype(F32) + mixed
    normed2, unit2, factor2 = normalize(hidden, gain2)
    n2 = gather_tokens(normed2.astype(B16))
    gate, up = dot(n2, full_gate), dot(n2, full_up)
    sigma = jax.nn.sigmoid(gate)
    act = (gate * sigma * up).astype(B16)
    grad_act = dot_nt(all_cotangent, full_down)
    grad_gate = (grad_act * up * sigma * (1.0 + gate * (1.0 - sigma))).astype(B16)
    grad_up = (grad_act * gate * sigma).astype(B16)
    grad_n2 = scatter_tokens(dot_nt(grad_gate, full_gate) + dot_nt(grad_up, full_up))

    def rows_home(grad):
        parts = ring_sum(grad.astype(B16).reshape(groups, near * piece, -1))
        parts = trade_near(parts.astype(B16).reshape(near, piece, -1))
        return parts

    def joined(parts):
        return parts.transpose(1, 0, 2).reshape(piece, -1).astype(F32)

    def cols_home(grad):
        parts = grad.astype(B16).reshape(-1, groups, near * piece).transpose(1, 0, 2)
        parts = ring_sum(parts).astype(B16)
        parts = trade_near(parts.reshape(-1, near, piece).transpose(1, 0, 2))
        return parts.reshape(-1, piece).astype(F32)

    feed = scatter_tokens(dot(act, full_down))
    output = (hidden + feed).astype(B16)
    sum_wgate = joined(rows_home(dot_tn(n2, grad_gate)))
    sum_wup = joined(rows_home(dot_tn(n2, grad_up)))
    sum_wdown = cols_home(dot_tn(act, all_cotangent))

    grad_norm2, grad_g2 = norm_back(grad_n2, unit2, factor2, gain2)
    grad_hidden = cotangent.astype(F32) + grad_norm2
    grad_mixed = gather_tokens(grad_hidden.astype(B16))

    grad_attended = dot_nt(grad_mixed, full_o).astype(B16)
    grad_gated = dot_nt(grad_mixed, full_out).astype(B16).astype(F32)

    sig_z = jax.nn.sigmoid(z_proj)
    grad_y = grad_gated * z_proj * sig_z
    grad_z = (grad_gated * y.reshape(span, -1) * sig_z * (1.0 + z_proj * (1.0 - sig_z))).astype(B16)
    grad_y = grad_y.reshape(near, rows, dt_heads, channels)
    read = exact("cthp,ctn->hpn", grad_y * fade, cmat)
    all_reads = ring_gather(read.astype(B16))

    delta = jnp.sum(grad_attended.astype(F32) * attended32, 1, keepdims=True)
    grad_q, grad_kt, grad_vt = attend_back(
        queries, keys_t, values_t, first_position, grad_attended, lse, delta
    )
    k_parts = grad_kt.astype(B16).reshape(2, near, half_cols, -1).transpose(1, 0, 2, 3)
    v_parts = grad_vt.astype(B16).reshape(near, key_cols, -1)
    kv_parts = jnp.concatenate([k_parts.reshape(near, key_cols, -1), v_parts], 1)
    kv_parts = jnp.sum(trade_near(kv_parts).astype(F32), 0).astype(B16)
    kv_parts = kv_parts.reshape(-1, groups, span).transpose(1, 0, 2)
    kv_parts = lax.all_to_all(kv_parts, "group", 0, 0, tiled=True)
    grad_kv = jnp.sum(kv_parts.astype(F32), 0)
    gk_first, gk_second = rotate_pair(
        grad_kv[:half_cols], grad_kv[half_cols:key_cols], cos_k, -sin_k
    )
    grad_q = jnp.concatenate(rotate_pair(grad_q[:, :half], grad_q[:, half:], cos_q, -sin_q), 1)
    grad_q = grad_q.astype(B16)

    leaving = jnp.zeros_like(entering)
    for turn in reversed(range(1, groups)):
        passed = jnp.exp(all_totals[turn])[:, None, None] * leaving + all_reads[turn].astype(F32)
        leaving = jnp.where(turn > group, passed, leaving)
    grad_scaled, grad_b, grad_c, grad_last = scan_backward(
        scaled, bmat, cmat, cum, states, state_out, grad_y, leaving
    )
    grad_bc = jnp.stack([grad_b, grad_c]).transpose(0, 3, 1, 2).reshape(2, STATE, span).astype(B16)
    kept = lax.dynamic_index_in_dim(grad_bc, core, 0, False)
    given = lax.dynamic_index_in_dim(grad_bc, 1 - core, 0, False)
    kept = (kept.astype(F32) + swap_cores(given).astype(F32)).astype(B16)
    grad_bc = jnp.sum(trade_near(kept.reshape(near, -1, span)).astype(F32), 0)

    grad_cum = jnp.sum(grad_y * outputs - grad_scaled * scaled, -1).transpose(0, 2, 1)
    grad_cum = grad_cum.at[..., -1].add(grad_last)
    grad_logs = exact("cht,ts->chs", grad_cum, triangle)
    grad_logs = grad_logs.transpose(1, 0, 2).reshape(dt_heads, span)
    grad_dt = jnp.sum(grad_scaled * xh, -1).transpose(2, 0, 1).reshape(dt_heads, span)
    grad_dt = grad_dt - grad_logs * decay_rate
    grad_dt_pre = grad_dt * jax.nn.sigmoid(dt_pre)
    grad_dt_low = grad_dt_pre.astype(B16)
    grad_xc = grad_scaled * dt_col + skip[:, None] * grad_y
    grad_skip = jnp.sum(grad_y * xh, (0, 1, 3))
    grad_alog = jnp.sum(grad_logs * logs, 1)
    grad_dtbias = jnp.sum(grad_dt_pre, 1)

    grad_xpre = grad_xc.reshape(span, -1) * silu_slope(x_pre)
    grad_bcpre = grad_bc * silu_slope(bc_pre)
    next_x = step_group(grad_xpre[: CONV - 1], -1)
    next_bc = step_group(grad_bcpre[:, : CONV - 1], -1)
    grad_x, grad_tapx, grad_biasx = conv_back(grad_xpre, next_x, x_proj, x_edge, taps_x, 0)
    grad_bcp, grad_tapbc, grad_biasbc = conv_back(
        grad_bcpre, next_bc, bc_proj, bc_edge, taps_bc, 1
    )
    grad_x = grad_x.astype(B16)
    grad_kvbc = jnp.concatenate([gk_first, gk_second, grad_kv[key_cols:], grad_bcp], 0).astype(B16)

    partial1 = (
        dot_nt(grad_q, full_q)
        + dot(grad_kvbc, full_kvbc, ((0,), (1,)))
        + dot_nt(grad_z, full_z)
        + dot_nt(grad_x, full_x)
        + dot_tn(grad_dt_low, full_dt)
    )
    grad_n1 = scatter_tokens(partial1)
    _, unit1, factor1 = normalize(tokens.astype(F32), gain1)
    grad_norm1, grad_g1 = norm_back(grad_n1, unit1, factor1, gain1)
    grad_tokens = grad_hidden + grad_norm1

    grad3 = jnp.concatenate([dot_tn(attended, grad_mixed), dot_tn(gated, grad_mixed)], 0)
    home3 = grad3.astype(B16).reshape(-1, groups, near * piece).transpose(1, 0, 2)
    home3 = ring_sum(home3).astype(B16)
    home3 = trade_near(home3.reshape(-1, near, piece).transpose(1, 0, 2)).astype(F32)
    sum_wo = home3[:, :o_rows].reshape(-1, piece)
    sum_wout = home3[:, o_rows:].reshape(-1, piece)
    sum_wz = joined(rows_home(dot_tn(n1, grad_z)))
    grad_kvbc_w = dot(n1, grad_kvbc, ((0,), (1,)))
    home1 = rows_home(jnp.concatenate([dot_tn(n1, grad_q), grad_kvbc_w], 1))
    at = [wq_cols, wq_cols + key_cols, wq_cols + 2 * key_cols]
    home_q, home_k, home_v, home_bc = jnp.split(home1, at, 2)
    sum_wq, sum_wv = joined(home_q), joined(home_v)
    sum_wk = home_k.reshape(near, piece, 2, half_cols).transpose(1, 2, 0, 3)
    sum_wk = sum_wk.reshape(piece, -1).astype(F32)
    bc_mine = joined(home_bc).astype(B16)
    sum_wbc = both_halves(bc_mine, swap_cores(bc_mine), 1).astype(F32)
    sum_wx = joined(rows_home(dot_tn(n1, grad_x)))
    grad_wdt = dot(grad_dt_low, n1)
    dt_parts = jnp.pad(grad_wdt.astype(B16), ((0, -dt_heads % 8), (0, 0)))
    dt_parts = ring_sum(dt_parts.reshape(-1, groups, near * piece).transpose(1, 0, 2)).astype(B16)
    dt_parts = trade_near(dt_parts.reshape(-1, near, piece).transpose(1, 0, 2))
    sum_wdt = dt_parts[:, :dt_heads].reshape(-1, piece).T.astype(F32)

    grads_bc = jnp.concatenate([grad_tapbc.reshape(-1), grad_biasbc])
    other_bc = swap_cores(grads_bc)
    mine = [grad_g1, grad_g2, grad_tapx.reshape(-1), grad_biasx, grad_dtbias, grad_alog, grad_skip]
    mine = [*mine, both_halves(grads_bc, other_bc, 0)]
    ends, at = [], 0
    for g in mine[:-1]:
        at += g.shape[0]
        ends.append(at)
    packed = jnp.concatenate(mine)
    packed = lax.all_to_all(
        jnp.broadcast_to(packed, (devices, packed.shape[0])), ("group", "near"), 0, 0, tiled=True
    )
    every = jnp.split(packed, ends, 1)
    place = group * near + here

    def own(x):
        return lax.dynamic_slice_in_dim(jnp.sum(x, 0), place * piece, piece, 0)

    def by_near(x):
        return jnp.sum(x.reshape(groups, near, -1), 0)

    sum_g1, sum_g2 = own(every[0]), own(every[1])
    sum_convx = by_near(every[2]).reshape(near, CONV, -1).transpose(1, 0, 2).reshape(CONV, -1)
    sum_convxb, sum_dtbias, sum_alog, sum_dskip = (by_near(x).reshape(-1) for x in every[3:7])
    sum_bc = by_near(every[7]).reshape(near, 2, CONV + 1, -1).transpose(2, 1, 0, 3)
    sum_bc = sum_bc.reshape(CONV + 1, -1)
    bc_cols = conv_bc.shape[1]
    sum_bc = lax.dynamic_slice_in_dim(sum_bc, place * bc_cols, bc_cols, 1)
    return (
        output,
        grad_tokens,
        sum_g1,
        sum_wq,
        sum_wk,
        sum_wv,
        sum_wo,
        sum_wz,
        sum_wx,
        sum_wbc,
        sum_wdt,
        sum_bc[:CONV],
        sum_bc[CONV],
        sum_wout,
        sum_g2,
        sum_wgate,
        sum_wup,
        sum_wdown,
        sum_convx,
        sum_convxb,
        sum_dtbias,
        sum_alog,
        sum_dskip,
    )


def solution(mesh):
    seq, cores = mesh.shape["seq"], mesh.shape["head"]
    near = math.gcd(seq, 4)
    split = Mesh(mesh.devices.reshape(seq // near, near, cores), ("group", "near", "head"))
    seq = ("group", "near")
    row_split = P(seq, "head")
    col_split = P("head", seq)
    weights = (
        P(seq),
        row_split,
        row_split,
        row_split,
        col_split,
        row_split,
        row_split,
        P(seq, None),
        row_split,
        P(None, seq),
        P(seq),
        col_split,
        P(seq),
        row_split,
        row_split,
        col_split,
        P(None, "head"),
        P("head"),
        P("head"),
        P("head"),
        P("head"),
    )
    tokens = P(seq, None)
    return jax.shard_map(
        per_device,
        mesh=split,
        in_specs=(tokens, tokens, *weights),
        out_specs=(tokens, tokens, *weights),
        check_vma=False,
    )
```

time: 4000 us -> 1080 us (0.27)
  waiting for transfers between devices: 3070 us -> 321 us
  blocking collectives: 430 us -> 18.9 us
  local copies, waits for them, and re-layouts: 52.8 us -> 202 us
  starting transfers between devices: 15.4 us -> 161 us
  matrix products: 274 us -> 215 us
    reduce_scatter x12 -> x0, waiting for transfers between devices: 2130 us -> none  [the longest x1 355 us: reduce_mlp(): lax.psum_scatter(down_grad, 'seq', scatter_dimension=1, tiled=True)]
    all_gather x13 -> x0, waiting for transfers between devices: 844 us -> none  [the longest x1 251 us: entering(): gathered = jax.tree.map(lambda a: lax.all_gather(a, axis), part)]
    all_gather x8 -> x0, blocking collectives: 318 us -> none  [the longest x1 43.4 us: per_device(): lax.all_gather(w_v, 'seq', axis=0, tiled=True)]
    ppermute x4 -> x74, waiting for transfers between devices: 3.41 us -> 226 us  [the longest x30 125 us: ring_gather(): x = lax.ppermute(x, 'group', ring_route('group'))]
    all_to_all x1 -> x28, starting transfers between devices: 4.57 us -> 117 us  [the longest x25 103 us: trade_near(): return lax.all_to_all(x, 'near', 0, 0, tiled=True)]
    unnamed x2 -> x0, blocking collectives: 109 us -> none
    all_to_all x1 -> x28, waiting for transfers between devices: 31.9 us -> 94.6 us  [the longest x25 76.9 us: trade_near(): return lax.all_to_all(x, 'near', 0, 0, tiled=True)]
    dot_general x76 -> x52, matrix products: 274 us -> 215 us  [the longest x36 160 us: dot(): lax.dot_general(left, right, (dims, ((), ())), preferred_element_type=F32)]
  transfers between devices with their start and end apart: 34 -> 102, of which waited for: 24 -> 51; matrix products, arithmetic and copies ran while one was open for 8% -> 36% of each run, Pallas kernels for 0% -> 0%
where the time goes in v1:
time: 1080 us; the launch traced here: 1060 us
  waiting for transfers between devices  321 us (30%)
  matrix products  215 us (20%)
  local copies, waits for them, and re-layouts  202 us (19%)
  starting transfers between devices  161 us (15%)
  other arithmetic  141 us (13%)
  blocking collectives  18.9 us (2%)
    dot_general x36, matrix products, dot(): lax.dot_general(left, right, (dims, ((), ())), preferred_element_type=F32)  160 us
    ppermute x30, waiting for transfers between devices, ring_gather(): x = lax.ppermute(x, 'group', ring_route('group'))  125 us
    all_to_all x25, starting transfers between devices, trade_near(): return lax.all_to_all(x, 'near', 0, 0, tiled=True)  103 us
    ppermute x24, waiting for transfers between devices, ring_sum(): moving = lax.ppermute(moving, 'group', ring_route('group'))  91.5 us
    all_to_all x25, waiting for transfers between devices, trade_near(): return lax.all_to_all(x, 'near', 0, 0, tiled=True)  76.9 us
    dot_general x16, matrix products, exact(): return jnp.einsum(spec, *operands, precision=HIGHEST)  55 us
    unnamed x458, local copies, waits for them, and re-layouts  51.5 us
    dynamic_update_slice x31, local copies, waits for them, and re-layouts, ring_gather(): held = lax.dynamic_update_index_in_dim(held, x, (place - turn) % count, 0)  39.2 us
  transfers between devices with their start and end apart: 102, of which 51 were waited for; matrix products, arithmetic and copies ran while one was open for 36% of the time, Pallas kernels for 0%

profile of v1, /device:TPU:0, one launch (start us, length us, event | category | flops | bytes accessed | tf_op | source)
XLA Modules:
  0.0 1063.9 jit_solution(15247323090113676349)
XLA Ops:
  61.4 11.2 %collective-permute-done.14 = bf16[8,512]{1,0:T(8,128)(2,1)S(1)} collective-permute-done((bf16[8,512]{1,0:T(8,128)(2,1)S(1)}, bf16[8,512]{1,0:T(8,128)(2,1)S(1)}, u32[]{:S(2)}, u32[]{:S(2)}) %collective-permute-start.14) | collective-permute-done | bytes 8224 | tf_op jit(solution)/shard_map/ppermute | solution.py:69
  94.6 9.1 collective-permute-done.7
  241.7 8.1 fusion.12
  264.4 8.0 collective-permute-done.23
  273.4 6.5 collective-permute-done.24
  287.9 7.0 multiply_convert_fusion.4
  303.9 7.8 fusion.283
  311.7 8.1 fusion
  319.8 7.8 fusion.8
  341.0 18.9 %all_to_all.150 = bf16[4,128,1024]{1,2,0:T(8,128)(2,1)} all-to-all(bf16[4,128,1024]{1,2,0:T(8,128)(2,1)S(1)} %pad_maximum_fusion.14), channel_id=1, replica_groups=mesh['group'=4,'near'=4,'head'=2] {'near'}, dimensions={0} | all-to-all | bytes 2097152 | tf_op jit(solution)/shard_map/all_to_all | solution.py:28
  381.4 19.3 %all-to-all-done.8 = bf16[4,256,1024]{2,1,0:T(8,128)(2,1)S(1)} async-done(((bf16[4,256,1024]{2,1,0:T(8,128)(2,1)}), bf16[4,256,1024]{2,1,0:T(8,128)(2,1)S(1)}, u32[]{:S(2)}, u32[]{:S(2)}) %all-to-all-start.8) | async-done | bytes 2097184 | tf_op jit(solution)/shard_map/all_to_all | solution.py:28
  409.4 22.8 %all-to-all-done.13 = bf16[4,256,1024]{2,1,0:T(8,128)(2,1)} async-done(((bf16[4,256,1024]{2,1,0:T(8,128)(2,1)}), bf16[4,256,1024]{2,1,0:T(8,128)(2,1)}, u32[]{:S(2)}, u32[]{:S(2)}) %all-to-all-start.13) | async-done | bytes 2097184 | tf_op jit(solution)/shard_map/all_to_all | solution.py:28
  451.4 8.6 collective-permute-done.30
  467.1 8.5 collective-permute-done.31
  478.1 9.7 collective-permute-done.32
  489.2 9.9 collective-permute-done.33
  539.4 15.8 %collective-permute-done.68 = bf16[512,512]{1,0:T(8,128)(2,1)S(1)} collective-permute-done((bf16[512,512]{1,0:T(8,128)(2,1)S(1)}, bf16[512,512]{1,0:T(8,128)(2,1)S(1)}, u32[]{:S(2)}, u32[]{:S(2)}) %collective-permute-start.68) | collective-permute-done | bytes 524320 | tf_op jit(solution)/shard_map/ppermute | solution.py:82
  562.5 8.9 collective-permute-done.69
  580.1 6.6 collective-permute-done.70
  643.8 9.2 collective-permute-done.66
  654.3 9.9 collective-permute-done.72
  666.6 8.8 collective-permute-done.67
  724.4 8.3 multiply_reduce_fusion
  732.7 9.9 fusion.15
  742.7 7.8 multiply_convert_fusion
  776.7 7.1 fusion.286
  811.2 13.2 %collective-permute-done.41 = bf16[6,64,256]{2,1,0:T(8,128)(2,1)S(1)} collective-permute-done((bf16[6,64,256]{2,1,0:T(8,128)(2,1)S(1)}, bf16[6,64,256]{2,1,0:T(8,128)(2,1)S(1)}, u32[]{:S(2)}, u32[]{:S(2)}) %collective-permute-start.41) | collective-permute-done | bytes 196640 | tf_op jit(solution)/shard_map/ppermute | solution.py:69
  874.9 7.1 fusion.73
  907.9 12.8 %add_add_fusion = f32[1024,2048]{1,0:T(8,128)} fusion(f32[1024,2048]{1,0:T(8,128)} %fusion.73, f32[1024,2048]{1,0:T(8,128)} %fusion.286, f32[1024,2048]{1,0:T(8,128)} %fusion.137, f32[1024,2048]{1,0:T(8,128)S(1)} %fusion.133, bf16[6,2048]{1,0:T(8,128)(2,1)S(1)} %bitcast.804, bf16[6,1024]{1,0:T(8,128)(2,1)S(1)} %get-tuple-element.274), kind=kOutput, calls=%fused_computation.14 | convolution fusion | flops 33554432 | bytes 41979904 | tf_op jit(solution)/shard_map/dot_general | solution.py:96
  946.6 9.2 collective-permute-done.54
  986.5 9.9 collective-permute-done.59
  1047.4 9.3 all-to-all-done.20
  (985 shorter events, 734.6 us)
Async XLA Ops:
  52.1 33.7 %all-to-all-start = ((bf16[4,256,1024]{2,1,0:T(8,128)(2,1)}), bf16[4,256,1024]{2,1,0:T(8,128)(2,1)S(1)}, u32[]{:S(2)}, u32[]{:S(2)}) async-start(bf16[4,256,1024]{2,1,0:T(8,128)(2,1)} %broadcast_in_dim.235), calls=%async_computation | async-start | bytes 4194304 | tf_op jit(solution)/shard_map/all_to_all | solution.py:28
  85.9 44.8 %collective-permute-start = (bf16[1024,1024]{1,0:T(8,128)(2,1)S(1)}, bf16[1024,1024]{1,0:T(8,128)(2,1)}, u32[]{:S(2)}, u32[]{:S(2)}) collective-permute-start(bf16[1024,1024]{1,0:T(8,128)(2,1)S(1)} %bitcast.733), channel_id=1, source_target_pairs={{0,1},{1,0},{2,3},{3,2},{4,5},{5,4},{6,7},{7,6},{8,9},{9,8},{10,11... | collective-permute-start | bytes 6291464 | tf_op jit(solution)/shard_map/ppermute | solution.py:24
  126.0 102.3 %collective-permute-start.10 = (bf16[4,512,128]{2,1,0:T(8,128)(2,1)}, bf16[4,512,128]{2,1,0:T(8,128)(2,1)}, u32[]{:S(2)}, u32[]{:S(2)}) collective-permute-start(bf16[4,512,128]{2,1,0:T(8,128)(2,1)} %all-to-all-done.5), channel_id=1, source_target_pairs={{0,8},{8,16},{16,24},{24,0},{1,9},{9,17},{17,25},{25,1},{2,10},{10... | collective-permute-start | bytes 1572872 | tf_op jit(solution)/shard_map/ppermute | solution.py:69
  150.4 35.6 %collective-permute-start.17 = (f32[64,3]{1,0:T(8,128)}, f32[64,3]{1,0:T(8,128)}, u32[]{:S(2)}, u32[]{:S(2)}) collective-permute-start(f32[64,3]{1,0:T(8,128)} %slice.398), channel_id=1, source_target_pairs={{0,8},{8,16},{16,24},{1,9},{9,17},{17,25},{2,10},{10,18},{18,26},{... | collective-permute-start | bytes 2312 | tf_op jit(solution)/shard_map/ppermute | solution.py:92
  155.9 36.8 %collective-permute-start.13 = (f32[3,384]{1,0:T(4,128)}, f32[3,384]{1,0:T(4,128)}, u32[]{:S(2)}, u32[]{:S(2)}) collective-permute-start(f32[3,384]{1,0:T(4,128)} %slice.387), channel_id=1, source_target_pairs={{0,8},{8,16},{16,24},{1,9},{9,17},{17,25},{2,10},{10,18},{18,26},{... | collective-permute-start | bytes 13832 | tf_op jit(solution)/shard_map/ppermute | solution.py:92
  167.5 33.7 %collective-permute-start.4 = (bf16[64,1024]{1,0:T(8,128)(2,1)}, bf16[64,1024]{1,0:T(8,128)(2,1)}, u32[]{:S(2)}, u32[]{:S(2)}) collective-permute-start(bf16[64,1024]{1,0:T(8,128)(2,1)} %pad_maximum_fusion.28), channel_id=1, source_target_pairs={{0,8},{8,16},{16,24},{24,0},{1,9},{9,17},{17,25},{25,1},{2,10},{10... | collective-permute-start | bytes 393224 | tf_op jit(solution)/shard_map/ppermute | solution.py:69
  201.3 30.9 %collective-permute-start.18 = (bf16[256,1024]{1,0:T(8,128)(2,1)S(1)}, bf16[256,1024]{1,0:T(8,128)(2,1)}, u32[]{:S(2)}, u32[]{:S(2)}) collective-permute-start(bf16[256,1024]{1,0:T(8,128)(2,1)S(1)} %bitcast.759), channel_id=1, source_target_pairs={{0,1},{1,0},{2,3},{3,2},{4,5},{5,4},{6,7},{7,6},{8,9},{9,8},{10,11... | collective-permute-start | bytes 1572872 | tf_op jit(solution)/shard_map/ppermute | solution.py:24
  223.8 76.4 %all-to-all-start.3 = ((bf16[4,4,64,1024]{3,1,2,0:T(4,128)(2,1)}), bf16[4,4,64,1024]{3,1,2,0:T(4,128)(2,1)}, u32[]{:S(2)}, u32[]{:S(2)}) async-start(bf16[4,4,64,1024]{3,1,2,0:T(4,128)(2,1)} %broadcast_in_dim.246), calls=%async_computation.3 | async-start | bytes 4194304 | tf_op jit(solution)/shard_map/all_to_all | solution.py:28
  256.0 38.9 %collective-permute-start.12 = (bf16[4,512,128]{2,1,0:T(8,128)(2,1)}, bf16[4,512,128]{2,1,0:T(8,128)(2,1)}, u32[]{:S(2)}, u32[]{:S(2)}) collective-permute-start(bf16[4,512,128]{2,1,0:T(8,128)(2,1)} %collective-permute-done.11), channel_id=1, source_target_pairs={{0,8},{8,16},{16,24},{24,0},{1,9},{9,17},{17,25},{25,1},{2,10},{10... | collective-permute-start | bytes 1572872 | tf_op jit(solution)/shard_map/ppermute | solution.py:69
  335.6 30.5 %collective-permute-start.25 = (bf16[1024,1024]{1,0:T(8,128)(2,1)S(1)}, bf16[1024,1024]{1,0:T(8,128)(2,1)}, u32[]{:S(2)}, u32[]{:S(2)}) collective-permute-start(bf16[1024,1024]{1,0:T(8,128)(2,1)S(1)} %dynamic-slice_convert_fusion.3), channel_id=1, source_target_pairs={{0,1},{1,0},{2,3},{3,2},{4,5},{5,4},{6,7},{7,6},{8,9},{9,8},{10,11... | collective-permute-start | bytes 6291464 | tf_op jit(solution)/shard_map/ppermute | solution.py:24
  373.6 27.1 %all-to-all-start.8 = ((bf16[4,256,1024]{2,1,0:T(8,128)(2,1)}), bf16[4,256,1024]{2,1,0:T(8,128)(2,1)S(1)}, u32[]{:S(2)}, u32[]{:S(2)}) async-start(bf16[4,256,1024]{2,1,0:T(8,128)(2,1)} %bitcast.737), calls=%async_computation.8 | async-start | bytes 4194304 | tf_op jit(solution)/shard_map/all_to_all | solution.py:28
  379.5 28.3 %collective-permute-start.28 = (bf16[512,1024]{1,0:T(8,128)(2,1)}, bf16[512,1024]{1,0:T(8,128)(2,1)}, u32[]{:S(2)}, u32[]{:S(2)}) collective-permute-start(bf16[512,1024]{1,0:T(8,128)(2,1)} %bitcast.746), channel_id=1, source_target_pairs={{0,8},{8,16},{16,24},{24,0},{1,9},{9,17},{17,25},{25,1},{2,10},{10... | collective-permute-start | bytes 3145736 | tf_op jit(solution)/shard_map/ppermute | solution.py:69
  403.3 29.0 %all-to-all-start.13 = ((bf16[4,256,1024]{2,1,0:T(8,128)(2,1)}), bf16[4,256,1024]{2,1,0:T(8,128)(2,1)}, u32[]{:S(2)}, u32[]{:S(2)}) async-start(bf16[4,256,1024]{2,1,0:T(8,128)(2,1)} %broadcast_in_dim.285), calls=%async_computation.13 | async-start | bytes 4194304 | tf_op jit(solution)/shard_map/all_to_all | solution.py:28
  407.8 26.5 %collective-permute-start.29 = (bf16[512,1024]{1,0:T(8,128)(2,1)}, bf16[512,1024]{1,0:T(8,128)(2,1)}, u32[]{:S(2)}, u32[]{:S(2)}) collective-permute-start(bf16[512,1024]{1,0:T(8,128)(2,1)} %collective-permute-done.28), channel_id=1, source_target_pairs={{0,8},{8,16},{16,24},{24,0},{1,9},{9,17},{17,25},{25,1},{2,10},{10... | collective-permute-start | bytes 3145736 | tf_op jit(solution)/shard_map/ppermute | solution.py:69
  432.3 43.3 %collective-permute-start.36 = (bf16[1024,1024]{1,0:T(8,128)(2,1)}, bf16[1024,1024]{1,0:T(8,128)(2,1)}, u32[]{:S(2)}, u32[]{:S(2)}) collective-permute-start(bf16[1024,1024]{1,0:T(8,128)(2,1)} %bitcast.123), channel_id=1, source_target_pairs={{0,1},{1,0},{2,3},{3,2},{4,5},{5,4},{6,7},{7,6},{8,9},{9,8},{10,11... | collective-permute-start | bytes 6291464 | tf_op jit(solution)/shard_map/ppermute | solution.py:24
  438.8 28.3 %all-to-all-start.9 = ((bf16[4,256,1024]{2,1,0:T(8,128)(2,1)}), bf16[4,256,1024]{2,1,0:T(8,128)(2,1)}, u32[]{:S(2)}, u32[]{:S(2)}) async-start(bf16[4,256,1024]{2,1,0:T(8,128)(2,1)} %broadcast_in_dim.275), calls=%async_computation.9 | async-start | bytes 4194304 | tf_op jit(solution)/shard_map/all_to_all | solution.py:28
  467.1 34.4 %collective-permute-start.27 = (bf16[1024,1024]{1,0:T(8,128)(2,1)}, bf16[1024,1024]{1,0:T(8,128)(2,1)S(1)}, u32[]{:S(2)}, u32[]{:S(2)}) collective-permute-start(bf16[1024,1024]{1,0:T(8,128)(2,1)} %bitcast.104), channel_id=1, source_target_pairs={{0,1},{1,0},{2,3},{3,2},{4,5},{5,4},{6,7},{7,6},{8,9},{9,8},{10,11... | collective-permute-start | bytes 6291464 | tf_op jit(solution)/shard_map/ppermute | solution.py:24
  529.8 30.4 %all-to-all-start.14 = ((bf16[4,256,1024]{2,1,0:T(8,128)(2,1)}), bf16[4,256,1024]{2,1,0:T(8,128)(2,1)}, u32[]{:S(2)}, u32[]{:S(2)}) async-start(bf16[4,256,1024]{2,1,0:T(8,128)(2,1)} %bitcast.734), calls=%async_computation.14 | async-start | bytes 4194304 | tf_op jit(solution)/shard_map/all_to_all | solution.py:28
  562.4 30.5 %collective-permute-start.38 = (f32[256,1024]{1,0:T(8,128)S(1)}, f32[256,1024]{1,0:T(8,128)}, u32[]{:S(2)}, u32[]{:S(2)}) collective-permute-start(f32[256,1024]{1,0:T(8,128)S(1)} %convert_reduce_fusion.1), channel_id=1, source_target_pairs={{0,1},{1,0},{2,3},{3,2},{4,5},{5,4},{6,7},{7,6},{8,9},{9,8},{10,11... | collective-permute-start | bytes 3145736 | tf_op jit(solution)/shard_map/ppermute | solution.py:24
  580.1 47.1 %collective-permute-start.34 = (bf16[1024,1024]{1,0:T(8,128)(2,1)}, bf16[1024,1024]{1,0:T(8,128)(2,1)}, u32[]{:S(2)}, u32[]{:S(2)}) collective-permute-start(bf16[1024,1024]{1,0:T(8,128)(2,1)} %dynamic-slice_convert_fusion.2), channel_id=1, source_target_pairs={{0,1},{1,0},{2,3},{3,2},{4,5},{5,4},{6,7},{7,6},{8,9},{9,8},{10,11... | collective-permute-start | bytes 6291464 | tf_op jit(solution)/shard_map/ppermute | solution.py:24
  601.1 31.1 %all-to-all-start.15 = ((bf16[4,256,1024]{2,1,0:T(8,128)(2,1)}), bf16[4,256,1024]{2,1,0:T(8,128)(2,1)}, u32[]{:S(2)}, u32[]{:S(2)}) async-start(bf16[4,256,1024]{2,1,0:T(8,128)(2,1)} %broadcast_in_dim.286), calls=%async_computation.15 | async-start | bytes 4194304 | tf_op jit(solution)/shard_map/all_to_all | solution.py:28
  632.2 44.1 %all-to-all-start.12 = ((bf16[4,256,1024]{2,1,0:T(8,128)(2,1)}), bf16[4,256,1024]{2,1,0:T(8,128)(2,1)S(1)}, u32[]{:S(2)}, u32[]{:S(2)}) async-start(bf16[4,256,1024]{2,1,0:T(8,128)(2,1)} %bitcast.736), calls=%async_computation.12 | async-start | bytes 4194304 | tf_op jit(solution)/shard_map/all_to_all | solution.py:28
  665.1 36.1 %collective-permute-start.39 = (bf16[1024,1024]{1,0:T(8,128)(2,1)}, bf16[1024,1024]{1,0:T(8,128)(2,1)}, u32[]{:S(2)}, u32[]{:S(2)}) collective-permute-start(bf16[1024,1024]{1,0:T(8,128)(2,1)} %bitcast.126), channel_id=1, source_target_pairs={{0,1},{1,0},{2,3},{3,2},{4,5},{5,4},{6,7},{7,6},{8,9},{9,8},{10,11... | collective-permute-start | bytes 6291464 | tf_op jit(solution)/shard_map/ppermute | solution.py:24
  788.2 82.6 %all-to-all-start.16 = ((bf16[4,64,4096]{2,1,0:T(8,128)(2,1)}), bf16[4,64,4096]{2,1,0:T(8,128)(2,1)}, u32[]{:S(2)}, u32[]{:S(2)}) async-start(bf16[4,64,4096]{2,1,0:T(8,128)(2,1)} %pad_maximum_fusion.7), calls=%async_computation.16 | async-start | bytes 4194304 | tf_op jit(solution)/shard_map/all_to_all | solution.py:28
  802.4 26.8 %collective-permute-start.52 = (bf16[512,512]{1,0:T(8,128)(2,1)}, bf16[512,512]{1,0:T(8,128)(2,1)}, u32[]{:S(2)}, u32[]{:S(2)}) collective-permute-start(bf16[512,512]{1,0:T(8,128)(2,1)} %dynamic-slice_bitcast_fusion.2), channel_id=1, source_target_pairs={{0,8},{8,16},{16,24},{24,0},{1,9},{9,17},{17,25},{25,1},{2,10},{10... | collective-permute-start | bytes 1572872 | tf_op jit(solution)/shard_map/ppermute | solution.py:82
  826.7 101.9 %collective-permute-start.56 = (bf16[512,384]{1,0:T(8,128)(2,1)}, bf16[512,384]{1,0:T(8,128)(2,1)}, u32[]{:S(2)}, u32[]{:S(2)}) collective-permute-start(bf16[512,384]{1,0:T(8,128)(2,1)} %fusion.118), channel_id=1, source_target_pairs={{0,8},{8,16},{16,24},{24,0},{1,9},{9,17},{17,25},{25,1},{2,10},{10... | collective-permute-start | bytes 1179656 | tf_op jit(solution)/shard_map/ppermute | solution.py:82
  831.4 99.6 %collective-permute-start.53 = (bf16[512,512]{1,0:T(8,128)(2,1)}, bf16[512,512]{1,0:T(8,128)(2,1)}, u32[]{:S(2)}, u32[]{:S(2)}) collective-permute-start(bf16[512,512]{1,0:T(8,128)(2,1)} %fusion.106), channel_id=1, source_target_pairs={{0,8},{8,16},{16,24},{24,0},{1,9},{9,17},{17,25},{25,1},{2,10},{10... | collective-permute-start | bytes 1572872 | tf_op jit(solution)/shard_map/ppermute | solution.py:82
  852.9 39.8 %collective-permute-start.62 = (bf16[8,512]{1,0:T(8,128)(2,1)S(1)}, bf16[8,512]{1,0:T(8,128)(2,1)S(1)}, u32[]{:S(2)}, u32[]{:S(2)}) collective-permute-start(bf16[8,512]{1,0:T(8,128)(2,1)S(1)} %fusion.237), channel_id=1, source_target_pairs={{0,8},{8,16},{16,24},{24,0},{1,9},{9,17},{17,25},{25,1},{2,10},{10... | collective-permute-start | bytes 24584 | tf_op jit(solution)/shard_map/ppermute | solution.py:82
  892.7 34.5 %collective-permute-start.63 = (bf16[8,512]{1,0:T(8,128)(2,1)S(1)}, bf16[8,512]{1,0:T(8,128)(2,1)S(1)}, u32[]{:S(2)}, u32[]{:S(2)}) collective-permute-start(bf16[8,512]{1,0:T(8,128)(2,1)S(1)} %fusion.235), channel_id=1, source_target_pairs={{0,8},{8,16},{16,24},{24,0},{1,9},{9,17},{17,25},{25,1},{2,10},{10... | collective-permute-start | bytes 24584 | tf_op jit(solution)/shard_map/ppermute | solution.py:82
  924.8 46.2 %collective-permute-start.46 = (bf16[1024,1024]{1,0:T(8,128)(2,1)}, bf16[1024,1024]{1,0:T(8,128)(2,1)}, u32[]{:S(2)}, u32[]{:S(2)}) collective-permute-start(bf16[1024,1024]{1,0:T(8,128)(2,1)} %dynamic-slice_convert_fusion), channel_id=1, source_target_pairs={{0,1},{1,0},{2,3},{3,2},{4,5},{5,4},{6,7},{7,6},{8,9},{9,8},{10,11... | collective-permute-start | bytes 6291464 | tf_op jit(solution)/shard_map/ppermute | solution.py:24
  933.4 48.4 %collective-permute-start.58 = (bf16[512,384]{1,0:T(8,128)(2,1)}, bf16[512,384]{1,0:T(8,128)(2,1)}, u32[]{:S(2)}, u32[]{:S(2)}) collective-permute-start(bf16[512,384]{1,0:T(8,128)(2,1)} %dynamic-slice_bitcast_fusion.3), channel_id=1, source_target_pairs={{0,8},{8,16},{16,24},{24,0},{1,9},{9,17},{17,25},{25,1},{2,10},{10... | collective-permute-start | bytes 1179656 | tf_op jit(solution)/shard_map/ppermute | solution.py:82
  978.2 33.7 %all-to-all-start.19 = ((bf16[4,256,1024]{2,1,0:T(8,128)(2,1)}), bf16[4,256,1024]{2,1,0:T(8,128)(2,1)S(1)}, u32[]{:S(2)}, u32[]{:S(2)}) async-start(bf16[4,256,1024]{2,1,0:T(8,128)(2,1)} %bitcast.735), calls=%async_computation.19 | async-start | bytes 4194304 | tf_op jit(solution)/shard_map/all_to_all | solution.py:28
  (283 other events, 3563.0 us)

commit v2 on v1

v2 whole, which is shorter than its diff:
```python
import functools
import math

import jax
import jax.numpy as jnp
from jax import lax
from jax.experimental import pallas as pl
from jax.experimental.pallas import tpu as pltpu
from jax.sharding import Mesh, PartitionSpec as P

HEAD_DIM = 128
STATE = 256
CONV = 4
EPS = 1e-05
ROPE_BASE = 100000000000.0
MASKED = -1e30
HIGHEST = lax.Precision.HIGHEST
F32 = jnp.float32
B16 = jnp.bfloat16
ATTEND_ROWS = 256
ATTEND_KEYS = 512
VMEM_LIMIT = 40 << 20


def after(x, *earlier):
    return lax.optimization_barrier((x, earlier))[0]


def swap_cores(x):
    return lax.ppermute(x, "head", [(0, 1), (1, 0)])


def to_near(x, k):
    return lax.ppermute(x, "near", [(i, i ^ k) for i in range(lax.axis_size("near"))])


def around(x, distance):
    count = lax.axis_size("group")
    return lax.ppermute(x, "group", [(i, (i + distance) % count) for i in range(count)])


def step_group(x, distance):
    count = lax.axis_size("group")
    route = [(i, i + distance) for i in range(count) if 0 <= i + distance < count]
    return lax.ppermute(x, "group", route)


def place_kernel(index, *refs):
    *blocks, out = refs
    for k, block in enumerate(blocks):
        out[index[k]] = block[...]


def placed(index, blocks):
    shape = jax.ShapeDtypeStruct((len(blocks), *blocks[0].shape), blocks[0].dtype)
    return whole_call(place_kernel, shape, [], 0, jnp.stack(index).astype(jnp.int32), *blocks)


def near_places():
    here = lax.axis_index("near")
    return [here ^ k for k in range(lax.axis_size("near"))]


def sent_near(x):
    blocks = [lax.dynamic_index_in_dim(x, at, 0, False) for at in near_places()]
    return [to_near(b, k) if k else b for k, b in enumerate(blocks)]


def trade_near(x):
    return placed(near_places(), sent_near(x))


def added(blocks):
    total = blocks[0].astype(F32)
    for block in blocks[1:]:
        total = total + block.astype(F32)
    return total


def gather_near(x):
    places = near_places()
    return placed(places, [x] + [to_near(x, k) for k in range(1, len(places))])


def gather_groups(x):
    count, group = lax.axis_size("group"), lax.axis_index("group")
    places = [(group - r) % count for r in range(count)]
    return placed(places, [x] + [around(x, r) for r in range(1, count)])


def trade_all(x):
    return lax.all_to_all(x, ("group", "near"), 0, 0, tiled=True)


def both_halves(mine, other, dim):
    first = lax.axis_index("head") == 0
    return jnp.concatenate([jnp.where(first, mine, other), jnp.where(first, other, mine)], dim)


def own_half(x):
    half = x.shape[0] // 2
    return lax.dynamic_slice_in_dim(x, lax.axis_index("head") * half, half, 0)


def tokens_kernel(gained, index, *refs):
    *refs, out = refs
    gain = refs.pop()[...] if gained else None
    count = len(refs) // 2
    for k in range(count):
        for side in range(2):
            value = refs[k + side * count][...]
            if gained:
                value = value.astype(F32)
                power = jnp.mean(value * value, 1, keepdims=True)
                value = (value * lax.rsqrt(power + EPS) * gain).astype(B16)
            out[index[k], index[count + side]] = value


def sent_tokens(mine):
    got = [mine] + [to_near(mine, k) for k in range(1, lax.axis_size("near"))]
    return [*got, *map(swap_cores, got)]


def placed_tokens(parts, gain=None):
    core, places = lax.axis_index("head"), near_places()
    rows, width = parts[0].shape
    index = jnp.stack([*places, core, 1 - core]).astype(jnp.int32)
    operands = [index, *parts]
    if gain is not None:
        operands.append(gain[None, :])
    shape = jax.ShapeDtypeStruct((len(places), 2, rows, width), parts[0].dtype)
    kernel = functools.partial(tokens_kernel, gain is not None)
    return whole_call(kernel, shape, [], 8 * shape.size, *operands).reshape(-1, width)


def gather_tokens(mine):
    return placed_tokens(sent_tokens(mine))


def dots_kernel(turned, core, *refs):
    *refs, give, keep = refs
    pairs = len(turned)
    for out, side in (give, 1 - core[0]), (keep, core[0]):
        lefts = []
        for left in refs[:pairs]:
            blocks = [left[j, side] for j in range(left.shape[0])]
            lefts.append(jnp.concatenate(blocks, 0))
        width = out.shape[1]
        tile = min(width, 512)
        for n in range(width // tile):
            cols = slice(n * tile, (n + 1) * tile)
            total = None
            for left, right, turn in zip(lefts, refs[pairs:], turned):
                part = dot_nt(left, right[cols]) if turn else dot(left, right[:, cols])
                total = part if total is None else total + part
            out[:, cols] = total.astype(B16)


def summed_dots(width, *pairs):
    lefts, rights, specs, turned, work = [], [], [], [], 0
    near = lax.axis_size("near")
    for left, right in pairs:
        span, depth = left.shape
        lefts.append(left.reshape(near, 2, span // near // 2, depth))
        turned.append(isinstance(right, tuple))
        array, at = right if turned[-1] else (right, 0)
        shape = (width, depth) if turned[-1] else array.shape
        specs.append(pl.BlockSpec(shape, lambda i, at=at: (0, at)))
        rights.append(array)
        work += 2 * span * width * depth
    smem = pl.BlockSpec(memory_space=pltpu.SMEM)
    wholes = [pl.BlockSpec(a.shape, lambda i: (0, 0, 0, 0)) for a in lefts]
    shape = (lefts[0].shape[0] * lefts[0].shape[2], width)
    return pl.pallas_call(
        functools.partial(dots_kernel, turned),
        grid=(1,),
        in_specs=[smem, *wholes, *specs],
        out_specs=[pl.BlockSpec(shape, lambda i: (0, 0))] * 2,
        out_shape=[jax.ShapeDtypeStruct(shape, B16)] * 2,
        cost_estimate=pl.CostEstimate(flops=work, bytes_accessed=4 << 20, transcendentals=0),
        compiler_params=pltpu.CompilerParams(vmem_limit_bytes=VMEM_LIMIT),
    )(lax.axis_index("head").astype(jnp.int32).reshape(1), *lefts, *rights)


def grads_kernel(count, *refs):
    *refs, out = refs
    at = 0
    for left, right in zip(refs[:count], refs[count:]):
        cols = slice(at, at + right.shape[1])
        out[:, cols] = dot_tn(left[...], right[...]).astype(B16)
        at = cols.stop


def joined_grads(*pairs):
    lefts, rights = zip(*pairs)
    span, width = lefts[0].shape
    total = sum(r.shape[1] for r in rights)
    tile = min(width, 512)
    return pl.pallas_call(
        functools.partial(grads_kernel, len(pairs)),
        grid=(width // tile,),
        in_specs=[pl.BlockSpec((span, tile), lambda i: (0, i))] * len(pairs)
        + [pl.BlockSpec(r.shape, lambda i: (0, 0)) for r in rights],
        out_specs=pl.BlockSpec((tile, total), lambda i: (i, 0)),
        out_shape=jax.ShapeDtypeStruct((width, total), B16),
        cost_estimate=pl.CostEstimate(
            flops=2 * span * width * total, bytes_accessed=16 << 20, transcendentals=0
        ),
        compiler_params=pltpu.CompilerParams(vmem_limit_bytes=VMEM_LIMIT),
    )(*lefts, *rights)


def meet_kernel(index, keep, got, *outs):
    rows = outs[0].shape[0]
    for k, out in enumerate(outs):
        part = pl.ds(pl.multiple_of(index[k] * rows, rows), rows)
        out[...] = (keep[part].astype(F32) + got[part].astype(F32)).astype(B16)


def partial_tokens(width, pairs):
    return met_tokens(*summed_dots(width, *pairs))


def met_tokens(give, keep):
    places = near_places()
    got = swap_cores(give)
    rows, width = keep.shape[0] // len(places), keep.shape[1]
    shapes = [jax.ShapeDtypeStruct((rows, width), B16)] * len(places)
    index = jnp.stack(places).astype(jnp.int32)
    return whole_call(meet_kernel, shapes, [], 2 * keep.size, index, keep, got)


def scatter_tokens(blocks, alongside=None):
    blocks = [to_near(b, k) if k else b for k, b in enumerate(blocks)]
    if alongside is not None:
        blocks, alongside = lax.optimization_barrier((blocks, alongside))
    return added(blocks), alongside


def dot(left, right, dims=((1,), (0,))):
    return lax.dot_general(left, right, (dims, ((), ())), preferred_element_type=F32)


def dot_nt(left, right):
    return dot(left, right, ((1,), (1,)))


def dot_tn(left, right):
    return dot(left, right, ((0,), (0,)))


def dot_exact(left, right, dims=((1,), (0,))):
    return lax.dot_general(
        left, right, (dims, ((), ())), precision=HIGHEST, preferred_element_type=F32
    )


def normalize(values, gain):
    factor = lax.rsqrt(jnp.mean(values * values, -1, keepdims=True) + EPS)
    unit = values * factor
    return unit * gain, unit, factor


def norm_back(grad_out, unit, factor, gain):
    grad_unit = grad_out * gain[None, :]
    grad_in = factor * (grad_unit - unit * jnp.mean(grad_unit * unit, -1, keepdims=True))
    return grad_in, jnp.sum(grad_out * unit, 0)


def rotate_pair(first, second, cosine, sine):
    return first * cosine - second * sine, second * cosine + first * sine


def conv(inputs, edge, weight, bias, dim):
    length = inputs.shape[dim]
    padded = jnp.concatenate([edge, inputs], dim)
    total = bias
    for tap in range(CONV):
        total = total + weight[tap] * lax.slice_in_dim(padded, tap, tap + length, axis=dim)
    return total


def conv_back(grad, grad_edge, inputs, edge, weight, dim):
    length = inputs.shape[dim]
    padded = jnp.concatenate([edge, inputs], dim)
    late = jnp.concatenate([grad, grad_edge], dim)
    total = 0.0
    taps = []
    for tap in range(CONV):
        back = CONV - 1 - tap
        total = total + weight[tap] * lax.slice_in_dim(late, back, back + length, axis=dim)
        taps.append(jnp.sum(grad * lax.slice_in_dim(padded, tap, tap + length, axis=dim), dim))
    return total, jnp.stack(taps), jnp.sum(grad, dim)


def silu_slope(v):
    s = jax.nn.sigmoid(v)
    return s * (1.0 + v * (1.0 - s))


def row_block(i):
    return slice(i * ATTEND_ROWS, (i + 1) * ATTEND_ROWS)


def attend_kernel(index, q, *refs):
    *parts, out, lse, k_t, v_t, total, top, mass = refs
    span = q.shape[0]
    wide = min(ATTEND_KEYS, span)
    keys = HEAD_DIM // len(parts)
    half = keys // 2

    @pl.loop(0, index[0] + 1)
    def _(r):
        for k, part in enumerate(parts):
            at = pl.multiple_of(index[k + 1] * half, half)
            k_t[r, pl.ds(at, half)] = part[r, :half]
            k_t[r, pl.ds(at + HEAD_DIM // 2, half)] = part[r, half:keys]
            at = pl.multiple_of(index[k + 1] * keys, keys)
            v_t[r, pl.ds(at, keys)] = part[r, keys:]

    @pl.loop(index[0] + 1, k_t.shape[0])
    def _(r):
        k_t[r] = jnp.zeros(k_t.shape[1:], B16)
        v_t[r] = jnp.zeros(v_t.shape[1:], B16)

    def meet(i, keys_t, values_t, first):
        scores = dot(q[row_block(i)], keys_t) * HEAD_DIM**-0.5
        if first:
            rows = i * ATTEND_ROWS + lax.broadcasted_iota(jnp.int32, scores.shape, 0)
            cols = lax.broadcasted_iota(jnp.int32, scores.shape, 1)
            scores = jnp.where(cols <= rows, scores, MASKED)
        peak = jnp.max(scores, 1, keepdims=True)
        if not first:
            old = top[row_block(i)]
            peak = jnp.maximum(old, peak)
            fade = jnp.exp(old - peak)
        probs = jnp.exp(scores - peak)
        weight = jnp.sum(probs, 1, keepdims=True)
        read = dot_nt(probs.astype(B16), values_t)
        if not first:
            weight = weight + fade * mass[row_block(i)]
            read = read + fade * total[row_block(i)]
        top[row_block(i)] = peak
        mass[row_block(i)] = weight
        total[row_block(i)] = read

    for i in range(span // ATTEND_ROWS):
        keys = (i + 1) * ATTEND_ROWS
        meet(i, k_t[0, :, :keys], v_t[0, :, :keys], True)

    @pl.loop(1, index[0] + 1)
    def _(r):
        for j in range(span // wide):
            keys_t = k_t[r, :, j * wide : (j + 1) * wide]
            values_t = v_t[r, :, j * wide : (j + 1) * wide]
            for i in range(span // ATTEND_ROWS):
                meet(i, keys_t, values_t, False)

    out[...] = total[...] / mass[...]
    lse[...] = top[...] + jnp.log(mass[...])


def whole_call(kernel, out_shape, scratch, cost, *operands):
    vmem = pl.BlockSpec(memory_space=pltpu.VMEM)
    smem = pl.BlockSpec(memory_space=pltpu.SMEM)
    return pl.pallas_call(
        kernel,
        out_shape=out_shape,
        in_specs=[smem] + [vmem] * (len(operands) - 1),
        out_specs=jax.tree.map(lambda _: vmem, out_shape),
        scratch_shapes=scratch,
        cost_estimate=pl.CostEstimate(flops=cost, bytes_accessed=4 << 20, transcendentals=0),
        compiler_params=pltpu.CompilerParams(vmem_limit_bytes=VMEM_LIMIT),
    )(*operands)


def attend(index, queries, parts):
    span, groups = queries.shape[0], parts[0].shape[0]
    shape = jax.ShapeDtypeStruct
    turned = shape((groups, HEAD_DIM, span), B16)
    column = pltpu.VMEM((span, 1), F32)
    return whole_call(
        attend_kernel,
        (shape((span, HEAD_DIM), F32), shape((span, 1), F32), turned, turned),
        [pltpu.VMEM((span, HEAD_DIM), F32), column, column],
        2 * span * span * groups * HEAD_DIM,
        index,
        queries,
        *parts,
    )


def attend_back_kernel(index, q, q_t, d, d_t, k_t, v_t, lse, delta, grad_q, *refs):
    *outs, sum_k, sum_v = refs
    span = q.shape[0]
    keys = HEAD_DIM // len(outs)
    half = keys // 2
    wide = min(ATTEND_KEYS, span)
    blocks = span // ATTEND_ROWS

    def meet(i, keys_t, values_t, offset, total_q):
        part = row_block(i)
        scores = dot(q[part], keys_t) * HEAD_DIM**-0.5
        if offset is not None:
            rows = i * ATTEND_ROWS + lax.broadcasted_iota(jnp.int32, scores.shape, 0)
            cols = offset + lax.broadcasted_iota(jnp.int32, scores.shape, 1)
            scores = jnp.where(cols <= rows, scores, MASKED)
        probs = jnp.exp(scores - lse[part])
        grad_scores = (probs * (dot(d[part], values_t) - delta[part])).astype(B16)
        update = dot_nt(grad_scores, keys_t)
        grad_q[part] = update if total_q is None else grad_q[part] + update
        return dot(q_t[:, part], grad_scores), dot(d_t[:, part], probs.astype(B16))

    def store(r, cols, pair):
        sum_k[...] = (pair[0] * HEAD_DIM**-0.5).astype(B16)
        sum_v[...] = pair[1].astype(B16)
        for k, out in enumerate(outs):
            at = pl.multiple_of(index[k + 1] * half, half)
            out[r, :half, cols] = sum_k[pl.ds(at, half)]
            out[r, half:keys, cols] = sum_k[pl.ds(at + HEAD_DIM // 2, half)]
            at = pl.multiple_of(index[k + 1] * keys, keys)
            out[r, keys:, cols] = sum_v[pl.ds(at, keys)]

    for j in range(span // wide):
        cols = slice(j * wide, (j + 1) * wide)
        pair = None
        for i in range(j * wide // ATTEND_ROWS, blocks):
            more = meet(i, k_t[0, :, cols], v_t[0, :, cols], j * wide, None if j == 0 else True)
            pair = more if pair is None else (pair[0] + more[0], pair[1] + more[1])
        store(0, cols, pair)

    @pl.loop(1, index[0] + 1)
    def _(r):
        for j in range(span // wide):
            cols = slice(j * wide, (j + 1) * wide)
            pair = None
            for i in range(blocks):
                more = meet(i, k_t[r, :, cols], v_t[r, :, cols], None, True)
                pair = more if pair is None else (pair[0] + more[0], pair[1] + more[1])
            store(r, cols, pair)

    @pl.loop(index[0] + 1, k_t.shape[0])
    def _(r):
        for out in outs:
            out[r] = jnp.zeros(out.shape[1:], B16)


def attend_back(index, queries, keys_t, values_t, grad, lse, delta):
    span, groups = queries.shape[0], keys_t.shape[0]
    near = lax.axis_size("near")
    shape = jax.ShapeDtypeStruct
    part = shape((groups, 2 * HEAD_DIM // near, span), B16)
    wide = pltpu.VMEM((HEAD_DIM, min(ATTEND_KEYS, span)), B16)
    grad_q, *parts = whole_call(
        attend_back_kernel,
        (shape(queries.shape, F32), *[part] * near),
        [wide, wide],
        5 * span * span * groups * HEAD_DIM,
        index,
        queries,
        queries.T,
        grad,
        grad.T,
        keys_t,
        values_t,
        lse,
        delta,
    )
    return grad_q, parts


def spread(per_head, of_head):
    return dot_exact(per_head, of_head, ((0,), (0,)))


def head_decay(cum, cum_t, h):
    length = cum.shape[0]
    rows = lax.broadcasted_iota(jnp.int32, (length, length), 0)
    cols = lax.broadcasted_iota(jnp.int32, (length, length), 1)
    gap = cum[:, h : h + 1] - cum_t[h : h + 1, :]
    return jnp.exp(jnp.where(cols <= rows, gap, MASKED))


def in_head(shape, h, channels):
    lane = lax.broadcasted_iota(jnp.int32, shape, 1)
    return (lane >= h * channels) & (lane < (h + 1) * channels)


def scan_kernel(heads, x, dt, cum, cum_t, b_t, c_t, of_head, y, states, last, state):
    @pl.when(pl.program_id(0) == 0)
    def _():
        state[...] = jnp.zeros_like(state)

    channels = x.shape[1] // heads
    per = HEAD_DIM // channels
    owner = of_head[...]
    cums, cums_t = cum[...], cum_t[...]
    scaled = x[...] * spread(dt[...], owner)
    inner = dot_tn(c_t[...], b_t[...])
    wide = spread(cums_t, owner)
    end = wide[-1:]
    states[0] = state[...]
    carried = dot_exact(c_t[...].astype(F32), state[...], ((0,), (0,))) * jnp.exp(wide)
    for at in range(heads // per):
        lanes = slice(at * HEAD_DIM, (at + 1) * HEAD_DIM)
        block = scaled[:, lanes]
        within = None
        for k in range(per):
            mixing = head_decay(cums, cums_t, at * per + k) * inner
            part = dot_exact(mixing, block)
            mine = in_head(part.shape, k, channels)
            within = part if within is None else jnp.where(mine, part, within)
        y[:, lanes] = within + carried[:, lanes]
    added = dot_exact(b_t[...].astype(F32), scaled * jnp.exp(end - wide))
    state[...] = jnp.exp(end) * state[...] + added
    last[...] = state[...]


def scan_forward(heads, x, dt, cum, cum_t, b_t, c_t, of_head, rows):
    span, inner = x.shape
    chunks = span // rows
    by_row = lambda width: pl.BlockSpec((rows, width), lambda c: (c, 0))
    by_col = lambda height: pl.BlockSpec((height, rows), lambda c: (0, c))
    whole = lambda a: pl.BlockSpec(a.shape, lambda c: (0,) * a.ndim)
    shape = jax.ShapeDtypeStruct
    return pl.pallas_call(
        functools.partial(scan_kernel, heads),
        grid=(chunks,),
        in_specs=[
            by_row(inner),
            by_col(dt.shape[0]),
            by_row(cum.shape[1]),
            by_col(dt.shape[0]),
            by_col(STATE),
            by_col(STATE),
            whole(of_head),
        ],
        out_specs=[
            by_row(inner),
            pl.BlockSpec((1, STATE, inner), lambda c: (c, 0, 0)),
            pl.BlockSpec((STATE, inner), lambda c: (0, 0)),
        ],
        out_shape=[
            shape((span, inner), F32),
            shape((chunks, STATE, inner), F32),
            shape((STATE, inner), F32),
        ],
        scratch_shapes=[pltpu.VMEM((STATE, inner), F32)],
        cost_estimate=pl.CostEstimate(
            flops=60 * span * rows * inner, bytes_accessed=8 << 20, transcendentals=0
        ),
        compiler_params=pltpu.CompilerParams(vmem_limit_bytes=VMEM_LIMIT),
    )(x, dt, cum, cum_t, b_t, c_t, of_head)


def scan_back_kernel(
    heads,
    x,
    dt,
    cum,
    cum_t,
    b_t,
    c_t,
    of_head,
    skip,
    state_in,
    state_out,
    y,
    grad,
    leaving,
    grad_x,
    grad_bt,
    grad_ct,
    grad_logs,
    grad_dt,
    grad_skip,
    grad_state,
):
    @pl.when(pl.program_id(0) == 0)
    def _():
        grad_state[...] = leaving[...]
        grad_skip[...] = jnp.zeros_like(grad_skip)

    channels = x.shape[1] // heads
    per = HEAD_DIM // channels
    owner = of_head[...]
    cums, cums_t = cum[...], cum_t[...]
    times = spread(dt[...], owner)
    values = x[...]
    scaled = values * times
    inner = dot_tn(c_t[...], b_t[...])
    wide = spread(cums_t, owner)
    end = wide[-1:]
    tail = jnp.exp(end - wide)
    back = grad[...]
    faded = back * jnp.exp(wide)
    b32, c32 = b_t[...].astype(F32), c_t[...].astype(F32)
    to_state = grad_state[...]
    grad_inner = jnp.zeros_like(inner)
    within = []
    for at in range(heads // per):
        lanes = slice(at * HEAD_DIM, (at + 1) * HEAD_DIM)
        total = None
        for k in range(per):
            decay = head_decay(cums, cums_t, at * per + k)
            part = dot_exact(decay * inner, back[:, lanes], ((0,), (0,)))
            mine = in_head(part.shape, k, channels)
            total = part if total is None else jnp.where(mine, part, total)
            only = jnp.where(mine, back[:, lanes], 0.0)
            grad_inner += dot_exact(only, scaled[:, lanes], ((1,), (1,))) * decay
        within.append(total)
    grad_scaled = jnp.concatenate(within, 1)
    grad_scaled += tail * dot_exact(b32, to_state, ((0,), (0,)))
    grad_ct[...] = (
        dot_exact(b32, grad_inner, ((1,), (1,))) + dot_exact(state_in[0], faded, ((1,), (1,)))
    ).astype(B16)
    grad_bt[...] = (
        dot_exact(c32, grad_inner) + dot_exact(to_state, scaled * tail, ((1,), (1,)))
    ).astype(B16)
    grad_x[...] = grad_scaled * times + skip[...] * back
    grad_skip[...] += jnp.sum(back * values, 0, keepdims=True)
    at_end = jnp.sum(state_out[0] * to_state, 0, keepdims=True)
    change = back * y[...] - grad_scaled * scaled
    rows = lax.broadcasted_iota(jnp.int32, change.shape, 0)
    change = change + jnp.where(rows == change.shape[0] - 1, at_end, 0.0)
    per_head = dot_exact(owner, change, ((1,), (1,)))
    length = change.shape[0]
    later = lax.broadcasted_iota(jnp.int32, (length, length), 0) >= lax.broadcasted_iota(
        jnp.int32, (length, length), 1
    )
    grad_logs[...] = dot_exact(per_head, later.astype(F32))
    grad_dt[...] = dot_exact(owner, grad_scaled * values, ((1,), (1,)))
    grad_state[...] = jnp.exp(end) * to_state + dot_exact(c32, faded)


def scan_backward(
    heads, x, dt, cum, cum_t, b_t, c_t, of_head, skip, states, y, grad, leaving, rows
):
    span, inner = x.shape
    chunks = span // rows
    last = chunks - 1
    by_row = lambda width: pl.BlockSpec((rows, width), lambda c: (last - c, 0))
    by_col = lambda height: pl.BlockSpec((height, rows), lambda c: (0, last - c))
    whole = lambda a: pl.BlockSpec(a.shape, lambda c: (0,) * a.ndim)
    at_state = lambda more: pl.BlockSpec((1, STATE, inner), lambda c: (last - c + more, 0, 0))
    padded = dt.shape[0]
    shape = jax.ShapeDtypeStruct
    return pl.pallas_call(
        functools.partial(scan_back_kernel, heads),
        grid=(chunks,),
        in_specs=[
            by_row(inner),
            by_col(padded),
            by_row(cum.shape[1]),
            by_col(padded),
            by_col(STATE),
            by_col(STATE),
            whole(of_head),
            whole(skip),
            at_state(0),
            at_state(1),
            by_row(inner),
            by_row(inner),
            whole(leaving),
        ],
        out_specs=[
            by_row(inner),
            by_col(STATE),
            by_col(STATE),
            by_col(padded),
            by_col(padded),
            whole(skip),
        ],
        out_shape=[
            shape((span, inner), F32),
            shape((STATE, span), B16),
            shape((STATE, span), B16),
            shape((padded, span), F32),
            shape((padded, span), F32),
            shape(skip.shape, F32),
        ],
        scratch_shapes=[pltpu.VMEM((STATE, inner), F32)],
        cost_estimate=pl.CostEstimate(
            flops=120 * span * rows * inner, bytes_accessed=16 << 20, transcendentals=0
        ),
        compiler_params=pltpu.CompilerParams(vmem_limit_bytes=VMEM_LIMIT),
    )(x, dt, cum, cum_t, b_t, c_t, of_head, skip, states, states, y, grad, leaving)


def per_device(
    tokens,
    cotangent,
    g1,
    w_q,
    w_k,
    w_v,
    w_o,
    w_z,
    w_x,
    w_bc,
    w_dt,
    conv_bc,
    conv_bc_bias,
    w_out,
    g2,
    w_gate,
    w_up,
    w_down,
    conv_x,
    conv_x_bias,
    dt_bias,
    a_log,
    d_skip,
):
    near, groups = lax.axis_size("near"), lax.axis_size("group")
    here, group, core = (lax.axis_index(a) for a in ("near", "group", "head"))
    rows, width = tokens.shape
    span = near * rows
    piece = w_q.shape[0]

    def columns(w):
        return w.reshape(w.shape[0], near, -1).transpose(1, 0, 2)

    def share(x, dim):
        size = x.shape[dim] // near
        return lax.dynamic_slice_in_dim(x, here * size, size, dim)

    devices = near * groups
    key_cols = HEAD_DIM // near
    half_cols = key_cols // 2
    state_cols = STATE // near
    heads = w_dt.shape[1] // near
    padded = heads + -heads % 8
    k_cols = w_k.reshape(piece, 2, near, half_cols).transpose(2, 0, 1, 3)
    w_bc_mine = lax.dynamic_slice_in_dim(w_bc, core * STATE, STATE, 1)
    pack1 = [columns(w_x), k_cols.reshape(near, piece, key_cols), columns(w_v)]
    pack1 = jnp.concatenate([*pack1, columns(w_bc_mine)], 2)
    extra = jnp.concatenate([g1, g2, conv_bc.reshape(-1), conv_bc_bias])
    n_small, n_dt = extra.shape[0], heads * piece
    extra = jnp.broadcast_to(extra, (near, n_small))
    extra = jnp.concatenate([extra, w_dt.T.reshape(near, n_dt)], 1)
    extra = jnp.pad(extra, ((0, 0), (0, -extra.shape[1] % (8 * pack1.shape[2]))))
    pack1 = jnp.concatenate([pack1, extra.reshape(near, -1, pack1.shape[2])], 1)
    inner, q_cols, ff = w_z.shape[1] // near, w_q.shape[1] // near, w_gate.shape[1] // near
    pack1 = trade_near(pack1)
    full1 = gather_groups(pack1.reshape(-1, pack1.shape[2]))
    token_parts = sent_tokens(after(own_half(tokens), pack1))
    pack2 = [columns(w_z), columns(w_out.T), columns(w_q), columns(w_o.T)]
    sent2 = sent_near(after(jnp.concatenate(pack2, 2), *token_parts[:near]))
    pack3 = jnp.concatenate([columns(w_gate), columns(w_up), columns(w_down.T)], 2)
    sent3 = sent_near(after(pack3, *sent2))
    grad_parts = sent_tokens(after(own_half(cotangent), *sent3))
    pack2 = placed(near_places(), sent2).reshape(near * piece, -1)

    positions = (group * span + jnp.arange(span)).astype(F32)
    half = HEAD_DIM // 2
    freqs = ROPE_BASE ** (-jnp.arange(half, dtype=F32) / half)
    angle = positions[:, None] * freqs[None, :]
    cos_q, sin_q = jnp.cos(angle), jnp.sin(angle)
    cos_k, sin_k = (share(x, 1).T for x in (cos_q, sin_q))
    full1, cos_q, sin_q, cos_k, sin_k, pack2 = lax.optimization_barrier(
        (full1, cos_q, sin_q, cos_k, sin_k, pack2)
    )
    full2 = lax.all_gather(pack2, "group", axis=0, tiled=True)

    full1 = full1.reshape(devices, -1, full1.shape[2])
    extra = full1[:, piece:].reshape(devices, -1)
    full_dt = extra[:, n_small : n_small + n_dt].reshape(devices, heads, piece)
    full_dt = full_dt.transpose(1, 0, 2).reshape(heads, width)
    full_dt = jnp.pad(full_dt, ((0, padded - heads), (0, 0)))
    smalls = extra[:, :n_small].astype(F32)
    gain1 = smalls[:, :piece].reshape(-1)
    gain2 = smalls[:, piece : 2 * piece].reshape(-1)
    taps_bc = smalls[:, 2 * piece : -conv_bc_bias.shape[0]].reshape(devices, CONV, -1)
    taps_bc = taps_bc.transpose(1, 0, 2).reshape(CONV, 2, near, -1)
    taps_bc = taps_bc[:, core, here][:, :, None]
    bias_bc = smalls[:, -conv_bc_bias.shape[0] :].reshape(2, near, -1)[core, here][:, None]
    full1 = full1[:, :piece].reshape(width, -1)
    n1 = placed_tokens(token_parts, gain1)
    full_x, full_kvbc = full1[:, :inner], full1[:, inner:]
    full_z, full_out_t = full2[:, :inner], full2[:, inner : 2 * inner]
    full_q, full_o_t = full2[:, 2 * inner : 2 * inner + q_cols], full2[:, 2 * inner + q_cols :]

    kvbc = dot(full_kvbc, n1, ((0,), (1,)))
    k_first, k_second = rotate_pair(kvbc[:half_cols], kvbc[half_cols:key_cols], cos_k, sin_k)
    kv = jnp.concatenate([k_first, k_second, kvbc[key_cols : 2 * key_cols]], 0).astype(B16)
    kv_parts = [kv] + [step_group(kv, r) for r in range(1, groups)]
    sent3 = lax.optimization_barrier((sent3, n1))[0]
    pack3 = placed(near_places(), sent3).reshape(near * piece, -1)
    n1_x, pack3 = lax.optimization_barrier((n1, pack3, kv))[:2]
    full3 = lax.all_gather(pack3, "group", axis=0, tiled=True)
    full_gu, full_down_t = full3[:, : 2 * ff], full3[:, 2 * ff :]

    bc_proj = kvbc[2 * key_cols :]
    bc_edge = step_group(bc_proj[:, span - CONV + 1 :], 1)
    bc_pre = conv(bc_proj, bc_edge, taps_bc, bias_bc, 1)
    bc_mine = gather_near(jax.nn.silu(bc_pre).astype(B16)).reshape(STATE, span)
    bc_other = swap_cores(bc_mine)
    first = core == 0
    b_t, c_t = jnp.where(first, bc_mine, bc_other), jnp.where(first, bc_other, bc_mine)

    def by_head(x):
        return jnp.pad(share(x, 0).astype(F32), (0, padded - heads))[:, None]

    of_head = jnp.arange(inner)[None, :] // (inner // heads) == jnp.arange(padded)[:, None]
    of_head = of_head.astype(F32)
    dt_pre = dot_nt(full_dt, n1) + by_head(dt_bias)
    dt = jax.nn.softplus(dt_pre)
    decay_rate = jnp.exp(by_head(a_log))
    logs = -dt * decay_rate
    triangle = jnp.triu(jnp.ones((rows, rows), F32))
    cum_t = dot_exact(logs.reshape(padded * near, rows), triangle).reshape(padded, near, rows)
    chunk_total = cum_t[:, :, -1]
    before = jnp.cumsum(chunk_total, 1) - chunk_total
    group_total = jnp.sum(chunk_total, 1, keepdims=True)
    fade = jnp.exp(spread((cum_t + before[:, :, None]).reshape(padded, span), of_head))
    cum_t = cum_t.reshape(padded, span)
    cum = cum_t.T
    group_decay = jnp.exp(spread(group_total, of_head))

    x_proj = dot(n1_x, full_x)
    x_edge = step_group(x_proj[span - CONV + 1 :], 1)
    taps_x = share(conv_x, 1).astype(F32)[:, None, :]
    bias_x = share(conv_x_bias, 0).astype(F32)[None, :]
    skip = spread(by_head(d_skip), of_head)
    x_pre = conv(x_proj, x_edge, taps_x, bias_x, 0)
    xc = jax.nn.silu(x_pre)
    kv_parts = jnp.stack(kv_parts)
    xc = after(xc, kv_parts, *grad_parts)
    kv_parts = [to_near(kv_parts, k) if k else kv_parts for k in range(near)]
    outputs, states, state_out = scan_forward(heads, xc, dt, cum, cum_t, b_t, c_t, of_head, rows)

    def sent_states(state, direction):
        pad = jnp.broadcast_to(group_decay, (16, inner))
        sent = jnp.concatenate([state, pad], 0).astype(B16)
        return [step_group(sent, direction * r) for r in range(1, groups)]

    def chained(parts):
        total = jnp.zeros((STATE, inner), F32)
        for part in reversed(parts):
            part = part.astype(F32)
            total = part[STATE : STATE + 1] * total + part[:STATE]
        return total

    entering = sent_states(state_out, 1)
    q_proj = dot(n1, full_q)
    queries = jnp.concatenate(rotate_pair(q_proj[:, :half], q_proj[:, half:], cos_q, sin_q), 1)
    queries = queries.astype(B16)
    z_proj = dot(n1, full_z)
    index = jnp.stack([group, *near_places()]).astype(jnp.int32)
    attended32, lse, keys_t, values_t = attend(index, queries, kv_parts)
    attended = attended32.astype(B16)
    entering = chained(after(entering, attended, z_proj))

    outputs = outputs + fade * dot_tn(c_t, entering.astype(B16))
    y = outputs + skip * xc
    gated = (y * jax.nn.silu(z_proj)).astype(B16)

    at_q, o_rows = 2 * inner // q_cols, w_o.shape[0] // near
    pairs = [(gated, (full2, 1)), (attended, (full2, at_q + 1))]
    mixed, all_cotangent = scatter_tokens(partial_tokens(width, pairs), placed_tokens(grad_parts))
    my_tokens, my_cotangent = own_half(tokens).astype(F32), own_half(cotangent).astype(F32)
    hidden = my_tokens + mixed
    normed2, unit2, factor2 = normalize(hidden, gain2)
    n2 = gather_tokens(normed2.astype(B16))
    both = dot(n2, full_gu)
    gate, up = both[:, :ff], both[:, ff:]
    sigma = jax.nn.sigmoid(gate)
    act = (gate * sigma * up).astype(B16)
    grad_act = dot(all_cotangent, full_down_t)
    grad_gate = grad_act * up * sigma * (1.0 + gate * (1.0 - sigma))
    grad_gu = jnp.concatenate([grad_gate, grad_act * gate * sigma], 1).astype(B16)

    def sum_groups(grad):
        return lax.psum_scatter(grad, "group", scatter_dimension=0, tiled=True)

    def by_near_rows(own):
        return trade_near(own.reshape(near, piece, -1))

    def joined(parts):
        return parts.transpose(1, 0, 2).reshape(piece, -1).astype(F32)

    def joined_t(parts):
        return parts.transpose(0, 2, 1).reshape(-1, piece).astype(F32)

    partial2 = partial_tokens(width, [(grad_gu, (full3, 0))])
    grads3 = joined_grads((n2, grad_gu), (all_cotangent, act))
    grad_n2, (grads3, feed) = scatter_tokens(
        partial2, alongside=(grads3, summed_dots(width, (act, (full3, 2))))
    )
    home3 = sum_groups(grads3)

    grad_norm2, grad_g2 = norm_back(grad_n2, unit2, factor2, gain2)
    grad_hidden = my_cotangent + grad_norm2
    grad_mixed = gather_tokens(grad_hidden.astype(B16))

    grad_attended = dot(grad_mixed, full_o_t).astype(B16)
    grad_gated = dot(grad_mixed, full_out_t).astype(B16).astype(F32)

    sig_z = jax.nn.sigmoid(z_proj)
    grad_y = grad_gated * z_proj * sig_z
    grad_z = (grad_gated * y * sig_z * (1.0 + z_proj * (1.0 - sig_z))).astype(B16)
    read = sent_states(dot(c_t, (grad_y * fade).astype(B16)), -1)
    feed, _ = scatter_tokens(met_tokens(*after(feed, grad_mixed)))
    output = (hidden + feed).astype(B16)
    output = both_halves(output, swap_cores(output), 0)
    grad_attended = after(grad_attended, output, grad_y, grad_z)

    delta = jnp.sum(grad_attended.astype(F32) * attended32, 1, keepdims=True)
    grad_q, kv_parts = attend_back(
        index, queries, keys_t, values_t, grad_attended, lse, delta
    )
    kv_parts = added([to_near(p, k) if k else p for k, p in enumerate(kv_parts)])
    kv_sent = kv_parts.astype(B16)
    grad_kv = kv_parts[0]
    for r in range(1, groups):
        grad_kv = grad_kv + step_group(kv_sent[r], -r).astype(F32)
    gk_first, gk_second = rotate_pair(
        grad_kv[:half_cols], grad_kv[half_cols:key_cols], cos_k, -sin_k
    )
    grad_q = grad_q * HEAD_DIM**-0.5
    grad_q = jnp.concatenate(rotate_pair(grad_q[:, :half], grad_q[:, half:], cos_q, -sin_q), 1)
    grad_zq = jnp.concatenate([grad_z, grad_q.astype(B16)], 1)
    mixer_out = jnp.concatenate([gated, attended], 1)
    grads2 = joined_grads((grad_mixed, mixer_out), (n1, grad_zq))
    home2 = sum_groups(grads2)

    before_wide = jnp.exp(spread(before, of_head))
    states = jnp.concatenate([states, state_out[None]], 0)
    before_wide = jnp.concatenate([before_wide, group_decay], 0)
    states = states + before_wide[:, None, :] * entering
    grad_y = after(grad_y, kv_sent, grads2)
    leaving = chained(after(read, kv_sent))
    grad_xc, grad_bt, grad_ct, grad_logs, grad_dt, grad_skip = scan_backward(
        heads, xc, dt, cum, cum_t, b_t, c_t, of_head, skip, states, outputs, grad_y, leaving, rows
    )
    kept = jnp.where(first, grad_bt, grad_ct)
    given = swap_cores(jnp.where(first, grad_ct, grad_bt))
    kept = (kept.astype(F32) + given.astype(F32)).astype(B16)
    grad_bc = added(sent_near(kept.reshape(near, -1, span)))
    grad_dt = grad_dt - grad_logs * decay_rate
    grad_dt_pre = grad_dt * jax.nn.sigmoid(dt_pre)
    grad_dt_low = grad_dt_pre.astype(B16)
    grad_skip = dot_exact(of_head, grad_skip, ((1,), (1,)))[:heads, 0]
    grad_alog = jnp.sum(grad_logs * logs, 1)[:heads]
    grad_dtbias = jnp.sum(grad_dt_pre, 1)[:heads]

    grad_xpre = grad_xc * silu_slope(x_pre)
    grad_bcpre = grad_bc * silu_slope(bc_pre)
    next_x = step_group(grad_xpre[: CONV - 1], -1)
    next_bc = step_group(grad_bcpre[:, : CONV - 1], -1)
    grad_x, grad_tapx, grad_biasx = conv_back(grad_xpre, next_x, x_proj, x_edge, taps_x, 0)
    grad_bcp, grad_tapbc, grad_biasbc = conv_back(
        grad_bcpre, next_bc, bc_proj, bc_edge, taps_bc, 1
    )
    grad_kvbc = jnp.concatenate([gk_first, gk_second, grad_kv[key_cols:], grad_bcp], 0)
    grad_first = jnp.concatenate([grad_x.astype(B16), grad_kvbc.astype(B16).T], 1)

    home1 = dot_tn(n1, grad_first).astype(B16).reshape(devices, piece, -1)
    grad_wdt = dot(grad_dt_low, n1).astype(B16).reshape(padded, devices, piece)
    grad_wdt = grad_wdt.transpose(1, 0, 2).reshape(devices, -1)
    grad_wdt = jnp.pad(grad_wdt, ((0, 0), (0, -grad_wdt.shape[1] % home1.shape[2])))
    grad_wdt = grad_wdt.reshape(devices, -1, home1.shape[2])
    home1 = trade_all(jnp.concatenate([home1, grad_wdt], 1))

    home3 = home3.reshape(near, piece, -1)
    pairs = [
        (grad_zq[:, :inner], (full2, 0)),
        (grad_zq[:, inner:], (full2, at_q)),
        (grad_first, (full1, 0)),
        (grad_dt_low.T, full_dt),
    ]
    partial1 = partial_tokens(width, pairs)
    home3 = trade_near(after(home3, *partial1))
    outs3 = joined(home3[:, :, :ff]), joined(home3[:, :, ff : 2 * ff]), joined_t(home3[:, :, 2 * ff :])
    grad_n1, outs3 = scatter_tokens(partial1, alongside=outs3)
    sum_wgate, sum_wup, sum_wdown = outs3
    _, unit1, factor1 = normalize(my_tokens, gain1)
    grad_norm1, grad_g1 = norm_back(grad_n1, unit1, factor1, gain1)
    grad_tokens = grad_hidden + grad_norm1
    grad_tokens = both_halves(grad_tokens, swap_cores(grad_tokens), 0)

    home2 = trade_near(after(home2, grad_n1).reshape(near, piece, -1))
    at_o = inner + o_rows
    sum_wout, sum_wo = joined_t(home2[:, :, :inner]), joined_t(home2[:, :, inner:at_o])
    sum_wz, sum_wq = joined(home2[:, :, at_o : at_o + inner]), joined(home2[:, :, at_o + inner :])
    home1 = after(home1, grad_n1)
    home1 = jnp.sum(home1.reshape(groups, near, *home1.shape[1:]).astype(F32), 0)
    sum_wdt = home1[:, piece:].reshape(near, -1)[:, : heads * piece].reshape(-1, piece).T
    at = [inner, inner + key_cols, inner + 2 * key_cols]
    home_x, home_k, home_v, home_bc = jnp.split(home1[:, :piece], at, 2)
    sum_wx, sum_wv = joined(home_x), joined(home_v)
    sum_wk = home_k.reshape(near, piece, 2, half_cols).transpose(1, 2, 0, 3)
    sum_wk = sum_wk.reshape(piece, -1)
    bc_mine = joined(home_bc)
    sum_wbc = both_halves(bc_mine, swap_cores(bc_mine), 1)

    crossing = jnp.concatenate([grad_g1, grad_g2, grad_tapbc.reshape(-1), grad_biasbc])
    other = swap_cores(crossing)
    gains = 2 * width
    mine = [crossing[:width] + other[:width], crossing[width:gains] + other[width:gains]]
    mine = [*mine, grad_tapx.reshape(-1), grad_biasx, grad_dtbias, grad_alog, grad_skip]
    mine = [*mine, both_halves(crossing[gains:], other[gains:], 0)]
    ends, at = [], 0
    for g in mine[:-1]:
        at += g.shape[0]
        ends.append(at)
    packed = jnp.concatenate(mine)
    size = packed.shape[0]
    packed = jnp.pad(packed, (0, -size % 1024)).reshape(-1, HEAD_DIM)
    packed = trade_all(jnp.broadcast_to(packed, (devices, *packed.shape)))
    packed = packed.reshape(devices, -1)[:, :size]
    every = jnp.split(packed, ends, 1)
    place = group * near + here

    def own(x):
        return lax.dynamic_slice_in_dim(jnp.sum(x, 0), place * piece, piece, 0)

    def by_near(x):
        return jnp.sum(x.reshape(groups, near, -1), 0)

    sum_g1, sum_g2 = own(every[0]), own(every[1])
    sum_convx = by_near(every[2]).reshape(near, CONV, -1).transpose(1, 0, 2).reshape(CONV, -1)
    sum_convxb, sum_dtbias, sum_alog, sum_dskip = (by_near(x).reshape(-1) for x in every[3:7])
    sum_bc = by_near(every[7]).reshape(near, 2, CONV + 1, -1).transpose(2, 1, 0, 3)
    sum_bc = sum_bc.reshape(CONV + 1, -1)
    bc_cols = conv_bc.shape[1]
    sum_bc = lax.dynamic_slice_in_dim(sum_bc, place * bc_cols, bc_cols, 1)
    return (
        output,
        grad_tokens,
        sum_g1,
        sum_wq,
        sum_wk,
        sum_wv,
        sum_wo,
        sum_wz,
        sum_wx,
        sum_wbc,
        sum_wdt,
        sum_bc[:CONV],
        sum_bc[CONV],
        sum_wout,
        sum_g2,
        sum_wgate,
        sum_wup,
        sum_wdown,
        sum_convx,
        sum_convxb,
        sum_dtbias,
        sum_alog,
        sum_dskip,
    )


def solution(mesh):
    seq, cores = mesh.shape["seq"], mesh.shape["head"]
    near = math.gcd(seq, 4)
    split = Mesh(mesh.devices.reshape(seq // near, near, cores), ("group", "near", "head"))
    seq = ("group", "near")
    row_split = P(seq, "head")
    col_split = P("head", seq)
    weights = (
        P(seq),
        row_split,
        row_split,
        row_split,
        col_split,
        row_split,
        row_split,
        P(seq, None),
        row_split,
        P(None, seq),
        P(seq),
        col_split,
        P(seq),
        row_split,
        row_split,
        col_split,
        P(None, "head"),
        P("head"),
        P("head"),
        P("head"),
        P("head"),
    )
    tokens = P(seq, None)
    return jax.shard_map(
        per_device,
        mesh=split,
        in_specs=(tokens, tokens, *weights),
        out_specs=(tokens, tokens, *weights),
        check_vma=False,
    )
```

time: 1080 us -> 790 us (0.73)
  matrix products: 215 us -> 45.2 us
  Pallas kernels: 0 us -> 101 us
  other arithmetic: 141 us -> 83.2 us
  waiting for transfers between devices: 321 us -> 264 us
  local copies, waits for them, and re-layouts: 202 us -> 152 us
  starting transfers between devices: 161 us -> 116 us
  blocking collectives: 18.9 us -> 0 us
  between operations: 4.42 us -> 17.1 us
    dot_general x36 -> x13, matrix products: 160 us -> 41.2 us  [dot(): lax.dot_general(left, right, (dims, ((), ())), preferred_element_type=F32)]
    all_to_all x28 -> x2, starting transfers between devices: 117 us -> 12.8 us  [trade_all(): return lax.all_to_all(x, ('group', 'near'), 0, 0, tiled=True)]
    pallas_call x0 -> x25, Pallas kernels: none -> 101 us  [the longest x17 28 us: whole_call(): pl.pallas_call(kernel, out_shape=out_shape, in_specs=[smem] + [vmem] * (l...]
    all_to_all x28 -> x2, waiting for transfers between devices: 94.6 us -> 5.32 us  [trade_all(): return lax.all_to_all(x, ('group', 'near'), 0, 0, tiled=True)]
    ppermute x4 -> x16, waiting for transfers between devices: 5.13 us -> 70.7 us  [step_group(): return lax.ppermute(x, 'group', route)]
    dot_general x16 -> x6, matrix products: 55 us -> 4 us  [dot_exact(): lax.dot_general(left, right, (dims, ((), ())), precision=HIGHEST, preferr...]
    dynamic_update_slice x38 -> x0, local copies, waits for them, and re-layouts: 45.8 us -> none  [the longest x31 39.2 us: ring_gather(): held = lax.dynamic_update_index_in_dim(held, x, (place - turn) % count, 0)]
    ppermute x54, waiting for transfers between devices: 217 us -> 176 us  [the longest x51 158 us: to_near(): lax.ppermute(x, 'near', [(i, i ^ k) for i in range(lax.axis_size('near'))])]
  transfers between devices with their start and end apart: 102 -> 102, of which waited for: 51 -> 39; matrix products, arithmetic and copies ran while one was open for 36% -> 26% of each run, Pallas kernels for 0% -> 12%
where the time goes in v2:
time: 790 us; the launch traced here: 778 us
  waiting for transfers between devices  264 us (33%)
  local copies, waits for them, and re-layouts  152 us (19%)
  starting transfers between devices  116 us (15%)
  Pallas kernels  101 us (13%)
  other arithmetic  83.2 us (11%)
  matrix products  45.2 us (6%)
  between operations  17.1 us (2%)
    ppermute x51, waiting for transfers between devices, to_near(): lax.ppermute(x, 'near', [(i, i ^ k) for i in range(lax.axis_size('near'))])  158 us
    unnamed x411, local copies, waits for them, and re-layouts  72.1 us
    ppermute x16, waiting for transfers between devices, step_group(): return lax.ppermute(x, 'group', route)  70.7 us
    ppermute x51, starting transfers between devices, to_near(): lax.ppermute(x, 'near', [(i, i ^ k) for i in range(lax.axis_size('near'))])  64.6 us
    dot_general x13, matrix products, dot(): lax.dot_general(left, right, (dims, ((), ())), preferred_element_type=F32)  41.2 us
    ppermute x16, starting transfers between devices, step_group(): return lax.ppermute(x, 'group', route)  28 us
    pallas_call x17, Pallas kernels, whole_call(): pl.pallas_call(kernel, out_shape=out_shape, in_specs=[smem] + [vmem] * (l...  28 us
    pallas_call x1, Pallas kernels, scan_backward(): pl.pallas_call(functools.partial(scan_back_kernel, heads), grid=(chunks,)...  27.8 us
  transfers between devices with their start and end apart: 102, of which 39 were waited for; matrix products, arithmetic and copies ran while one was open for 26% of the time, Pallas kernels for 12%

profile of v2, /device:TPU:0, one launch (start us, length us, event | category | flops | bytes accessed | tf_op | source)
XLA Modules:
  0.0 778.4 jit_solution(1163324433850077305)
XLA Ops:
  33.3 8.1 %collective-permute-done.5.refs_3_ = bf16[128,2048]{1,0:T(8,128)(2,1)} collective-permute-done((bf16[128,2048]{1,0:T(8,128)(2,1)S(1)}, bf16[128,2048]{1,0:T(8,128)(2,1)}, u32[]{:S(2)}, u32[]{:S(2)}) %collective-permute-start.5) | collective-permute-done | bytes 524320 | tf_op jit(solution)/shard_map/ppermute | solution.py:34
  42.9 8.4 %collective-permute-done.4.refs_2_ = bf16[128,2048]{1,0:T(8,128)(2,1)} collective-permute-done((bf16[128,2048]{1,0:T(8,128)(2,1)S(1)}, bf16[128,2048]{1,0:T(8,128)(2,1)}, u32[]{:S(2)}, u32[]{:S(2)}) %collective-permute-start.4) | collective-permute-done | bytes 524320 | tf_op jit(solution)/shard_map/ppermute | solution.py:34
  61.6 17.8 %collective-permute-done.11.refs_2_ = bf16[544,512]{1,0:T(8,128)(2,1)S(1)} collective-permute-done((bf16[544,512]{1,0:T(8,128)(2,1)S(1)}, bf16[544,512]{1,0:T(8,128)(2,1)S(1)}, u32[]{:S(2)}, u32[]{:S(2)}) %collective-permute-start.11) | collective-permute-done | bytes 557088 | tf_op jit(solution)/shard_map/ppermute | solution.py:39
  177.9 6.8 collective-permute-done.24.refs_2_
  194.4 12.3 %shard_map.404 = (f32[1024,384]{1,0:T(8,128)S(1)}, f32[4,256,384]{2,1,0:T(8,128)S(1)}, f32[256,384]{1,0:T(8,128)S(1)}) custom-call(f32[1024,384]{1,0:T(8,128)S(1)} %get-tuple-element.126.x, f32[8,1024]{1,0:T(8,128)S(1)} %get-tuple-element.406.dt, f32[1024,8]{1,0:T(8,128)S(1)} %copy-done.65, f32[8,1024]{1,0:T(8,128)S(1)} %reshape_reshape.3.cum_t, ...), custom_call_target="tpu_custom_call" | custom-call | flops 6039797760 | bytes 8388608 | tf_op jit(solution)/shard_map/pallas_call | solution.py:526
  214.9 5.1 fusion.21
  231.0 8.5 %collective-permute-done.35 = bf16[272,384]{1,0:T(8,128)(2,1)S(1)} collective-permute-done((bf16[272,384]{1,0:T(8,128)(2,1)}, bf16[272,384]{1,0:T(8,128)(2,1)S(1)}, u32[]{:S(2)}, u32[]{:S(2)}) %collective-permute-start.35) | collective-permute-done | bytes 208928 | tf_op jit(solution)/shard_map/ppermute | solution.py:45
  261.3 7.6 collective-permute-done.42
  268.9 11.6 %collective-permute-done.43 = bf16[128,2048]{1,0:T(8,128)(2,1)S(1)} collective-permute-done((bf16[128,2048]{1,0:T(8,128)(2,1)S(1)}, bf16[128,2048]{1,0:T(8,128)(2,1)S(1)}, u32[]{:S(2)}, u32[]{:S(2)}) %collective-permute-start.43) | collective-permute-done | bytes 524320 | tf_op jit(solution)/shard_map/ppermute | solution.py:34
  284.9 12.3 %collective-permute-done.47.refs_3_ = bf16[128,2048]{1,0:T(8,128)(2,1)S(1)} collective-permute-done((bf16[128,2048]{1,0:T(8,128)(2,1)S(1)}, bf16[128,2048]{1,0:T(8,128)(2,1)S(1)}, u32[]{:S(2)}, u32[]{:S(2)}) %collective-permute-start.47) | collective-permute-done | bytes 524320 | tf_op jit(solution)/shard_map/ppermute | solution.py:34
  297.2 9.3 %collective-permute-done.46.refs_2_ = bf16[128,2048]{1,0:T(8,128)(2,1)S(1)} collective-permute-done((bf16[128,2048]{1,0:T(8,128)(2,1)S(1)}, bf16[128,2048]{1,0:T(8,128)(2,1)S(1)}, u32[]{:S(2)}, u32[]{:S(2)}) %collective-permute-start.46) | collective-permute-done | bytes 524320 | tf_op jit(solution)/shard_map/ppermute | solution.py:34
  312.1 7.8 %fusion = f32[1024,1024]{1,0:T(8,128)S(1)} fusion(bf16[1024,2048]{1,0:T(8,128)(2,1)} %bitcast.328, bf16[2048,1536]{1,0:T(8,128)(2,1)} %all-gather.5.cloned.1.call-done.refs_1_), kind=kOutput, calls=%fused_computation.1 | convolution fusion | flops 4294967296 | bytes 12582912 | tf_op jit(solution)/shard_map/dot_general | solution.py:241
  319.9 5.9 multiply_convert_fusion.2
  348.9 9.2 %shard_map.412 = bf16[2048,1536]{1,0:T(8,128)(2,1)} custom-call(bf16[1024,2048]{1,0:T(8,128)(2,1)S(1)} %bitcast.329, bf16[1024,2048]{1,0:T(8,128)(2,1)S(1)} %bitcast.327, bf16[1024,1024]{1,0:T(8,128)(2,1)S(1)} %copy-done.27, bf16[1024,512]{1,0:T(8,128)(2,1)S(1)} %copy-done.81), custom_call_target="tpu_custom_call" | custom-call | flops 6442450944 | bytes 16777216 | tf_op jit(solution)/shard_map/pallas_call | solution.py:199
  358.9 10.7 %collective-permute-done.54 = bf16[128,2048]{1,0:T(8,128)(2,1)} collective-permute-done((bf16[128,2048]{1,0:T(8,128)(2,1)}, bf16[128,2048]{1,0:T(8,128)(2,1)}, u32[]{:S(2)}, u32[]{:S(2)}) %collective-permute-start.54) | collective-permute-done | bytes 524320 | tf_op jit(solution)/shard_map/ppermute | solution.py:34
  379.7 12.3 %collective-permute-done.58.refs_3_ = bf16[128,2048]{1,0:T(8,128)(2,1)S(1)} collective-permute-done((bf16[128,2048]{1,0:T(8,128)(2,1)S(1)}, bf16[128,2048]{1,0:T(8,128)(2,1)S(1)}, u32[]{:S(2)}, u32[]{:S(2)}) %collective-permute-start.58) | collective-permute-done | bytes 524320 | tf_op jit(solution)/shard_map/ppermute | solution.py:34
  392.0 9.5 %collective-permute-done.57.refs_2_ = bf16[128,2048]{1,0:T(8,128)(2,1)S(1)} collective-permute-done((bf16[128,2048]{1,0:T(8,128)(2,1)S(1)}, bf16[128,2048]{1,0:T(8,128)(2,1)S(1)}, u32[]{:S(2)}, u32[]{:S(2)}) %collective-permute-start.57) | collective-permute-done | bytes 524320 | tf_op jit(solution)/shard_map/ppermute | solution.py:34
  425.1 5.6 fusion.7
  430.7 5.6 collective-permute-done.64
  436.3 11.8 %collective-permute-done.65 = bf16[128,2048]{1,0:T(8,128)(2,1)S(1)} collective-permute-done((bf16[128,2048]{1,0:T(8,128)(2,1)S(1)}, bf16[128,2048]{1,0:T(8,128)(2,1)S(1)}, u32[]{:S(2)}, u32[]{:S(2)}) %collective-permute-start.65) | collective-permute-done | bytes 524320 | tf_op jit(solution)/shard_map/ppermute | solution.py:34
  481.4 6.6 shard_map.417
  504.0 9.8 %collective-permute-done.71 = bf16[272,384]{1,0:T(8,128)(2,1)S(1)} collective-permute-done((bf16[272,384]{1,0:T(8,128)(2,1)}, bf16[272,384]{1,0:T(8,128)(2,1)S(1)}, u32[]{:S(2)}, u32[]{:S(2)}) %collective-permute-start.71) | collective-permute-done | bytes 208928 | tf_op jit(solution)/shard_map/ppermute | solution.py:45
  516.0 27.8 %shard_map.418 = (f32[1024,384]{1,0:T(8,128)S(1)}, bf16[256,1024]{1,0:T(8,128)(2,1)S(1)}, bf16[256,1024]{1,0:T(8,128)(2,1)S(1)}, f32[8,1024]{1,0:T(8,128)S(1)}, ...) custom-call(f32[1024,384]{1,0:T(8,128)S(1)} %get-tuple-element.126.x, f32[8,1024]{1,0:T(8,128)S(1)} %copy-done.75, ...), custom_call_target="tpu_custom_call" | custom-call | flops 12079595520 | bytes 16777216 | tf_op jit(solution)/shard_map/pallas_call | solution.py:648
  571.0 10.9 %collective-permute-done.75 = bf16[64,1024]{0,1:T(8,128)(2,1)S(1)} collective-permute-done((bf16[64,1024]{0,1:T(8,128)(2,1)}, bf16[64,1024]{0,1:T(8,128)(2,1)S(1)}, u32[]{:S(2)}, u32[]{:S(2)}) %collective-permute-start.75) | collective-permute-done | bytes 131104 | tf_op jit(solution)/shard_map/ppermute | solution.py:45
  582.9 10.7 %collective-permute-done.77 = bf16[64,1024]{0,1:T(8,128)(2,1)} collective-permute-done((bf16[64,1024]{0,1:T(8,128)(2,1)}, bf16[64,1024]{0,1:T(8,128)(2,1)}, u32[]{:S(2)}, u32[]{:S(2)}) %collective-permute-start.77) | collective-permute-done | bytes 131104 | tf_op jit(solution)/shard_map/ppermute | solution.py:45
  593.6 18.5 %collective-permute-done.76 = bf16[64,1024]{0,1:T(8,128)(2,1)} collective-permute-done((bf16[64,1024]{0,1:T(8,128)(2,1)}, bf16[64,1024]{0,1:T(8,128)(2,1)}, u32[]{:S(2)}, u32[]{:S(2)}) %collective-permute-start.76) | collective-permute-done | bytes 131104 | tf_op jit(solution)/shard_map/ppermute | solution.py:45
  634.5 6.8 shard_map.419
  656.9 18.2 %collective-permute-done.89.refs_3_ = bf16[128,1536]{1,0:T(8,128)(2,1)S(1)} collective-permute-done((bf16[128,1536]{1,0:T(8,128)(2,1)}, bf16[128,1536]{1,0:T(8,128)(2,1)S(1)}, u32[]{:S(2)}, u32[]{:S(2)}) %collective-permute-start.89) | collective-permute-done | bytes 393248 | tf_op jit(solution)/shard_map/ppermute | solution.py:34
  679.9 5.8 collective-permute-done.87.refs_1_
  697.0 11.3 %collective-permute-done.86 = bf16[128,2048]{1,0:T(8,128)(2,1)} collective-permute-done((bf16[128,2048]{1,0:T(8,128)(2,1)S(1)}, bf16[128,2048]{1,0:T(8,128)(2,1)}, u32[]{:S(2)}, u32[]{:S(2)}) %collective-permute-start.86) | collective-permute-done | bytes 524320 | tf_op jit(solution)/shard_map/ppermute | solution.py:34
  739.2 7.9 %all-to-all-start = ((f32[16,56,128]{2,1,0:T(8,128)}), f32[16,56,128]{2,1,0:T(8,128)}, u32[]{:S(2)}, u32[]{:S(2)}) async-start(f32[16,56,128]{2,1,0:T(8,128)} %broadcast_in_dim.22), calls=%async_computation.1 | async-start | bytes 917504 | tf_op jit(solution)/shard_map/all_to_all | solution.py:92
  756.2 5.3 all-to-all-done
  (864 shorter events, 435.4 us)
Async XLA Ops:
  7.2 207.6 %all-gather.3.cloned.1.call-start = ((), (), s32[]{:S(2)}) async-start(), calls=%async_computation.4 | async-start | bytes 5242880 | tf_op jit(solution)/shard_map/all_gather | solution.py:764
  33.2 46.2 %collective-permute-start.11 = (bf16[544,512]{1,0:T(8,128)(2,1)S(1)}, bf16[544,512]{1,0:T(8,128)(2,1)S(1)}, u32[]{:S(2)}, u32[]{:S(2)}) collective-permute-start(bf16[544,512]{1,0:T(8,128)(2,1)S(1)} %bitcast.336), channel_id=1, source_target_pairs={{0,16},{8,24},{16,0},{24,8},{1,17},{9,25},{17,1},{25,9},{2,18},{10... | collective-permute-start | bytes 1671176 | tf_op jit(solution)/shard_map/ppermute | solution.py:39
  41.4 38.9 %collective-permute-start.10 = (bf16[544,512]{1,0:T(8,128)(2,1)S(1)}, bf16[544,512]{1,0:T(8,128)(2,1)S(1)}, u32[]{:S(2)}, u32[]{:S(2)}) collective-permute-start(bf16[544,512]{1,0:T(8,128)(2,1)S(1)} %bitcast.337), channel_id=1, source_target_pairs={{0,8},{8,16},{16,24},{24,0},{1,9},{9,17},{17,25},{25,1},{2,10},{10... | collective-permute-start | bytes 1671176 | tf_op jit(solution)/shard_map/ppermute | solution.py:39
  52.6 32.3 %collective-permute-start.15 = (bf16[128,1024]{1,0:T(8,128)(2,1)}, bf16[128,1024]{1,0:T(8,128)(2,1)}, u32[]{:S(2)}, u32[]{:S(2)}) collective-permute-start(bf16[128,1024]{1,0:T(8,128)(2,1)} %get-tuple-element.379), channel_id=1, source_target_pairs={{0,6},{2,4},{4,2},{6,0},{1,7},{3,5},{5,3},{7,1},{8,14},{10,12},{12... | collective-permute-start | bytes 786440 | tf_op jit(solution)/shard_map/ppermute | solution.py:34
  54.0 30.9 %collective-permute-start.14 = (bf16[128,1024]{1,0:T(8,128)(2,1)}, bf16[128,1024]{1,0:T(8,128)(2,1)}, u32[]{:S(2)}, u32[]{:S(2)}) collective-permute-start(bf16[128,1024]{1,0:T(8,128)(2,1)} %get-tuple-element.380), channel_id=1, source_target_pairs={{0,4},{2,6},{4,0},{6,2},{1,5},{3,7},{5,1},{7,3},{8,12},{10,14},{12... | collective-permute-start | bytes 786440 | tf_op jit(solution)/shard_map/ppermute | solution.py:34
  55.5 29.5 %collective-permute-start.13 = (bf16[128,1024]{1,0:T(8,128)(2,1)}, bf16[128,1024]{1,0:T(8,128)(2,1)}, u32[]{:S(2)}, u32[]{:S(2)}) collective-permute-start(bf16[128,1024]{1,0:T(8,128)(2,1)} %get-tuple-element.381), channel_id=1, source_target_pairs={{0,2},{2,0},{4,6},{6,4},{1,3},{3,1},{5,7},{7,5},{8,10},{10,8},{12,... | collective-permute-start | bytes 786440 | tf_op jit(solution)/shard_map/ppermute | solution.py:34
  87.3 224.8 %all-gather.5.cloned.1.call-start = ((), (), s32[]{:S(2)}) async-start(), calls=%async_computation.5 | async-start | bytes 7864320 | tf_op jit(solution)/shard_map/all_gather | solution.py:791
  103.9 43.1 %collective-permute-start.18 = (bf16[128,1536]{1,0:T(8,128)(2,1)}, bf16[128,1536]{1,0:T(8,128)(2,1)}, u32[]{:S(2)}, u32[]{:S(2)}) collective-permute-start(bf16[128,1536]{1,0:T(8,128)(2,1)} %get-tuple-element.358), channel_id=1, source_target_pairs={{0,6},{2,4},{4,2},{6,0},{1,7},{3,5},{5,3},{7,1},{8,14},{10,12},{12... | collective-permute-start | bytes 1179656 | tf_op jit(solution)/shard_map/ppermute | solution.py:34
  106.3 42.6 %collective-permute-start.17 = (bf16[128,1536]{1,0:T(8,128)(2,1)}, bf16[128,1536]{1,0:T(8,128)(2,1)}, u32[]{:S(2)}, u32[]{:S(2)}) collective-permute-start(bf16[128,1536]{1,0:T(8,128)(2,1)} %get-tuple-element.359), channel_id=1, source_target_pairs={{0,4},{2,6},{4,0},{6,2},{1,5},{3,7},{5,1},{7,3},{8,12},{10,14},{12... | collective-permute-start | bytes 1179656 | tf_op jit(solution)/shard_map/ppermute | solution.py:34
  108.0 43.1 %collective-permute-start.16 = (bf16[128,1536]{1,0:T(8,128)(2,1)}, bf16[128,1536]{1,0:T(8,128)(2,1)}, u32[]{:S(2)}, u32[]{:S(2)}) collective-permute-start(bf16[128,1536]{1,0:T(8,128)(2,1)} %get-tuple-element.360), channel_id=1, source_target_pairs={{0,2},{2,0},{4,6},{6,4},{1,3},{3,1},{5,7},{7,5},{8,10},{10,8},{12,... | collective-permute-start | bytes 1179656 | tf_op jit(solution)/shard_map/ppermute | solution.py:34
  158.3 488.3 %reduce-scatter.3.cloned.1.call-start = ((), (), s32[]{:S(2)}) async-start(), calls=%async_computation.6 | async-start | bytes 7864320 | tf_op jit(solution)/shard_map/reduce_scatter | solution.py:875
  187.4 34.7 %collective-permute-start.40 = (bf16[4,64,1024]{2,1,0:T(8,128)(2,1)}, bf16[4,64,1024]{2,1,0:T(8,128)(2,1)}, u32[]{:S(2)}, u32[]{:S(2)}) collective-permute-start(bf16[4,64,1024]{2,1,0:T(8,128)(2,1)} %pad_maximum_fusion.15.refs_0_), channel_id=1, source_target_pairs={{0,6},{2,4},{4,2},{6,0},{1,7},{3,5},{5,3},{7,1},{8,14},{10,12},{12... | collective-permute-start | bytes 1572872 | tf_op jit(solution)/shard_map/ppermute | solution.py:34
  189.7 33.9 %collective-permute-start.39 = (bf16[4,64,1024]{2,1,0:T(8,128)(2,1)}, bf16[4,64,1024]{2,1,0:T(8,128)(2,1)S(1)}, u32[]{:S(2)}, u32[]{:S(2)}) collective-permute-start(bf16[4,64,1024]{2,1,0:T(8,128)(2,1)} %pad_maximum_fusion.15.refs_0_), channel_id=1, source_target_pairs={{0,4},{2,6},{4,0},{6,2},{1,5},{3,7},{5,1},{7,3},{8,12},{10,14},{12... | collective-permute-start | bytes 1572872 | tf_op jit(solution)/shard_map/ppermute | solution.py:34
  192.2 31.5 %collective-permute-start.38 = (bf16[4,64,1024]{2,1,0:T(8,128)(2,1)}, bf16[4,64,1024]{2,1,0:T(8,128)(2,1)}, u32[]{:S(2)}, u32[]{:S(2)}) collective-permute-start(bf16[4,64,1024]{2,1,0:T(8,128)(2,1)} %pad_maximum_fusion.15.refs_0_), channel_id=1, source_target_pairs={{0,2},{2,0},{4,6},{6,4},{1,3},{3,1},{5,7},{7,5},{8,10},{10,8},{12,... | collective-permute-start | bytes 1572872 | tf_op jit(solution)/shard_map/ppermute | solution.py:34
  369.6 345.4 %reduce-scatter.5.cloned.1.call-start = ((), (), s32[]{:S(2)}) async-start(), calls=%async_computation.7 | async-start | bytes 5242880 | tf_op jit(solution)/shard_map/reduce_scatter | solution.py:875
  450.7 53.3 %collective-permute-start.73 = (bf16[272,384]{1,0:T(8,128)(2,1)}, bf16[272,384]{1,0:T(8,128)(2,1)}, u32[]{:S(2)}, u32[]{:S(2)}) collective-permute-start(bf16[272,384]{1,0:T(8,128)(2,1)} %pad_maximum_fusion.16), channel_id=1, source_target_pairs={{24,0},{25,1},{26,2},{27,3},{28,4},{29,5},{30,6},{31,7}} | collective-permute-start | bytes 626696 | tf_op jit(solution)/shard_map/ppermute | solution.py:45
  452.0 52.0 %collective-permute-start.72 = (bf16[272,384]{1,0:T(8,128)(2,1)}, bf16[272,384]{1,0:T(8,128)(2,1)}, u32[]{:S(2)}, u32[]{:S(2)}) collective-permute-start(bf16[272,384]{1,0:T(8,128)(2,1)} %pad_maximum_fusion.16), channel_id=1, source_target_pairs={{16,0},{24,8},{17,1},{25,9},{18,2},{26,10},{19,3},{27,11},{20,4},{... | collective-permute-start | bytes 626696 | tf_op jit(solution)/shard_map/ppermute | solution.py:45
  551.1 30.8 %collective-permute-start.75 = (bf16[64,1024]{0,1:T(8,128)(2,1)}, bf16[64,1024]{0,1:T(8,128)(2,1)S(1)}, u32[]{:S(2)}, u32[]{:S(2)}) collective-permute-start(bf16[64,1024]{0,1:T(8,128)(2,1)} %get-tuple-element.372), channel_id=1, source_target_pairs={{8,0},{16,8},{24,16},{9,1},{17,9},{25,17},{10,2},{18,10},{26,18},{... | collective-permute-start | bytes 393224 | tf_op jit(solution)/shard_map/ppermute | solution.py:45
  552.4 41.2 %collective-permute-start.77 = (bf16[64,1024]{0,1:T(8,128)(2,1)}, bf16[64,1024]{0,1:T(8,128)(2,1)}, u32[]{:S(2)}, u32[]{:S(2)}) collective-permute-start(bf16[64,1024]{0,1:T(8,128)(2,1)} %get-tuple-element.373), channel_id=1, source_target_pairs={{24,0},{25,1},{26,2},{27,3},{28,4},{29,5},{30,6},{31,7}} | collective-permute-start | bytes 393224 | tf_op jit(solution)/shard_map/ppermute | solution.py:45
  553.7 58.4 %collective-permute-start.76 = (bf16[64,1024]{0,1:T(8,128)(2,1)}, bf16[64,1024]{0,1:T(8,128)(2,1)}, u32[]{:S(2)}, u32[]{:S(2)}) collective-permute-start(bf16[64,1024]{0,1:T(8,128)(2,1)} %get-tuple-element.374), channel_id=1, source_target_pairs={{16,0},{24,8},{17,1},{25,9},{18,2},{26,10},{19,3},{27,11},{20,4},{... | collective-permute-start | bytes 393224 | tf_op jit(solution)/shard_map/ppermute | solution.py:45
  568.3 45.3 %collective-permute-start.79 = (bf16[64,1024]{0,1:T(8,128)(2,1)}, bf16[64,1024]{0,1:T(8,128)(2,1)}, u32[]{:S(2)}, u32[]{:S(2)}) collective-permute-start(bf16[64,1024]{0,1:T(8,128)(2,1)} %bitcast.98), channel_id=1, source_target_pairs={{0,2},{2,0},{4,6},{6,4},{1,3},{3,1},{5,7},{7,5},{8,10},{10,8},{12,... | collective-permute-start | bytes 393224 | tf_op jit(solution)/shard_map/ppermute | solution.py:34
  569.7 43.9 %collective-permute-start.80 = (bf16[64,1024]{0,1:T(8,128)(2,1)}, bf16[64,1024]{0,1:T(8,128)(2,1)}, u32[]{:S(2)}, u32[]{:S(2)}) collective-permute-start(bf16[64,1024]{0,1:T(8,128)(2,1)} %bitcast.99), channel_id=1, source_target_pairs={{0,4},{2,6},{4,0},{6,2},{1,5},{3,7},{5,1},{7,3},{8,12},{10,14},{12... | collective-permute-start | bytes 393224 | tf_op jit(solution)/shard_map/ppermute | solution.py:34
  581.9 31.7 %collective-permute-start.81 = (bf16[64,1024]{0,1:T(8,128)(2,1)}, bf16[64,1024]{0,1:T(8,128)(2,1)}, u32[]{:S(2)}, u32[]{:S(2)}) collective-permute-start(bf16[64,1024]{0,1:T(8,128)(2,1)} %bitcast.100), channel_id=1, source_target_pairs={{0,6},{2,4},{4,2},{6,0},{1,7},{3,5},{5,3},{7,1},{8,14},{10,12},{12... | collective-permute-start | bytes 393224 | tf_op jit(solution)/shard_map/ppermute | solution.py:34
  625.9 85.2 %all-to-all-start.1 = ((bf16[16,130,512]{2,1,0:T(8,128)(2,1)}), bf16[16,130,512]{2,1,0:T(8,128)(2,1)}, u32[]{:S(2)}, u32[]{:S(2)}) async-start(bf16[16,130,512]{2,1,0:T(8,128)(2,1)} %pad_maximum_fusion), calls=%async_computation.3 | async-start | bytes 4456448 | tf_op jit(solution)/shard_map/all_to_all | solution.py:92
  652.7 33.0 %collective-permute-start.87 = (bf16[128,1536]{1,0:T(8,128)(2,1)}, bf16[128,1536]{1,0:T(8,128)(2,1)S(1)}, u32[]{:S(2)}, u32[]{:S(2)}) collective-permute-start(bf16[128,1536]{1,0:T(8,128)(2,1)} %get-tuple-element.350), channel_id=1, source_target_pairs={{0,2},{2,0},{4,6},{6,4},{1,3},{3,1},{5,7},{7,5},{8,10},{10,8},{12,... | collective-permute-start | bytes 1179656 | tf_op jit(solution)/shard_map/ppermute | solution.py:34
  653.5 43.5 %collective-permute-start.84 = (bf16[128,2048]{1,0:T(8,128)(2,1)}, bf16[128,2048]{1,0:T(8,128)(2,1)}, u32[]{:S(2)}, u32[]{:S(2)}) collective-permute-start(bf16[128,2048]{1,0:T(8,128)(2,1)} %copy-done.80), channel_id=1, source_target_pairs={{0,2},{2,0},{4,6},{6,4},{1,3},{3,1},{5,7},{7,5},{8,10},{10,8},{12,... | collective-permute-start | bytes 1572872 | tf_op jit(solution)/shard_map/ppermute | solution.py:34
  655.4 41.6 %collective-permute-start.85 = (bf16[128,2048]{1,0:T(8,128)(2,1)}, bf16[128,2048]{1,0:T(8,128)(2,1)}, u32[]{:S(2)}, u32[]{:S(2)}) collective-permute-start(bf16[128,2048]{1,0:T(8,128)(2,1)} %copy-done.79), channel_id=1, source_target_pairs={{0,4},{2,6},{4,0},{6,2},{1,5},{3,7},{5,1},{7,3},{8,12},{10,14},{12... | collective-permute-start | bytes 1572872 | tf_op jit(solution)/shard_map/ppermute | solution.py:34
  675.1 33.2 %collective-permute-start.86 = (bf16[128,2048]{1,0:T(8,128)(2,1)S(1)}, bf16[128,2048]{1,0:T(8,128)(2,1)}, u32[]{:S(2)}, u32[]{:S(2)}) collective-permute-start(bf16[128,2048]{1,0:T(8,128)(2,1)S(1)} %get-tuple-element.192), channel_id=1, source_target_pairs={{0,6},{2,4},{4,2},{6,0},{1,7},{3,5},{5,3},{7,1},{8,14},{10,12},{12... | collective-permute-start | bytes 1572872 | tf_op jit(solution)/shard_map/ppermute | solution.py:34
  719.3 27.9 %collective-permute-start.95 = (f32[128,256]{0,1:T(8,128)}, f32[128,256]{0,1:T(8,128)}, u32[]{:S(2)}, u32[]{:S(2)}) collective-permute-start(f32[128,256]{0,1:T(8,128)} %bitcast.146), channel_id=1, source_target_pairs={{0,1},{1,0},{2,3},{3,2},{4,5},{5,4},{6,7},{7,6},{8,9},{9,8},{10,11... | collective-permute-start | bytes 393224 | tf_op jit(solution)/shard_map/ppermute | solution.py:30
  719.8 29.3 %collective-permute-start.94 = (bf16[128,1024]{1,0:T(8,128)(2,1)}, bf16[128,1024]{1,0:T(8,128)(2,1)S(1)}, u32[]{:S(2)}, u32[]{:S(2)}) collective-permute-start(bf16[128,1024]{1,0:T(8,128)(2,1)} %get-tuple-element.368), channel_id=1, source_target_pairs={{0,6},{2,4},{4,2},{6,0},{1,7},{3,5},{5,3},{7,1},{8,14},{10,12},{12... | collective-permute-start | bytes 786440 | tf_op jit(solution)/shard_map/ppermute | solution.py:34
  721.2 27.8 %collective-permute-start.92 = (bf16[128,1024]{1,0:T(8,128)(2,1)}, bf16[128,1024]{1,0:T(8,128)(2,1)S(1)}, u32[]{:S(2)}, u32[]{:S(2)}) collective-permute-start(bf16[128,1024]{1,0:T(8,128)(2,1)} %get-tuple-element.370), channel_id=1, source_target_pairs={{0,2},{2,0},{4,6},{6,4},{1,3},{3,1},{5,7},{7,5},{8,10},{10,8},{12,... | collective-permute-start | bytes 786440 | tf_op jit(solution)/shard_map/ppermute | solution.py:34
  736.9 31.7 %collective-permute-start.90 = (f32[128,2048]{1,0:T(8,128)S(1)}, f32[128,2048]{1,0:T(8,128)}, u32[]{:S(2)}, u32[]{:S(2)}) collective-permute-start(f32[128,2048]{1,0:T(8,128)S(1)} %fusion.36), channel_id=1, source_target_pairs={{0,1},{1,0},{2,3},{3,2},{4,5},{5,4},{6,7},{7,6},{8,9},{9,8},{10,11... | collective-permute-start | bytes 3145736 | tf_op jit(solution)/shard_map/ppermute | solution.py:30
  (264 other events, 3032.1 us)
Sparse Core Ops, SparseCore 0:
  87.4 84.6 all-gather.2
  173.7 129.6 all-gather.4
  369.8 131.7 reduce-scatter.2
  503.7 102.6 reduce-scatter.4

commit v3 on v2

v3 whole, which is shorter than its diff:
```python
import functools
import math

import jax
import jax.numpy as jnp
from jax import lax
from jax.experimental import pallas as pl
from jax.experimental.layout import Layout, with_layout_constraint
from jax.experimental.pallas import tpu as pltpu
from jax.sharding import Mesh, PartitionSpec as P

HEAD_DIM = 128
STATE = 256
CONV = 4
EPS = 1e-05
ROPE_BASE = 100000000000.0
MASKED = -1e30
HIGHEST = lax.Precision.HIGHEST
F32 = jnp.float32
B16 = jnp.bfloat16
ATTEND_ROWS = 256
ATTEND_KEYS = 512
VMEM_LIMIT = 40 << 20


def after(x, *earlier):
    return lax.optimization_barrier((x, earlier))[0]


def swap_cores(x):
    return lax.ppermute(x, "head", [(0, 1), (1, 0)])


def to_near(x, k):
    return lax.ppermute(x, "near", [(i, i ^ k) for i in range(lax.axis_size("near"))])


def around(x, distance):
    count = lax.axis_size("group")
    return lax.ppermute(x, "group", [(i, (i + distance) % count) for i in range(count)])


def step_group(x, distance):
    count = lax.axis_size("group")
    route = [(i, i + distance) for i in range(count) if 0 <= i + distance < count]
    return lax.ppermute(x, "group", route)


def place_kernel(count, index, *refs):
    for k, block in enumerate(refs[:count]):
        at = 0
        for out in refs[count:]:
            cols = slice(at, at + out.shape[-1])
            out[index[k]] = block[..., cols]
            at = cols.stop


def placed(index, blocks, widths=None):
    block = blocks[0]
    shapes = [
        jax.ShapeDtypeStruct((len(blocks), *block.shape[:-1], w), block.dtype)
        for w in widths or block.shape[-1:]
    ]
    kernel = functools.partial(place_kernel, len(blocks))
    out = whole_call(kernel, shapes, [], jnp.stack(index).astype(jnp.int32), *blocks)
    return out if widths else out[0]


def near_places():
    here = lax.axis_index("near")
    return [here ^ k for k in range(lax.axis_size("near"))]


def sent_near(x):
    blocks = [lax.dynamic_index_in_dim(x, at, 0, False) for at in near_places()]
    return [to_near(b, k) if k else b for k, b in enumerate(blocks)]


def trade_near(x):
    return placed(near_places(), sent_near(x))


def added(blocks):
    total = blocks[0].astype(F32)
    for block in blocks[1:]:
        total = total + block.astype(F32)
    return total


def gather_near(x):
    places = near_places()
    return placed(places, [x] + [to_near(x, k) for k in range(1, len(places))])


def trade_all(x):
    return lax.all_to_all(x, ("group", "near"), 0, 0, tiled=True)


def both_halves(mine, other, dim):
    first = lax.axis_index("head") == 0
    return jnp.concatenate([jnp.where(first, mine, other), jnp.where(first, other, mine)], dim)


def own_half(x):
    half = x.shape[0] // 2
    return lax.dynamic_slice_in_dim(x, lax.axis_index("head") * half, half, 0)


def tokens_kernel(gained, index, *refs):
    *refs, out = refs
    gain = refs.pop()[...] if gained else None
    count = len(refs) // 2
    for k in range(count):
        for side in range(2):
            value = refs[k + side * count][...]
            if gained:
                value = value.astype(F32)
                power = jnp.mean(value * value, 1, keepdims=True)
                value = (value * lax.rsqrt(power + EPS) * gain).astype(B16)
            out[index[k], index[count + side]] = value


def sent_tokens(mine):
    got = [mine] + [to_near(mine, k) for k in range(1, lax.axis_size("near"))]
    return [*got, *map(swap_cores, got)]


def placed_tokens(parts, gain=None):
    core, places = lax.axis_index("head"), near_places()
    rows, width = parts[0].shape
    index = jnp.stack([*places, core, 1 - core]).astype(jnp.int32)
    operands = [index, *parts]
    if gain is not None:
        operands.append(gain[None, :])
    shape = jax.ShapeDtypeStruct((len(places), 2, rows, width), parts[0].dtype)
    kernel = functools.partial(tokens_kernel, gain is not None)
    return whole_call(kernel, shape, [], *operands).reshape(-1, width)


def gather_tokens(mine):
    return placed_tokens(sent_tokens(mine))


def dots_kernel(turned, core, *refs):
    *refs, give, keep = refs
    pairs = len(turned)
    for out, side in (give, 1 - core[0]), (keep, core[0]):
        lefts = []
        for left in refs[:pairs]:
            blocks = [left[j, side] for j in range(left.shape[0])]
            lefts.append(jnp.concatenate(blocks, 0))
        width = out.shape[1]
        tile = min(width, 512)
        for n in range(width // tile):
            cols = slice(n * tile, (n + 1) * tile)
            total = None
            for left, right, turn in zip(lefts, refs[pairs:], turned):
                part = dot_nt(left, right[cols]) if turn else dot(left, right[:, cols])
                total = part if total is None else total + part
            out[:, cols] = total.astype(B16)


def summed_dots(width, *pairs):
    lefts, rights, specs, turned, work = [], [], [], [], 0
    near = lax.axis_size("near")
    for left, right in pairs:
        span, depth = left.shape
        lefts.append(left.reshape(near, 2, span // near // 2, depth))
        turned.append(isinstance(right, tuple))
        array, at = right if turned[-1] else (right, 0)
        shape = (width, depth) if turned[-1] else array.shape
        specs.append(pl.BlockSpec(shape, lambda i, at=at: (0, at)))
        rights.append(array)
        work += 2 * span * width * depth
    smem = pl.BlockSpec(memory_space=pltpu.SMEM)
    wholes = [pl.BlockSpec(a.shape, lambda i: (0, 0, 0, 0)) for a in lefts]
    shape = (lefts[0].shape[0] * lefts[0].shape[2], width)
    return pl.pallas_call(
        functools.partial(dots_kernel, turned),
        grid=(1,),
        in_specs=[smem, *wholes, *specs],
        out_specs=[pl.BlockSpec(shape, lambda i: (0, 0))] * 2,
        out_shape=[jax.ShapeDtypeStruct(shape, B16)] * 2,
        cost_estimate=pl.CostEstimate(flops=0, bytes_accessed=0, transcendentals=0),
        compiler_params=pltpu.CompilerParams(vmem_limit_bytes=VMEM_LIMIT),
    )(lax.axis_index("head").astype(jnp.int32).reshape(1), *lefts, *rights)


def grads_kernel(count, *refs):
    *refs, out = refs
    at = 0
    for left, right in zip(refs[:count], refs[count:]):
        cols = slice(at, at + right.shape[1])
        out[:, cols] = dot_tn(left[...], right[...]).astype(B16)
        at = cols.stop


def joined_grads(*pairs):
    lefts, rights = zip(*pairs)
    span, width = lefts[0].shape
    total = sum(r.shape[1] for r in rights)
    tile = min(width, 512)
    return pl.pallas_call(
        functools.partial(grads_kernel, len(pairs)),
        grid=(width // tile,),
        in_specs=[pl.BlockSpec((span, tile), lambda i: (0, i))] * len(pairs)
        + [pl.BlockSpec(r.shape, lambda i: (0, 0)) for r in rights],
        out_specs=pl.BlockSpec((tile, total), lambda i: (i, 0)),
        out_shape=jax.ShapeDtypeStruct((width, total), B16),
        cost_estimate=pl.CostEstimate(flops=0, bytes_accessed=0, transcendentals=0),
        compiler_params=pltpu.CompilerParams(vmem_limit_bytes=VMEM_LIMIT),
    )(*lefts, *rights)


def meet_kernel(index, keep, got, *outs):
    rows = outs[0].shape[0]
    for k, out in enumerate(outs):
        part = pl.ds(pl.multiple_of(index[k] * rows, rows), rows)
        out[...] = (keep[part].astype(F32) + got[part].astype(F32)).astype(B16)


def partial_tokens(width, pairs):
    return met_tokens(*summed_dots(width, *pairs))


def met_tokens(give, keep):
    places = near_places()
    got = swap_cores(give)
    rows, width = keep.shape[0] // len(places), keep.shape[1]
    shapes = [jax.ShapeDtypeStruct((rows, width), B16)] * len(places)
    index = jnp.stack(places).astype(jnp.int32)
    return whole_call(meet_kernel, shapes, [], index, keep, got)


def scatter_tokens(blocks, alongside=None):
    blocks = [to_near(b, k) if k else b for k, b in enumerate(blocks)]
    if alongside is not None:
        blocks, alongside = lax.optimization_barrier((blocks, alongside))
    return added(blocks), alongside


def dot(left, right, dims=((1,), (0,))):
    return lax.dot_general(left, right, (dims, ((), ())), preferred_element_type=F32)


def dot_nt(left, right):
    return dot(left, right, ((1,), (1,)))


def dot_tn(left, right):
    return dot(left, right, ((0,), (0,)))


def dot_exact(left, right, dims=((1,), (0,))):
    return lax.dot_general(
        left, right, (dims, ((), ())), precision=HIGHEST, preferred_element_type=F32
    )


def normalize(values, gain):
    factor = lax.rsqrt(jnp.mean(values * values, -1, keepdims=True) + EPS)
    unit = values * factor
    return unit * gain, unit, factor


def norm_back(grad_out, unit, factor, gain):
    grad_unit = grad_out * gain[None, :]
    grad_in = factor * (grad_unit - unit * jnp.mean(grad_unit * unit, -1, keepdims=True))
    return grad_in, jnp.sum(grad_out * unit, 0)


def rotate_pair(first, second, cosine, sine):
    return first * cosine - second * sine, second * cosine + first * sine


def conv(inputs, edge, weight, bias, dim):
    length = inputs.shape[dim]
    padded = jnp.concatenate([edge, inputs], dim)
    total = bias
    for tap in range(CONV):
        total = total + weight[tap] * lax.slice_in_dim(padded, tap, tap + length, axis=dim)
    return total


def conv_back(grad, grad_edge, inputs, edge, weight, dim):
    length = inputs.shape[dim]
    padded = jnp.concatenate([edge, inputs], dim)
    late = jnp.concatenate([grad, grad_edge], dim)
    total = 0.0
    taps = []
    for tap in range(CONV):
        back = CONV - 1 - tap
        total = total + weight[tap] * lax.slice_in_dim(late, back, back + length, axis=dim)
        taps.append(jnp.sum(grad * lax.slice_in_dim(padded, tap, tap + length, axis=dim), dim))
    return total, jnp.stack(taps), jnp.sum(grad, dim)


def silu_slope(v):
    s = jax.nn.sigmoid(v)
    return s * (1.0 + v * (1.0 - s))


def row_block(i):
    return slice(i * ATTEND_ROWS, (i + 1) * ATTEND_ROWS)


def attend_kernel(index, q, *refs):
    *parts, out, lse, k_t, v_t, total, top, mass = refs
    span = q.shape[0]
    wide = min(ATTEND_KEYS, span)
    keys = HEAD_DIM // len(parts)
    half = keys // 2

    @pl.loop(0, index[0] + 1)
    def _(r):
        for k, part in enumerate(parts):
            at = pl.multiple_of(index[k + 1] * half, half)
            own = pl.multiple_of(r * 2 * keys, 2 * keys)
            k_t[r, pl.ds(at, half)] = part[pl.ds(own, half)]
            k_t[r, pl.ds(at + HEAD_DIM // 2, half)] = part[pl.ds(own + half, half)]
            at = pl.multiple_of(index[k + 1] * keys, keys)
            v_t[r, pl.ds(at, keys)] = part[pl.ds(own + keys, keys)]

    @pl.loop(index[0] + 1, k_t.shape[0])
    def _(r):
        k_t[r] = jnp.zeros(k_t.shape[1:], B16)
        v_t[r] = jnp.zeros(v_t.shape[1:], B16)

    def meet(i, keys_t, values_t, first):
        scores = dot(q[row_block(i)], keys_t) * HEAD_DIM**-0.5
        if first:
            rows = i * ATTEND_ROWS + lax.broadcasted_iota(jnp.int32, scores.shape, 0)
            cols = lax.broadcasted_iota(jnp.int32, scores.shape, 1)
            scores = jnp.where(cols <= rows, scores, MASKED)
        peak = jnp.max(scores, 1, keepdims=True)
        if not first:
            old = top[row_block(i)]
            peak = jnp.maximum(old, peak)
            fade = jnp.exp(old - peak)
        probs = jnp.exp(scores - peak)
        weight = jnp.sum(probs, 1, keepdims=True)
        read = dot_nt(probs.astype(B16), values_t)
        if not first:
            weight = weight + fade * mass[row_block(i)]
            read = read + fade * total[row_block(i)]
        top[row_block(i)] = peak
        mass[row_block(i)] = weight
        total[row_block(i)] = read

    for i in range(span // ATTEND_ROWS):
        keys = (i + 1) * ATTEND_ROWS
        meet(i, k_t[0, :, :keys], v_t[0, :, :keys], True)

    @pl.loop(1, index[0] + 1)
    def _(r):
        for j in range(span // wide):
            keys_t = k_t[r, :, j * wide : (j + 1) * wide]
            values_t = v_t[r, :, j * wide : (j + 1) * wide]
            for i in range(span // ATTEND_ROWS):
                meet(i, keys_t, values_t, False)

    out[...] = total[...] / mass[...]
    lse[...] = top[...] + jnp.log(mass[...])


def whole_call(kernel, out_shape, scratch, index, *operands):
    def whole(array):
        return pl.BlockSpec(array.shape, lambda i: (0,) * len(array.shape))

    return pl.pallas_call(
        kernel,
        grid=(1,),
        out_shape=out_shape,
        in_specs=[pl.BlockSpec(memory_space=pltpu.SMEM), *map(whole, operands)],
        out_specs=jax.tree.map(whole, out_shape),
        scratch_shapes=scratch,
        cost_estimate=pl.CostEstimate(flops=0, bytes_accessed=0, transcendentals=0),
        compiler_params=pltpu.CompilerParams(vmem_limit_bytes=VMEM_LIMIT),
    )(index, *operands)


def attend(index, queries, parts):
    span, groups = queries.shape[0], lax.axis_size("group")
    shape = jax.ShapeDtypeStruct
    turned = shape((groups, HEAD_DIM, span), B16)
    column = pltpu.VMEM((span, 1), F32)
    return whole_call(
        attend_kernel,
        (shape((span, HEAD_DIM), F32), shape((span, 1), F32), turned, turned),
        [pltpu.VMEM((span, HEAD_DIM), F32), column, column],
        index,
        queries,
        *parts,
    )


def attend_back_kernel(index, q, q_t, d, d_t, k_t, v_t, lse, delta, grad_q, *refs):
    *outs, sum_k, sum_v = refs
    span = q.shape[0]
    keys = HEAD_DIM // len(outs)
    half = keys // 2
    wide = min(ATTEND_KEYS, span)
    blocks = span // ATTEND_ROWS

    def meet(i, keys_t, values_t, offset, total_q):
        part = row_block(i)
        scores = dot(q[part], keys_t) * HEAD_DIM**-0.5
        if offset is not None:
            rows = i * ATTEND_ROWS + lax.broadcasted_iota(jnp.int32, scores.shape, 0)
            cols = offset + lax.broadcasted_iota(jnp.int32, scores.shape, 1)
            scores = jnp.where(cols <= rows, scores, MASKED)
        probs = jnp.exp(scores - lse[part])
        grad_scores = (probs * (dot(d[part], values_t) - delta[part])).astype(B16)
        update = dot_nt(grad_scores, keys_t)
        grad_q[part] = update if total_q is None else grad_q[part] + update
        return dot(q_t[:, part], grad_scores), dot(d_t[:, part], probs.astype(B16))

    def store(r, cols, pair):
        sum_k[...] = (pair[0] * HEAD_DIM**-0.5).astype(B16)
        sum_v[...] = pair[1].astype(B16)
        for k, out in enumerate(outs):
            at = pl.multiple_of(index[k + 1] * half, half)
            own = r * 2 * keys if isinstance(r, int) else pl.multiple_of(r * 2 * keys, 2 * keys)
            out[pl.ds(own, half), cols] = sum_k[pl.ds(at, half)]
            out[pl.ds(own + half, half), cols] = sum_k[pl.ds(at + HEAD_DIM // 2, half)]
            at = pl.multiple_of(index[k + 1] * keys, keys)
            out[pl.ds(own + keys, keys), cols] = sum_v[pl.ds(at, keys)]

    for j in range(span // wide):
        cols = slice(j * wide, (j + 1) * wide)
        pair = None
        for i in range(j * wide // ATTEND_ROWS, blocks):
            more = meet(i, k_t[0, :, cols], v_t[0, :, cols], j * wide, None if j == 0 else True)
            pair = more if pair is None else (pair[0] + more[0], pair[1] + more[1])
        store(0, cols, pair)

    @pl.loop(1, index[0] + 1)
    def _(r):
        for j in range(span // wide):
            cols = slice(j * wide, (j + 1) * wide)
            pair = None
            for i in range(blocks):
                more = meet(i, k_t[r, :, cols], v_t[r, :, cols], None, True)
                pair = more if pair is None else (pair[0] + more[0], pair[1] + more[1])
            store(r, cols, pair)

    @pl.loop(index[0] + 1, k_t.shape[0])
    def _(r):
        for out in outs:
            own = pl.ds(pl.multiple_of(r * 2 * keys, 2 * keys), 2 * keys)
            out[own] = jnp.zeros((2 * keys, span), B16)


def attend_back(index, queries, keys_t, values_t, grad, lse, delta):
    span, groups = queries.shape[0], keys_t.shape[0]
    near = lax.axis_size("near")
    shape = jax.ShapeDtypeStruct
    part = shape((groups * 2 * HEAD_DIM // near, span), B16)
    wide = pltpu.VMEM((HEAD_DIM, min(ATTEND_KEYS, span)), B16)
    grad_q, *parts = whole_call(
        attend_back_kernel,
        (shape(queries.shape, F32), *[part] * near),
        [wide, wide],
        index,
        queries,
        queries.T,
        grad,
        grad.T,
        keys_t,
        values_t,
        lse,
        delta,
    )
    return grad_q, parts


def in_two(x):
    high = x.astype(B16)
    return high, (x - high.astype(F32)).astype(B16)


def dot_half(low, x, dims=((1,), (0,))):
    high, rest = in_two(x)
    return dot(low, high, dims) + dot(low, rest, dims)


def dot_fine(left, right, dims=((1,), (0,))):
    high, rest = in_two(left)
    other, more = in_two(right)
    return dot(high, other, dims) + (dot(high, more, dims) + dot(rest, other, dims))


def spread(per_head, of_head):
    return dot_exact(per_head, of_head, ((0,), (0,)))


def head_decay(cum, cum_t, h):
    length = cum.shape[0]
    rows = lax.broadcasted_iota(jnp.int32, (length, length), 0)
    cols = lax.broadcasted_iota(jnp.int32, (length, length), 1)
    gap = cum[:, h : h + 1] - cum_t[h : h + 1, :]
    return jnp.exp(jnp.where(cols <= rows, gap, MASKED))


def in_head(shape, h, channels):
    lane = lax.broadcasted_iota(jnp.int32, shape, 1)
    return (lane >= h * channels) & (lane < (h + 1) * channels)


def scan_kernel(heads, x, dt, cum, cum_t, b_t, c_t, of_head, y, ends, state):
    @pl.when(pl.program_id(0) == 0)
    def _():
        state[...] = jnp.zeros_like(state)

    channels = x.shape[1] // heads
    per = HEAD_DIM // channels
    owner = of_head[...]
    cums, cums_t = cum[...], cum_t[...]
    scaled = x[...] * spread(dt[...], owner)
    inner = dot_tn(c_t[...], b_t[...])
    wide = spread(cums_t, owner)
    end = wide[-1:]
    carried = dot_half(c_t[...], state[...], ((0,), (0,))) * jnp.exp(wide)
    for at in range(heads // per):
        lanes = slice(at * HEAD_DIM, (at + 1) * HEAD_DIM)
        block = scaled[:, lanes]
        within = None
        for k in range(per):
            mixing = head_decay(cums, cums_t, at * per + k) * inner
            part = dot_fine(mixing, block)
            mine = in_head(part.shape, k, channels)
            within = part if within is None else jnp.where(mine, part, within)
        y[:, lanes] = within + carried[:, lanes]
    state[...] = jnp.exp(end) * state[...] + dot_half(b_t[...], scaled * jnp.exp(end - wide))
    ends[0] = state[...]


class ChunkSpecs:
    def __init__(self, rows, chunks, turned):
        self.rows, self.chunks = rows, chunks
        self.chunk = (lambda c: chunks - 1 - c) if turned else (lambda c: c)

    def by_row(self, width):
        return pl.BlockSpec((self.rows, width), lambda c: (self.chunk(c), 0))

    def by_col(self, height):
        return pl.BlockSpec((height, self.rows), lambda c: (0, self.chunk(c)))

    def stacked(self, array, more=0):
        shape = (1, *array.shape[1:])
        return pl.BlockSpec(shape, lambda c: (jnp.maximum(self.chunk(c) + more, 0), 0, 0))

    def whole(self, array):
        return pl.BlockSpec(array.shape, lambda c: (0,) * len(array.shape))


def chunk_call(kernel, chunks, in_specs, out_specs, out_shape, scratch, *operands):
    return pl.pallas_call(
        kernel,
        grid=(chunks,),
        in_specs=in_specs,
        out_specs=out_specs,
        out_shape=out_shape,
        scratch_shapes=scratch,
        cost_estimate=pl.CostEstimate(flops=0, bytes_accessed=0, transcendentals=0),
        compiler_params=pltpu.CompilerParams(vmem_limit_bytes=VMEM_LIMIT),
    )(*operands)


def scan_forward(heads, x, dt, cum, cum_t, b_t, c_t, of_head, rows):
    span, inner = x.shape
    chunks, padded = span // rows, dt.shape[0]
    at = ChunkSpecs(rows, chunks, False)
    ends = jax.ShapeDtypeStruct((chunks, STATE, inner), F32)
    return chunk_call(
        functools.partial(scan_kernel, heads),
        chunks,
        [
            at.by_row(inner),
            at.by_col(padded),
            at.by_row(padded),
            at.by_col(padded),
            at.by_col(STATE),
            at.by_col(STATE),
            at.whole(of_head),
        ],
        [at.by_row(inner), at.stacked(ends)],
        [jax.ShapeDtypeStruct((span, inner), F32), ends],
        [pltpu.VMEM((STATE, inner), F32)],
        x,
        dt,
        cum,
        cum_t,
        b_t,
        c_t,
        of_head,
    )


def within_kernel(heads, x, dt, cum, cum_t, b_t, c_t, of_head, ends, through, entering, grad, *outs):
    within, grad_bt, grad_ct = outs
    channels = x.shape[1] // heads
    per = HEAD_DIM // channels
    owner = of_head[...]
    cums, cums_t = cum[...], cum_t[...]
    scaled = x[...] * spread(dt[...], owner)
    inner = dot_tn(c_t[...], b_t[...])
    back = grad[...]
    faded = back * jnp.exp(spread(cums_t, owner))
    grad_inner = jnp.zeros_like(inner)
    for at in range(heads // per):
        lanes = slice(at * HEAD_DIM, (at + 1) * HEAD_DIM)
        total = None
        for k in range(per):
            decay = head_decay(cums, cums_t, at * per + k)
            part = dot_fine(decay * inner, back[:, lanes], ((0,), (0,)))
            mine = in_head(part.shape, k, channels)
            total = part if total is None else jnp.where(mine, part, total)
            only = jnp.where(mine, back[:, lanes], 0.0)
            grad_inner += dot_fine(only, scaled[:, lanes], ((1,), (1,))) * decay
        within[:, lanes] = total
    state_in = through[0] * entering[...]
    state_in = state_in + jnp.where(pl.program_id(0) == 0, 0.0, ends[0])
    grad_ct[...] = (
        dot_half(b_t[...], grad_inner, ((1,), (1,))) + dot_fine(state_in, faded, ((1,), (1,)))
    ).astype(B16)
    grad_bt[...] = dot_half(c_t[...], grad_inner)


def scan_within(heads, x, dt, cum, cum_t, b_t, c_t, of_head, ends, through, entering, grad, rows):
    span, inner = x.shape
    chunks, padded = span // rows, dt.shape[0]
    at = ChunkSpecs(rows, chunks, False)
    shape = jax.ShapeDtypeStruct
    return chunk_call(
        functools.partial(within_kernel, heads),
        chunks,
        [
            at.by_row(inner),
            at.by_col(padded),
            at.by_row(padded),
            at.by_col(padded),
            at.by_col(STATE),
            at.by_col(STATE),
            at.whole(of_head),
            at.stacked(ends, -1),
            at.stacked(through),
            at.whole(entering),
            at.by_row(inner),
        ],
        [at.by_row(inner), at.by_col(STATE), at.by_col(STATE)],
        [shape((span, inner), F32), shape((STATE, span), F32), shape((STATE, span), B16)],
        [],
        x,
        dt,
        cum,
        cum_t,
        b_t,
        c_t,
        of_head,
        ends,
        through,
        entering,
        grad,
    )


def across_kernel(
    x,
    x_pre,
    dt,
    cum_t,
    b_t,
    c_t,
    of_head,
    skip,
    ends,
    through,
    entering,
    y,
    grad,
    within,
    bt_part,
    leaving,
    grad_xpre,
    grad_bt,
    grad_logs,
    grad_dt,
    grad_skip,
    grad_state,
):
    @pl.when(pl.program_id(0) == 0)
    def _():
        grad_state[...] = leaving[...]
        grad_skip[...] = jnp.zeros_like(grad_skip)

    owner = of_head[...]
    low_owner = owner.astype(B16)
    times = spread(dt[...], owner)
    values = x[...]
    scaled = values * times
    wide = spread(cum_t[...], owner)
    end = wide[-1:]
    tail = jnp.exp(end - wide)
    back = grad[...]
    to_state = grad_state[...]
    grad_scaled = within[...] + tail * dot_half(b_t[...], to_state, ((0,), (0,)))
    grad_bt[...] = (bt_part[...] + dot_fine(to_state, scaled * tail, ((1,), (1,)))).astype(B16)
    grad_xpre[...] = (grad_scaled * times + skip[...] * back) * silu_slope(x_pre[...])
    grad_skip[...] += jnp.sum(back * values, 0, keepdims=True)
    state_out = ends[0] + through[0] * entering[...]
    at_end = jnp.sum(state_out * to_state, 0, keepdims=True)
    change = back * y[...] - grad_scaled * scaled
    rows = lax.broadcasted_iota(jnp.int32, change.shape, 0)
    change = change + jnp.where(rows == change.shape[0] - 1, at_end, 0.0)
    per_head = dot_half(low_owner, change, ((1,), (1,)))
    length = change.shape[0]
    later = lax.broadcasted_iota(jnp.int32, (length, length), 0) >= lax.broadcasted_iota(
        jnp.int32, (length, length), 1
    )
    grad_logs[...] = dot_exact(per_head, later.astype(F32))
    grad_dt[...] = dot_half(low_owner, grad_scaled * values, ((1,), (1,)))
    faded = back * jnp.exp(wide)
    grad_state[...] = jnp.exp(end) * to_state + dot_half(c_t[...], faded)


def scan_across(
    x,
    x_pre,
    dt,
    cum_t,
    b_t,
    c_t,
    of_head,
    skip,
    ends,
    through,
    entering,
    y,
    grad,
    within,
    bt_part,
    leaving,
    rows,
):
    span, inner = x.shape
    chunks, padded = span // rows, dt.shape[0]
    at = ChunkSpecs(rows, chunks, True)
    shape = jax.ShapeDtypeStruct
    return chunk_call(
        across_kernel,
        chunks,
        [
            at.by_row(inner),
            at.by_row(inner),
            at.by_col(padded),
            at.by_col(padded),
            at.by_col(STATE),
            at.by_col(STATE),
            at.whole(of_head),
            at.whole(skip),
            at.stacked(ends),
            at.stacked(through, 1),
            at.whole(entering),
            at.by_row(inner),
            at.by_row(inner),
            at.by_row(inner),
            at.by_col(STATE),
            at.whole(leaving),
        ],
        [
            at.by_row(inner),
            at.by_col(STATE),
            at.by_col(padded),
            at.by_col(padded),
            at.whole(skip),
        ],
        [
            shape((span, inner), F32),
            shape((STATE, span), B16),
            shape((padded, span), F32),
            shape((padded, span), F32),
            shape(skip.shape, F32),
        ],
        [pltpu.VMEM((STATE, inner), F32)],
        x,
        x_pre,
        dt,
        cum_t,
        b_t,
        c_t,
        of_head,
        skip,
        ends,
        through,
        entering,
        y,
        grad,
        within,
        bt_part,
        leaving,
    )


def flat(x):
    return with_layout_constraint(x, Layout(tuple(range(x.ndim))))


def cotangent_half(cotangent):
    return own_half(cotangent).astype(F32)


def home_kernel(runs, index, *refs):
    blocks, outs = refs[: -len(runs)], refs[-len(runs) :]
    for k, block in enumerate(blocks):
        at = 0
        for out, (width, across) in zip(outs, runs):
            piece = block[:, at : at + width].astype(F32)
            at += width
            place = pl.ds(pl.multiple_of(index[k] * width, width), width)
            if across:
                out[:, place] = piece
            else:
                out[place] = piece.T


def homed(blocks, *runs):
    count, piece = len(blocks), blocks[0].shape[0]
    shapes = [(piece, count * w) if across else (count * w, piece) for w, across in runs]
    shapes = [jax.ShapeDtypeStruct(shape, F32) for shape in shapes]
    index = jnp.stack(near_places()).astype(jnp.int32)
    return whole_call(functools.partial(home_kernel, runs), shapes, [], index, *blocks)


def per_device(
    tokens,
    cotangent,
    g1,
    w_q,
    w_k,
    w_v,
    w_o,
    w_z,
    w_x,
    w_bc,
    w_dt,
    conv_bc,
    conv_bc_bias,
    w_out,
    g2,
    w_gate,
    w_up,
    w_down,
    conv_x,
    conv_x_bias,
    dt_bias,
    a_log,
    d_skip,
):
    near, groups = lax.axis_size("near"), lax.axis_size("group")
    here, group, core = (lax.axis_index(a) for a in ("near", "group", "head"))
    rows, width = tokens.shape
    span = near * rows
    piece = w_q.shape[0]
    devices = near * groups
    key_cols = HEAD_DIM // near
    half_cols = key_cols // 2
    heads = w_dt.shape[1] // near
    padded = heads + -heads % 8
    inner, q_cols, ff = w_z.shape[1] // near, w_q.shape[1] // near, w_gate.shape[1] // near
    o_rows = w_o.shape[0] // near
    at_q = 2 * inner // q_cols

    def columns(w):
        return w.reshape(w.shape[0], near, -1).transpose(1, 0, 2)

    def share(x, dim):
        size = x.shape[dim] // near
        return lax.dynamic_slice_in_dim(x, here * size, size, dim)

    def by_head(x):
        return jnp.pad(share(x, 0).astype(F32), (0, padded - heads))[:, None]

    k_cols = w_k.reshape(piece, 2, near, half_cols).transpose(2, 0, 1, 3)
    w_bc_mine = lax.dynamic_slice_in_dim(w_bc, core * STATE, STATE, 1)
    pack1 = [columns(w_x), k_cols.reshape(near, piece, key_cols), columns(w_v)]
    pack1 = jnp.concatenate([*pack1, columns(w_bc_mine)], 2)
    extra = jnp.concatenate([g1, g2, conv_bc.reshape(-1), conv_bc_bias])
    n_small, n_dt = extra.shape[0], heads * piece
    extra = jnp.broadcast_to(extra, (near, n_small))
    extra = jnp.concatenate([extra, w_dt.T.reshape(near, n_dt)], 1)
    extra = jnp.pad(extra, ((0, 0), (0, -extra.shape[1] % (8 * pack1.shape[2]))))
    pack1 = jnp.concatenate([pack1, extra.reshape(near, -1, pack1.shape[2])], 1)
    full1 = jnp.broadcast_to(pack1, (groups, *pack1.shape)).reshape(devices, *pack1.shape[1:])
    full1 = trade_all(full1)
    token_parts = sent_tokens(own_half(tokens))
    pack2 = [columns(w_z), columns(w_out.T), columns(w_q), columns(w_o.T)]
    pack2 = jnp.concatenate(pack2, 2)
    pack3 = jnp.concatenate([columns(w_gate), columns(w_up), columns(w_down.T)], 2)
    sent2 = sent_near(pack2)
    positions = (group * span + jnp.arange(span)).astype(F32)
    half = HEAD_DIM // 2
    freqs = ROPE_BASE ** (-jnp.arange(half, dtype=F32) / half)
    angle = positions[:, None] * freqs[None, :]
    cos_q, sin_q = jnp.cos(angle), jnp.sin(angle)
    cos_k, sin_k = (share(x, 1).T for x in (cos_q, sin_q))
    of_head = jnp.arange(inner)[None, :] // (inner // heads) == jnp.arange(padded)[:, None]
    of_head = of_head.astype(F32)
    decay_rate, head_bias = jnp.exp(by_head(a_log)), by_head(dt_bias)
    skip = spread(by_head(d_skip), of_head)
    triangle = jnp.triu(jnp.ones((rows, rows), F32))
    taps_x = share(conv_x, 1).astype(F32)[:, None, :]
    bias_x = share(conv_x_bias, 0).astype(F32)[None, :]
    my_tokens = own_half(tokens).astype(F32)
    early = (cos_q, sin_q, cos_k, sin_k, of_head, decay_rate, head_bias, skip, triangle)
    early = (*early, taps_x, bias_x, my_tokens, pack3)
    full1, early = lax.optimization_barrier((full1, early))
    cos_q, sin_q, cos_k, sin_k, of_head, decay_rate, head_bias, skip, triangle = early[:9]
    taps_x, bias_x, my_tokens, pack3 = early[9:]

    extra = full1[:, piece:].reshape(devices, -1)
    smalls = extra[:, :n_small].astype(F32)
    gain1 = smalls[:, :piece].reshape(-1)
    gain2 = smalls[:, piece : 2 * piece].reshape(-1)
    full_dt = extra[:, n_small : n_small + n_dt].reshape(devices, heads, piece)
    full_dt = full_dt.transpose(1, 0, 2).reshape(heads, width)
    full_dt = jnp.pad(full_dt, ((0, padded - heads), (0, 0)))
    taps_bc = smalls[:, 2 * piece : -conv_bc_bias.shape[0]].reshape(devices, CONV, -1)
    taps_bc = taps_bc.transpose(1, 0, 2).reshape(CONV, 2, near, -1)
    taps_bc = taps_bc[:, core, here][:, :, None]
    bias_bc = smalls[:, -conv_bc_bias.shape[0] :].reshape(2, near, -1)[core, here][:, None]
    full1 = full1[:, :piece].reshape(width, -1)
    full_x, full_kvbc = full1[:, :inner], full1[:, inner:]
    n1 = placed_tokens(token_parts, gain1)
    grad_parts = sent_tokens(after(own_half(cotangent), n1))

    kvbc = dot(full_kvbc, n1, ((0,), (1,)))
    k_first, k_second = rotate_pair(kvbc[:half_cols], kvbc[half_cols:key_cols], cos_k, sin_k)
    kv = jnp.concatenate([k_first, k_second, kvbc[key_cols : 2 * key_cols]], 0).astype(B16)
    kv = flat(kv)
    kv_parts = [kv] + [step_group(kv, r) for r in range(1, groups)]
    bc_proj = flat(kvbc[2 * key_cols :])
    bc_edge = step_group(bc_proj[:, span - CONV + 1 :], 1)
    sent2, n1, kv = lax.optimization_barrier((sent2, n1, kv))
    full2 = placed(near_places(), sent2).reshape(near * piece, -1)
    n1_x, full2 = lax.optimization_barrier((n1, full2))
    full2 = lax.all_gather(full2, "group", axis=0, tiled=True)

    x_proj = dot(n1_x, full_x)
    x_edge = step_group(x_proj[span - CONV + 1 :], 1)
    sent3 = sent_near(after(pack3, x_proj))

    bc_pre = conv(bc_proj, bc_edge, taps_bc, bias_bc, 1)
    bc_mine = gather_near(flat(jax.nn.silu(bc_pre).astype(B16))).reshape(STATE, span)
    bc_other = swap_cores(bc_mine)
    first = core == 0
    b_t, c_t = jnp.where(first, bc_mine, bc_other), jnp.where(first, bc_other, bc_mine)

    dt_pre = dot_nt(full_dt, n1) + head_bias
    dt = jax.nn.softplus(dt_pre)
    logs = -dt * decay_rate
    cum_t = dot_exact(logs.reshape(padded * near, rows), triangle).reshape(padded, near, rows)
    chunk_total = cum_t[:, :, -1]
    before = jnp.cumsum(chunk_total, 1) - chunk_total
    group_total = jnp.sum(chunk_total, 1, keepdims=True)
    fade = jnp.exp(spread((cum_t + before[:, :, None]).reshape(padded, span), of_head))
    cum_t = cum_t.reshape(padded, span)
    cum = cum_t.T
    group_decay = jnp.exp(spread(group_total, of_head))

    x_pre = conv(x_proj, x_edge, taps_x, bias_x, 0)
    xc = jax.nn.silu(x_pre)
    kv_parts = jnp.concatenate(kv_parts, 0)
    xc = after(xc, kv_parts, *grad_parts)
    sent3, xc = lax.optimization_barrier((sent3, xc))
    full3 = placed(near_places(), sent3).reshape(near * piece, -1)
    xc, full3 = lax.optimization_barrier((xc, full3))
    full3 = lax.all_gather(full3, "group", axis=0, tiled=True)
    kv_parts = [to_near(kv_parts, k) if k else kv_parts for k in range(near)]
    outputs, ends = scan_forward(heads, xc, dt, cum, cum_t, b_t, c_t, of_head, rows)
    through = jnp.concatenate([jnp.zeros_like(group_total), jnp.cumsum(chunk_total, 1)], 1)
    through = jnp.exp(spread(through, of_head))[:, None]

    def state_rows(state):
        pad = jnp.broadcast_to(group_decay, (16, inner))
        return jnp.concatenate([state, pad], 0).astype(B16)

    def sent_states(state, direction):
        return [step_group(state, direction * r) for r in range(1, groups)]

    def chained(parts):
        total = jnp.zeros((STATE, inner), F32)
        for part in reversed(parts):
            part = part.astype(F32)
            total = part[STATE : STATE + 1] * total + part[:STATE]
        return total

    entering = sent_states(state_rows(ends[-1]), 1)
    full_z, full_out_t = full2[:, :inner], full2[:, inner : 2 * inner]
    full_q, full_o_t = full2[:, 2 * inner : 2 * inner + q_cols], full2[:, 2 * inner + q_cols :]
    full_gu, full_down_t = full3[:, : 2 * ff], full3[:, 2 * ff :]
    q_proj = dot(n1, full_q)
    queries = jnp.concatenate(rotate_pair(q_proj[:, :half], q_proj[:, half:], cos_q, sin_q), 1)
    queries = queries.astype(B16)
    z_proj = dot(n1, full_z)
    index = jnp.stack([group, *near_places()]).astype(jnp.int32)
    attended32, lse, keys_t, values_t = attend(index, queries, kv_parts)
    attended = attended32.astype(B16)
    entering = chained(after(entering, attended, z_proj))

    outputs = outputs + fade * dot_tn(c_t, entering.astype(B16))
    y = outputs + skip * xc
    gated = (y * jax.nn.silu(z_proj)).astype(B16)

    pairs = [(gated, (full2, 1)), (attended, (full2, at_q + 1))]
    blocks = partial_tokens(width, pairs)
    all_cotangent = placed_tokens(after(grad_parts, blocks))
    mixed, all_cotangent = scatter_tokens(blocks, alongside=all_cotangent)
    hidden = my_tokens + mixed
    normed2, unit2, factor2 = normalize(hidden, gain2)
    n2 = gather_tokens(normed2.astype(B16))
    both = dot(n2, full_gu)
    gate, up = both[:, :ff], both[:, ff:]
    sigma = jax.nn.sigmoid(gate)
    act = (gate * sigma * up).astype(B16)
    grad_act = dot(all_cotangent, full_down_t)
    grad_gate = grad_act * up * sigma * (1.0 + gate * (1.0 - sigma))
    grad_gu = jnp.concatenate([grad_gate, grad_act * gate * sigma], 1).astype(B16)

    def sum_groups(grad):
        own = lax.psum_scatter(grad, "group", scatter_dimension=0, tiled=True)
        return own.reshape(near, piece, -1)

    partial2 = partial_tokens(width, [(grad_gu, (full3, 0))])
    grads3 = dot_tn(n2, grad_gu).astype(B16)
    grad_n2, (grads3, feed) = scatter_tokens(
        partial2, alongside=(grads3, summed_dots(width, (act, (full3, 2))))
    )
    home3 = sum_groups(grads3)

    grad_norm2, grad_g2 = norm_back(grad_n2, unit2, factor2, gain2)
    grad_hidden = cotangent_half(cotangent) + grad_norm2
    grad_mixed = gather_tokens(grad_hidden.astype(B16))

    grad_gated = dot(grad_mixed, full_out_t).astype(B16).astype(F32)
    sig_z = jax.nn.sigmoid(z_proj)
    grad_y = grad_gated * z_proj * sig_z
    grad_z = (grad_gated * y * sig_z * (1.0 + z_proj * (1.0 - sig_z))).astype(B16)
    read = state_rows(dot(c_t, (grad_y * fade).astype(B16)))
    read_parts = sent_states(read, -1)

    grad_mixed = after(grad_mixed, read)
    grad_attended = dot(grad_mixed, full_o_t).astype(B16)
    delta = jnp.sum(grad_attended.astype(F32) * attended32, 1, keepdims=True)
    grad_q, kv_parts = attend_back(
        index, queries, keys_t, values_t, grad_attended, lse, delta
    )
    kv_parts = [to_near(p, k) if k else p for k, p in enumerate(kv_parts)]
    grad_q = grad_q * HEAD_DIM**-0.5
    grad_q = jnp.concatenate(rotate_pair(grad_q[:, :half], grad_q[:, half:], cos_q, -sin_q), 1)
    grad_zq = jnp.concatenate([grad_z, grad_q.astype(B16)], 1)
    mixer_out = jnp.concatenate([gated, attended], 1)
    read_parts, grad_zq = lax.optimization_barrier((read_parts, grad_zq))
    grads2 = joined_grads((all_cotangent, act), (grad_mixed, mixer_out), (n1, grad_zq))
    home2 = sum_groups(grads2)

    kv_parts, grads2 = lax.optimization_barrier((kv_parts, grads2))
    kv_parts = flat(added(kv_parts))
    kv_sent = kv_parts.astype(B16)
    kv_rows = 2 * key_cols
    grad_kv = [kv_parts[:kv_rows]]
    for r in range(1, groups):
        grad_kv.append(step_group(kv_sent[r * kv_rows : (r + 1) * kv_rows], -r))
    feed = met_tokens(*after(feed, kv_sent))

    feed, grad_y_scan = lax.optimization_barrier((feed, grad_y))
    within, bt_part, grad_ct = scan_within(
        heads, xc, dt, cum, cum_t, b_t, c_t, of_head, ends, through, entering, grad_y_scan, rows
    )
    feed = [to_near(b, k) if k else b for k, b in enumerate(feed)]
    home3 = sent_near(after(home3, kv_sent))
    read_parts, within, home3, feed = lax.optimization_barrier((read_parts, within, home3, feed))
    leaving = chained(read_parts)
    grad_xpre, grad_bt, grad_logs, grad_dt, grad_skip = scan_across(
        xc,
        x_pre,
        dt,
        cum_t,
        b_t,
        c_t,
        of_head,
        skip,
        ends,
        through,
        entering,
        outputs,
        grad_y,
        within,
        bt_part,
        leaving,
        rows,
    )
    kept = jnp.where(first, grad_bt, grad_ct)
    given = swap_cores(jnp.where(first, grad_ct, grad_bt))
    kept = (kept.astype(F32) + given.astype(F32)).astype(B16)
    grad_bc = flat(added(sent_near(kept.reshape(near, -1, span))))

    grad_bcpre = grad_bc * silu_slope(bc_pre)
    next_x = step_group(grad_xpre[: CONV - 1], -1)
    next_bc = step_group(grad_bcpre[:, : CONV - 1], -1)
    grad_x, grad_tapx, grad_biasx = conv_back(grad_xpre, next_x, x_proj, x_edge, taps_x, 0)
    grad_bcp, grad_tapbc, grad_biasbc = conv_back(
        grad_bcpre, next_bc, bc_proj, bc_edge, taps_bc, 1
    )
    grad_kv = added(after(grad_kv, grad_xpre))
    gk_first, gk_second = rotate_pair(
        grad_kv[:half_cols], grad_kv[half_cols:key_cols], cos_k, -sin_k
    )
    grad_kvbc = jnp.concatenate([gk_first, gk_second, grad_kv[key_cols:], grad_bcp], 0)
    grad_first = jnp.concatenate([grad_x.astype(B16), flat(grad_kvbc.astype(B16)).T], 1)

    grad_dt = grad_dt - grad_logs * decay_rate
    grad_dt_pre = grad_dt * jax.nn.sigmoid(dt_pre)
    grad_dt_low = grad_dt_pre.astype(B16)
    grad_skip = dot_exact(of_head, grad_skip, ((1,), (1,)))[:heads, 0]
    grad_alog = jnp.sum(grad_logs * logs, 1)[:heads]
    grad_dtbias = jnp.sum(grad_dt_pre, 1)[:heads]

    grads1 = dot_tn(n1, grad_first).astype(B16)
    grad_first, grads1 = lax.optimization_barrier((grad_first, grads1))
    grad_wdt = dot(grad_dt_low, n1).reshape(padded, devices, piece).transpose(1, 0, 2)
    pairs = [
        (grad_zq[:, :inner], (full2, 0)),
        (grad_zq[:, inner:], (full2, at_q)),
        (grad_first, (full1, 0)),
        (grad_dt_low.T, full_dt),
    ]
    partial1 = partial_tokens(width, pairs)
    output = (hidden + added(after(feed, partial1))).astype(B16)
    output = both_halves(output, swap_cores(output), 0)
    outs3 = homed(after(home3, partial1), (ff, True), (ff, True))
    grad_n1, (sum_wgate, sum_wup, output) = scatter_tokens(partial1, alongside=(*outs3, output))
    _, unit1, factor1 = normalize(my_tokens, gain1)
    grad_norm1, grad_g1 = norm_back(grad_n1, unit1, factor1, gain1)
    grad_tokens = grad_hidden + grad_norm1

    grad_tokens = both_halves(grad_tokens, swap_cores(grad_tokens), 0)

    crossing = jnp.concatenate([grad_g1, grad_g2, grad_tapbc.reshape(-1), grad_biasbc])
    other = swap_cores(crossing)
    gains = 2 * width
    mine = [grad_tapx.reshape(-1), grad_biasx, grad_dtbias, grad_alog, grad_skip]
    mine = [*mine, both_halves(crossing[gains:], other[gains:], 0)]
    ends, at = [], 0
    for g in mine[:-1]:
        at += g.shape[0]
        ends.append(at)
    packed = jnp.concatenate(mine)
    size = packed.shape[0]
    packed = jnp.broadcast_to(packed, (devices, size))
    own_parts = [crossing[:width] + other[:width], crossing[width:gains] + other[width:gains]]
    own_parts = [grad_wdt.reshape(devices, -1), *(p.reshape(devices, -1) for p in own_parts)]
    packed = jnp.concatenate([*own_parts, packed], 1)
    packed = jnp.pad(packed, ((0, 0), (0, -packed.shape[1] % (8 * HEAD_DIM))))
    packed = trade_all(packed.reshape(devices, -1, HEAD_DIM))
    home1 = grads1.reshape(groups, near * piece, -1)
    home1 = [lax.dynamic_index_in_dim(home1, (group + r) % groups, 0, False) for r in range(groups)]
    home1 = [around(b, r) if r else b for r, b in enumerate(home1)]
    home2 = sent_near(after(home2, grad_n1))
    home1, home2 = lax.optimization_barrier((home1, home2))
    home1 = sent_near(added(home1).astype(B16).reshape(near, piece, -1))
    packed, home1 = lax.optimization_barrier((packed, home1))
    packed = packed.reshape(devices, -1)
    n_dt = padded * piece
    sum_wdt = jnp.sum(packed[:, :n_dt].reshape(groups, near, padded, piece), 0)
    sum_wdt = sum_wdt[:, :heads].reshape(-1, piece).T
    own_sums = jnp.sum(packed[:, n_dt : n_dt + 2 * piece], 0)
    packed = packed[:, n_dt + 2 * piece :][:, :size]

    sum_wdown, sum_wout, sum_wo, sum_wz, sum_wq = homed(
        home2, (ff, False), (inner, False), (o_rows, False), (inner, True), (q_cols, True)
    )
    (sum_wx,) = homed(home1, (inner, True))
    home_small = placed(near_places(), [b[:, inner:] for b in home1]).astype(F32)
    home_k, home_v, home_bc = jnp.split(home_small, [key_cols, 2 * key_cols], 2)
    sum_wv = home_v.transpose(1, 0, 2).reshape(piece, -1)
    sum_wk = home_k.reshape(near, piece, 2, half_cols).transpose(1, 2, 0, 3)
    sum_wk = sum_wk.reshape(piece, -1)
    bc_mine = home_bc.transpose(1, 0, 2).reshape(piece, -1)
    sum_wbc = both_halves(bc_mine, swap_cores(bc_mine), 1)

    every = jnp.split(packed, ends, 1)
    place = group * near + here

    def by_near(x):
        return jnp.sum(x.reshape(groups, near, -1), 0)

    sum_g1, sum_g2 = own_sums[:piece], own_sums[piece:]
    sum_convx = by_near(every[0]).reshape(near, CONV, -1).transpose(1, 0, 2).reshape(CONV, -1)
    sum_convxb, sum_dtbias, sum_alog, sum_dskip = (by_near(x).reshape(-1) for x in every[1:5])
    sum_bc = by_near(every[5]).reshape(near, 2, CONV + 1, -1).transpose(2, 1, 0, 3)
    sum_bc = sum_bc.reshape(CONV + 1, -1)
    bc_cols = conv_bc.shape[1]
    sum_bc = lax.dynamic_slice_in_dim(sum_bc, place * bc_cols, bc_cols, 1)
    return (
        output,
        grad_tokens,
        sum_g1,
        sum_wq,
        sum_wk,
        sum_wv,
        sum_wo,
        sum_wz,
        sum_wx,
        sum_wbc,
        sum_wdt,
        sum_bc[:CONV],
        sum_bc[CONV],
        sum_wout,
        sum_g2,
        sum_wgate,
        sum_wup,
        sum_wdown,
        sum_convx,
        sum_convxb,
        sum_dtbias,
        sum_alog,
        sum_dskip,
    )


def solution(mesh):
    seq, cores = mesh.shape["seq"], mesh.shape["head"]
    near = math.gcd(seq, 4)
    split = Mesh(mesh.devices.reshape(seq // near, near, cores), ("group", "near", "head"))
    seq = ("group", "near")
    row_split = P(seq, "head")
    col_split = P("head", seq)
    weights = (
        P(seq),
        row_split,
        row_split,
        row_split,
        col_split,
        row_split,
        row_split,
        P(seq, None),
        row_split,
        P(None, seq),
        P(seq),
        col_split,
        P(seq),
        row_split,
        row_split,
        col_split,
        P(None, "head"),
        P("head"),
        P("head"),
        P("head"),
        P("head"),
    )
    tokens = P(seq, None)
    return jax.shard_map(
        per_device,
        mesh=split,
        in_specs=(tokens, tokens, *weights),
        out_specs=(tokens, tokens, *weights),
        check_vma=False,
    )
```

time: 790 us -> 705 us (0.89)
  local copies, waits for them, and re-layouts: 152 us -> 83.9 us
  other arithmetic: 83.2 us -> 64.9 us
  matrix products: 45.2 us -> 55 us
  Pallas kernels: 101 us -> 92 us
  starting transfers between devices: 116 us -> 125 us
  waiting for transfers between devices: 264 us -> 255 us
    unnamed x411 -> x416, local copies, waits for them, and re-layouts: 72.1 us -> 43.4 us
    ppermute x16, starting transfers between devices: 28 us -> 43.1 us  [step_group(): return lax.ppermute(x, 'group', route)]
    ppermute x16, waiting for transfers between devices: 70.7 us -> 59.2 us  [step_group(): return lax.ppermute(x, 'group', route)]
    ppermute x6 -> x0, local copies, waits for them, and re-layouts: 10.4 us -> none  [to_near(): lax.ppermute(x, 'near', [(i, i ^ k) for i in range(lax.axis_size('near'))])]
    convert_element_type x8 -> x1, local copies, waits for them, and re-layouts: 11 us -> 0.84 us  [per_device(): grad_attended = dot(grad_mixed, full_o_t).astype(B16)]
    dot_general x13 -> x14, matrix products: 41.2 us -> 51 us  [dot(): lax.dot_general(left, right, (dims, ((), ())), preferred_element_type=F32)]
    ppermute x51, waiting for transfers between devices: 158 us -> 167 us  [to_near(): lax.ppermute(x, 'near', [(i, i ^ k) for i in range(lax.axis_size('near'))])]
    ppermute x3, waiting for transfers between devices: 17.8 us -> 9.37 us  [around(): lax.ppermute(x, 'group', [(i, (i + distance) % count) for i in range(coun...]
  transfers between devices with their start and end apart: 102 -> 102, of which waited for: 39 -> 43; matrix products, arithmetic and copies ran while one was open for 26% -> 20% of each run, Pallas kernels for 12% -> 12%
where the time goes in v3:
time: 705 us; the launch traced here: 694 us
  waiting for transfers between devices  255 us (36%)
  starting transfers between devices  125 us (18%)
  Pallas kernels  92 us (13%)
  local copies, waits for them, and re-layouts  83.9 us (12%)
  other arithmetic  64.9 us (9%)
  matrix products  55 us (8%)
  between operations  17.5 us (2%)
    ppermute x51, waiting for transfers between devices, to_near(): lax.ppermute(x, 'near', [(i, i ^ k) for i in range(lax.axis_size('near'))])  167 us
    ppermute x16, waiting for transfers between devices, step_group(): return lax.ppermute(x, 'group', route)  59.2 us
    ppermute x51, starting transfers between devices, to_near(): lax.ppermute(x, 'near', [(i, i ^ k) for i in range(lax.axis_size('near'))])  59.2 us
    dot_general x14, matrix products, dot(): lax.dot_general(left, right, (dims, ((), ())), preferred_element_type=F32)  51 us
    unnamed x416, local copies, waits for them, and re-layouts  43.4 us
    ppermute x16, starting transfers between devices, step_group(): return lax.ppermute(x, 'group', route)  43.1 us
    pallas_call x17, Pallas kernels, whole_call(): pl.pallas_call(kernel, grid=(1,), out_shape=out_shape, in_specs=[pl.Block...  35.5 us
    pallas_call x3, Pallas kernels, chunk_call(): pl.pallas_call(kernel, grid=(chunks,), in_specs=in_specs, out_specs=out_s...  28.8 us
  transfers between devices with their start and end apart: 102, of which 43 were waited for; matrix products, arithmetic and copies ran while one was open for 20% of the time, Pallas kernels for 12%

profile of v3, /device:TPU:0, one launch (start us, length us, event | category | flops | bytes accessed | tf_op | source)
XLA Modules:
  0.0 694.0 jit_solution(1118041271291590084)
XLA Ops:
  15.3 8.4 %all-to-all-start = ((bf16[16,136,512]{2,1,0:T(8,128)(2,1)}), bf16[16,136,512]{2,1,0:T(8,128)(2,1)}, u32[]{:S(2)}, u32[]{:S(2)}) async-start(bf16[16,136,512]{2,1,0:T(8,128)(2,1)} %bitcast.15), calls=%async_computation | async-start | bytes 4456448 | tf_op jit(solution)/shard_map/all_to_all | solution.py:96
  42.7 18.1 %collective-permute-done.2.refs_3_ = bf16[128,2048]{1,0:T(8,128)(2,1)} collective-permute-done((bf16[128,2048]{1,0:T(8,128)(2,1)S(1)}, bf16[128,2048]{1,0:T(8,128)(2,1)}, u32[]{:S(2)}, u32[]{:S(2)}) %collective-permute-start.2) | collective-permute-done | bytes 524320 | tf_op jit(solution)/shard_map/ppermute | solution.py:35
  60.8 11.6 %collective-permute-done.1.refs_2_ = bf16[128,2048]{1,0:T(8,128)(2,1)} collective-permute-done((bf16[128,2048]{1,0:T(8,128)(2,1)S(1)}, bf16[128,2048]{1,0:T(8,128)(2,1)}, u32[]{:S(2)}, u32[]{:S(2)}) %collective-permute-start.1) | collective-permute-done | bytes 524320 | tf_op jit(solution)/shard_map/ppermute | solution.py:35
  95.0 6.6 collective-permute-start.20
  123.2 6.5 collective-permute-done.19
  129.7 7.5 %collective-permute-start.21 = (bf16[64,1024]{1,0:T(8,128)(2,1)}, bf16[64,1024]{1,0:T(8,128)(2,1)S(1)}, u32[]{:S(2)}, u32[]{:S(2)}) collective-permute-start(bf16[64,1024]{1,0:T(8,128)(2,1)} %pad_maximum_fusion.17), channel_id=1, source_target_pairs={{0,24},{1,25},{2,26},{3,27},{4,28},{5,29},{6,30},{7,31}} | collective-permute-start | bytes 393224 | tf_op jit(solution)/shard_map/ppermute | solution.py:46
  184.2 7.9 %shard_map.402 = (f32[1024,384]{1,0:T(8,128)S(1)}, f32[4,256,384]{2,1,0:T(8,128)S(1)}) custom-call(f32[1024,384]{1,0:T(8,128)S(1)} %get-tuple-element.212.x, f32[8,1024]{1,0:T(8,128)S(1)} %get-tuple-element.505.dt, f32[1024,8]{1,0:T(8,128)S(1)} %copy.126.cum, f32[8,1024]{1,0:T(8,128)S(1)} %reshape_reshape.3.cum_t, ...), custom_call_target="tpu_custom_call" | custom-call | tf_op jit(solution)/shard_map/pallas_call | solution.py:558
  195.2 6.7 collective-permute-start.31
  220.5 8.5 %collective-permute-done.29 = bf16[272,384]{1,0:T(8,128)(2,1)} collective-permute-done((bf16[272,384]{1,0:T(8,128)(2,1)}, bf16[272,384]{1,0:T(8,128)(2,1)}, u32[]{:S(2)}, u32[]{:S(2)}) %collective-permute-start.29) | collective-permute-done | bytes 208928 | tf_op jit(solution)/shard_map/ppermute | solution.py:46
  251.1 9.5 %collective-permute-done.36 = bf16[128,2048]{1,0:T(8,128)(2,1)S(1)} collective-permute-done((bf16[128,2048]{1,0:T(8,128)(2,1)S(1)}, bf16[128,2048]{1,0:T(8,128)(2,1)S(1)}, u32[]{:S(2)}, u32[]{:S(2)}) %collective-permute-start.36) | collective-permute-done | bytes 524320 | tf_op jit(solution)/shard_map/ppermute | solution.py:35
  261.2 10.4 %collective-permute-done.38 = bf16[128,2048]{1,0:T(8,128)(2,1)S(1)} collective-permute-done((bf16[128,2048]{1,0:T(8,128)(2,1)S(1)}, bf16[128,2048]{1,0:T(8,128)(2,1)S(1)}, u32[]{:S(2)}, u32[]{:S(2)}) %collective-permute-start.38) | collective-permute-done | bytes 524320 | tf_op jit(solution)/shard_map/ppermute | solution.py:35
  276.4 12.3 %collective-permute-done.41.refs_3_ = bf16[128,2048]{1,0:T(8,128)(2,1)S(1)} collective-permute-done((bf16[128,2048]{1,0:T(8,128)(2,1)S(1)}, bf16[128,2048]{1,0:T(8,128)(2,1)S(1)}, u32[]{:S(2)}, u32[]{:S(2)}) %collective-permute-start.41) | collective-permute-done | bytes 524320 | tf_op jit(solution)/shard_map/ppermute | solution.py:35
  288.7 9.5 %collective-permute-done.40.refs_2_ = bf16[128,2048]{1,0:T(8,128)(2,1)S(1)} collective-permute-done((bf16[128,2048]{1,0:T(8,128)(2,1)S(1)}, bf16[128,2048]{1,0:T(8,128)(2,1)S(1)}, u32[]{:S(2)}, u32[]{:S(2)}) %collective-permute-start.40) | collective-permute-done | bytes 524320 | tf_op jit(solution)/shard_map/ppermute | solution.py:35
  307.7 7.9 %fusion = f32[1024,1024]{1,0:T(8,128)S(1)} fusion(bf16[1024,2048]{1,0:T(8,128)(2,1)} %bitcast.301, bf16[2048,1536]{1,0:T(8,128)(2,1)} %all-gather.5.cloned.1.call-done.refs_1_), kind=kOutput, calls=%fused_computation | convolution fusion | flops 4294967296 | bytes 12582912 | tf_op jit(solution)/shard_map/dot_general | solution.py:243
  334.1 6.6 convolution_convert_fusion
  345.6 12.0 %collective-permute-done.48 = bf16[128,2048]{1,0:T(8,128)(2,1)} collective-permute-done((bf16[128,2048]{1,0:T(8,128)(2,1)}, bf16[128,2048]{1,0:T(8,128)(2,1)}, u32[]{:S(2)}, u32[]{:S(2)}) %collective-permute-start.48) | collective-permute-done | bytes 524320 | tf_op jit(solution)/shard_map/ppermute | solution.py:35
  365.6 12.6 %collective-permute-done.52.refs_3_ = bf16[128,2048]{1,0:T(8,128)(2,1)} collective-permute-done((bf16[128,2048]{1,0:T(8,128)(2,1)}, bf16[128,2048]{1,0:T(8,128)(2,1)}, u32[]{:S(2)}, u32[]{:S(2)}) %collective-permute-start.52) | collective-permute-done | bytes 524320 | tf_op jit(solution)/shard_map/ppermute | solution.py:35
  378.2 9.4 %collective-permute-done.51.refs_2_ = bf16[128,2048]{1,0:T(8,128)(2,1)} collective-permute-done((bf16[128,2048]{1,0:T(8,128)(2,1)}, bf16[128,2048]{1,0:T(8,128)(2,1)}, u32[]{:S(2)}, u32[]{:S(2)}) %collective-permute-start.51) | collective-permute-done | bytes 524320 | tf_op jit(solution)/shard_map/ppermute | solution.py:35
  428.7 16.0 %collective-permute-done.58 = bf16[272,384]{1,0:T(8,128)(2,1)} collective-permute-done((bf16[272,384]{1,0:T(8,128)(2,1)}, bf16[272,384]{1,0:T(8,128)(2,1)}, u32[]{:S(2)}, u32[]{:S(2)}) %collective-permute-start.58) | collective-permute-done | bytes 208928 | tf_op jit(solution)/shard_map/ppermute | solution.py:46
  444.7 13.3 %collective-permute-done.57 = bf16[272,384]{1,0:T(8,128)(2,1)} collective-permute-done((bf16[272,384]{1,0:T(8,128)(2,1)}, bf16[272,384]{1,0:T(8,128)(2,1)}, u32[]{:S(2)}, u32[]{:S(2)}) %collective-permute-start.57) | collective-permute-done | bytes 208928 | tf_op jit(solution)/shard_map/ppermute | solution.py:46
  464.9 10.2 %shard_map.413 = bf16[2048,1536]{1,0:T(8,128)(2,1)} custom-call(bf16[1024,2048]{1,0:T(8,128)(2,1)S(1)} %bitcast.294, bf16[1024,2048]{1,0:T(8,128)(2,1)S(1)} %bitcast.292, bf16[1024,2048]{1,0:T(8,128)(2,1)} %bitcast.286, bf16[1024,512]{1,0:T(8,128)(2,1)S(1)} %copy-done.35, bf16[1024,512]{1,0:T(8,128)(2,1)S(1)} %copy-done.33, ...), custom_call_target="tpu_custom_call" | custom-call | tf_op jit(solution)/shard_map/pallas_call | solution.py:203
  496.8 6.9 collective-permute-done.67
  507.4 12.3 %shard_map.415 = (f32[1024,384]{1,0:T(8,128)S(1)}, f32[256,1024]{1,0:T(8,128)S(1)}, bf16[256,1024]{1,0:T(8,128)(2,1)S(1)}) custom-call(f32[1024,384]{1,0:T(8,128)S(1)} %get-tuple-element.212.x, f32[8,1024]{1,0:T(8,128)S(1)} %copy-done.54, f32[1024,8]{1,0:T(8,128)S(1)} %copy-done.30, f32[8,1024]{1,0:T(8,128)S(1)} %reshape_reshape.3.cum_t, ...), custom_call_target="tpu_custom_call" | custom-call | tf_op jit(solution)/shard_map/pallas_call | solution.py:558
  529.5 8.6 %shard_map.416 = (f32[1024,384]{1,0:T(8,128)S(1)}, bf16[256,1024]{1,0:T(8,128)(2,1)S(1)}, f32[8,1024]{1,0:T(8,128)S(1)}, f32[8,1024]{1,0:T(8,128)S(1)}, f32[1,384]{1,0:T(1,128)S(1)}) custom-call(f32[1024,384]{1,0:T(8,128)S(1)} %get-tuple-element.212.x, f32[1024,384]{1,0:T(8,128)S(1)} %copy-done.26, f32[8,1024]{1,0:T(8,128)S(1)} %copy-done.54, ...), custom_call_target="tpu_custom_call" | custom-call | tf_op jit(solution)/shard_map/pallas_call | solution.py:558
  558.3 6.9 multiply_reduce_fusion.3
  565.2 8.1 %collective-permute-done.78 = f32[64,3]{1,0:T(8,128)S(1)} collective-permute-done((f32[64,3]{1,0:T(8,128)S(1)}, f32[64,3]{1,0:T(8,128)S(1)}, u32[]{:S(2)}, u32[]{:S(2)}) %collective-permute-start.78) | collective-permute-done | bytes 800 | tf_op jit(solution)/shard_map/ppermute | solution.py:46
  580.1 6.8 shard_map.417
  600.1 6.9 %collective-permute-start.87 = (bf16[512,512]{1,0:T(8,128)(2,1)}, bf16[512,512]{1,0:T(8,128)(2,1)}, u32[]{:S(2)}, u32[]{:S(2)}) collective-permute-start(bf16[512,512]{1,0:T(8,128)(2,1)} %get-tuple-element.446), channel_id=1, source_target_pairs={{0,16},{8,24},{16,0},{24,8},{1,17},{9,25},{17,1},{25,9},{2,18},{10... | collective-permute-start | bytes 1572872 | tf_op jit(solution)/shard_map/ppermute | solution.py:40
  614.8 7.1 %collective-permute-done.80 = bf16[128,2048]{1,0:T(8,128)(2,1)S(1)} collective-permute-done((bf16[128,2048]{1,0:T(8,128)(2,1)S(1)}, bf16[128,2048]{1,0:T(8,128)(2,1)S(1)}, u32[]{:S(2)}, u32[]{:S(2)}) %collective-permute-start.80) | collective-permute-done | bytes 524320 | tf_op jit(solution)/shard_map/ppermute | solution.py:35
  622.6 9.3 %collective-permute-done.81 = bf16[128,2048]{1,0:T(8,128)(2,1)S(1)} collective-permute-done((bf16[128,2048]{1,0:T(8,128)(2,1)S(1)}, bf16[128,2048]{1,0:T(8,128)(2,1)S(1)}, u32[]{:S(2)}, u32[]{:S(2)}) %collective-permute-start.81) | collective-permute-done | bytes 524320 | tf_op jit(solution)/shard_map/ppermute | solution.py:35
  647.3 9.4 %collective-permute-done.87 = bf16[512,512]{1,0:T(8,128)(2,1)} collective-permute-done((bf16[512,512]{1,0:T(8,128)(2,1)}, bf16[512,512]{1,0:T(8,128)(2,1)}, u32[]{:S(2)}, u32[]{:S(2)}) %collective-permute-start.87) | collective-permute-done | bytes 524320 | tf_op jit(solution)/shard_map/ppermute | solution.py:40
  656.7 7.4 %collective-permute-done.90.refs_2_ = bf16[128,1536]{1,0:T(8,128)(2,1)S(1)} collective-permute-done((bf16[128,1536]{1,0:T(8,128)(2,1)S(1)}, bf16[128,1536]{1,0:T(8,128)(2,1)S(1)}, u32[]{:S(2)}, u32[]{:S(2)}) %collective-permute-start.90) | collective-permute-done | bytes 393248 | tf_op jit(solution)/shard_map/ppermute | solution.py:35
  (852 shorter events, 375.3 us)
Async XLA Ops:
  15.3 63.9 %all-to-all-start = ((bf16[16,136,512]{2,1,0:T(8,128)(2,1)}), bf16[16,136,512]{2,1,0:T(8,128)(2,1)}, u32[]{:S(2)}, u32[]{:S(2)}) async-start(bf16[16,136,512]{2,1,0:T(8,128)(2,1)} %bitcast.15), calls=%async_computation | async-start | bytes 4456448 | tf_op jit(solution)/shard_map/all_to_all | solution.py:96
  23.7 180.2 %all-gather.3.cloned.1.call-start = ((), (), s32[]{:S(2)}) async-start(), calls=%async_computation.4 | async-start | bytes 5242880 | tf_op jit(solution)/shard_map/all_gather | solution.py:947
  26.0 56.8 %collective-permute-start.3 = (bf16[128,2048]{1,0:T(8,128)(2,1)S(1)}, bf16[128,2048]{1,0:T(8,128)(2,1)S(1)}, u32[]{:S(2)}, u32[]{:S(2)}) collective-permute-start(bf16[128,2048]{1,0:T(8,128)(2,1)S(1)} %get-tuple-element.439.refs_0_), channel_id=1, source_target_pairs={{0,1},{1,0},{2,3},{3,2},{4,5},{5,4},{6,7},{7,6},{8,9},{9,8},{10,11... | collective-permute-start | bytes 1572872 | tf_op jit(solution)/shard_map/ppermute | solution.py:31
  26.0 34.8 %collective-permute-start.2 = (bf16[128,2048]{1,0:T(8,128)(2,1)S(1)}, bf16[128,2048]{1,0:T(8,128)(2,1)}, u32[]{:S(2)}, u32[]{:S(2)}) collective-permute-start(bf16[128,2048]{1,0:T(8,128)(2,1)S(1)} %get-tuple-element.439.refs_0_), channel_id=1, source_target_pairs={{0,6},{2,4},{4,2},{6,0},{1,7},{3,5},{5,3},{7,1},{8,14},{10,12},{12... | collective-permute-start | bytes 1572872 | tf_op jit(solution)/shard_map/ppermute | solution.py:35
  28.8 43.6 %collective-permute-start.1 = (bf16[128,2048]{1,0:T(8,128)(2,1)S(1)}, bf16[128,2048]{1,0:T(8,128)(2,1)}, u32[]{:S(2)}, u32[]{:S(2)}) collective-permute-start(bf16[128,2048]{1,0:T(8,128)(2,1)S(1)} %get-tuple-element.439.refs_0_), channel_id=1, source_target_pairs={{0,4},{2,6},{4,0},{6,2},{1,5},{3,7},{5,1},{7,3},{8,12},{10,14},{12... | collective-permute-start | bytes 1572872 | tf_op jit(solution)/shard_map/ppermute | solution.py:35
  29.4 49.4 %collective-permute-start = (bf16[128,2048]{1,0:T(8,128)(2,1)S(1)}, bf16[128,2048]{1,0:T(8,128)(2,1)}, u32[]{:S(2)}, u32[]{:S(2)}) collective-permute-start(bf16[128,2048]{1,0:T(8,128)(2,1)S(1)} %get-tuple-element.439.refs_0_), channel_id=1, source_target_pairs={{0,2},{2,0},{4,6},{6,4},{1,3},{3,1},{5,7},{7,5},{8,10},{10,8},{12,... | collective-permute-start | bytes 1572872 | tf_op jit(solution)/shard_map/ppermute | solution.py:35
  31.1 59.2 %collective-permute-start.14 = (bf16[128,1024]{1,0:T(8,128)(2,1)}, bf16[128,1024]{1,0:T(8,128)(2,1)}, u32[]{:S(2)}, u32[]{:S(2)}) collective-permute-start(bf16[128,1024]{1,0:T(8,128)(2,1)} %get-tuple-element.473), channel_id=1, source_target_pairs={{0,6},{2,4},{4,2},{6,0},{1,7},{3,5},{5,3},{7,1},{8,14},{10,12},{12... | collective-permute-start | bytes 786440 | tf_op jit(solution)/shard_map/ppermute | solution.py:35
  93.7 214.0 %all-gather.5.cloned.1.call-start = ((), (), s32[]{:S(2)}) async-start(), calls=%async_computation.5 | async-start | bytes 7864320 | tf_op jit(solution)/shard_map/all_gather | solution.py:978
  95.0 26.1 %collective-permute-start.20 = (bf16[64,1024]{1,0:T(8,128)(2,1)}, bf16[64,1024]{1,0:T(8,128)(2,1)}, u32[]{:S(2)}, u32[]{:S(2)}) collective-permute-start(bf16[64,1024]{1,0:T(8,128)(2,1)} %pad_maximum_fusion.17), channel_id=1, source_target_pairs={{0,16},{8,24},{1,17},{9,25},{2,18},{10,26},{3,19},{11,27},{4,20},{... | collective-permute-start | bytes 393224 | tf_op jit(solution)/shard_map/ppermute | solution.py:46
  101.6 43.4 %collective-permute-start.25 = (bf16[128,2048]{1,0:T(8,128)(2,1)S(1)}, bf16[128,2048]{1,0:T(8,128)(2,1)S(1)}, u32[]{:S(2)}, u32[]{:S(2)}) collective-permute-start(bf16[128,2048]{1,0:T(8,128)(2,1)S(1)} %constant_dynamic-slice_fusion.4.refs_0_), channel_id=1, source_target_pairs={{0,1},{1,0},{2,3},{3,2},{4,5},{5,4},{6,7},{7,6},{8,9},{9,8},{10,11... | collective-permute-start | bytes 1572872 | tf_op jit(solution)/shard_map/ppermute | solution.py:31
  103.4 43.4 %collective-permute-start.23 = (bf16[128,2048]{1,0:T(8,128)(2,1)S(1)}, bf16[128,2048]{1,0:T(8,128)(2,1)}, u32[]{:S(2)}, u32[]{:S(2)}) collective-permute-start(bf16[128,2048]{1,0:T(8,128)(2,1)S(1)} %constant_dynamic-slice_fusion.4.refs_0_), channel_id=1, source_target_pairs={{0,4},{2,6},{4,0},{6,2},{1,5},{3,7},{5,1},{7,3},{8,12},{10,14},{12... | collective-permute-start | bytes 1572872 | tf_op jit(solution)/shard_map/ppermute | solution.py:35
  119.5 27.3 %collective-permute-start.22 = (bf16[128,2048]{1,0:T(8,128)(2,1)S(1)}, bf16[128,2048]{1,0:T(8,128)(2,1)}, u32[]{:S(2)}, u32[]{:S(2)}) collective-permute-start(bf16[128,2048]{1,0:T(8,128)(2,1)S(1)} %constant_dynamic-slice_fusion.4.refs_0_), channel_id=1, source_target_pairs={{0,2},{2,0},{4,6},{6,4},{1,3},{3,1},{5,7},{7,5},{8,10},{10,8},{12,... | collective-permute-start | bytes 1572872 | tf_op jit(solution)/shard_map/ppermute | solution.py:35
  119.8 27.1 %collective-permute-start.28 = (bf16[128,2048]{1,0:T(8,128)(2,1)}, bf16[128,2048]{1,0:T(8,128)(2,1)S(1)}, u32[]{:S(2)}, u32[]{:S(2)}) collective-permute-start(bf16[128,2048]{1,0:T(8,128)(2,1)} %collective-permute-done.24.refs_3_), channel_id=1, source_target_pairs={{0,1},{1,0},{2,3},{3,2},{4,5},{5,4},{6,7},{7,6},{8,9},{9,8},{10,11... | collective-permute-start | bytes 1572872 | tf_op jit(solution)/shard_map/ppermute | solution.py:31
  164.7 327.4 %reduce-scatter.3.cloned.1.call-start = ((), (), s32[]{:S(2)}) async-start(), calls=%async_computation.6 | async-start | bytes 5242880 | tf_op jit(solution)/shard_map/reduce_scatter | solution.py:1031
  179.5 33.3 %collective-permute-start.34 = (bf16[256,1024]{1,0:T(8,128)(2,1)}, bf16[256,1024]{1,0:T(8,128)(2,1)}, u32[]{:S(2)}, u32[]{:S(2)}) collective-permute-start(bf16[256,1024]{1,0:T(8,128)(2,1)} %pad_maximum_fusion.10.refs_0_), channel_id=1, source_target_pairs={{0,6},{2,4},{4,2},{6,0},{1,7},{3,5},{5,3},{7,1},{8,14},{10,12},{12... | collective-permute-start | bytes 1572872 | tf_op jit(solution)/shard_map/ppermute | solution.py:35
  180.7 35.7 %collective-permute-start.33 = (bf16[256,1024]{1,0:T(8,128)(2,1)}, bf16[256,1024]{1,0:T(8,128)(2,1)}, u32[]{:S(2)}, u32[]{:S(2)}) collective-permute-start(bf16[256,1024]{1,0:T(8,128)(2,1)} %pad_maximum_fusion.10.refs_0_), channel_id=1, source_target_pairs={{0,4},{2,6},{4,0},{6,2},{1,5},{3,7},{5,1},{7,3},{8,12},{10,14},{12... | collective-permute-start | bytes 1572872 | tf_op jit(solution)/shard_map/ppermute | solution.py:35
  182.0 34.5 %collective-permute-start.32 = (bf16[256,1024]{1,0:T(8,128)(2,1)}, bf16[256,1024]{1,0:T(8,128)(2,1)}, u32[]{:S(2)}, u32[]{:S(2)}) collective-permute-start(bf16[256,1024]{1,0:T(8,128)(2,1)} %pad_maximum_fusion.10.refs_0_), channel_id=1, source_target_pairs={{0,2},{2,0},{4,6},{6,4},{1,3},{3,1},{5,7},{7,5},{8,10},{10,8},{12,... | collective-permute-start | bytes 1572872 | tf_op jit(solution)/shard_map/ppermute | solution.py:35
  357.7 282.2 %reduce-scatter.5.cloned.1.call-start = ((), (), s32[]{:S(2)}) async-start(), calls=%async_computation.7 | async-start | bytes 7864320 | tf_op jit(solution)/shard_map/reduce_scatter | solution.py:1031
  365.6 25.8 %collective-permute-start.53 = (bf16[128,2048]{1,0:T(8,128)(2,1)}, bf16[128,2048]{1,0:T(8,128)(2,1)}, u32[]{:S(2)}, u32[]{:S(2)}) collective-permute-start(bf16[128,2048]{1,0:T(8,128)(2,1)} %fusion.82.refs_0_), channel_id=1, source_target_pairs={{0,1},{1,0},{2,3},{3,2},{4,5},{5,4},{6,7},{7,6},{8,9},{9,8},{10,11... | collective-permute-start | bytes 1572872 | tf_op jit(solution)/shard_map/ppermute | solution.py:31
  404.2 40.5 %collective-permute-start.58 = (bf16[272,384]{1,0:T(8,128)(2,1)}, bf16[272,384]{1,0:T(8,128)(2,1)}, u32[]{:S(2)}, u32[]{:S(2)}) collective-permute-start(bf16[272,384]{1,0:T(8,128)(2,1)} %pad_maximum_fusion.11), channel_id=1, source_target_pairs={{16,0},{24,8},{17,1},{25,9},{18,2},{26,10},{19,3},{27,11},{20,4},{... | collective-permute-start | bytes 626696 | tf_op jit(solution)/shard_map/ppermute | solution.py:46
  421.2 53.9 %collective-permute-start.60 = (bf16[256,1024]{1,0:T(8,128)(2,1)}, bf16[256,1024]{1,0:T(8,128)(2,1)}, u32[]{:S(2)}, u32[]{:S(2)}) collective-permute-start(bf16[256,1024]{1,0:T(8,128)(2,1)} %copy-done.92), channel_id=1, source_target_pairs={{0,2},{2,0},{4,6},{6,4},{1,3},{3,1},{5,7},{7,5},{8,10},{10,8},{12,... | collective-permute-start | bytes 1572872 | tf_op jit(solution)/shard_map/ppermute | solution.py:35
  422.7 52.5 %collective-permute-start.61 = (bf16[256,1024]{1,0:T(8,128)(2,1)}, bf16[256,1024]{1,0:T(8,128)(2,1)}, u32[]{:S(2)}, u32[]{:S(2)}) collective-permute-start(bf16[256,1024]{1,0:T(8,128)(2,1)} %copy-done.91), channel_id=1, source_target_pairs={{0,4},{2,6},{4,0},{6,2},{1,5},{3,7},{5,1},{7,3},{8,12},{10,14},{12... | collective-permute-start | bytes 1572872 | tf_op jit(solution)/shard_map/ppermute | solution.py:35
  423.3 51.9 %collective-permute-start.62 = (bf16[256,1024]{1,0:T(8,128)(2,1)}, bf16[256,1024]{1,0:T(8,128)(2,1)}, u32[]{:S(2)}, u32[]{:S(2)}) collective-permute-start(bf16[256,1024]{1,0:T(8,128)(2,1)} %copy-done.90), channel_id=1, source_target_pairs={{0,6},{2,4},{4,2},{6,0},{1,7},{3,5},{5,3},{7,1},{8,14},{10,12},{12... | collective-permute-start | bytes 1572872 | tf_op jit(solution)/shard_map/ppermute | solution.py:35
  424.9 33.1 %collective-permute-start.57 = (bf16[272,384]{1,0:T(8,128)(2,1)}, bf16[272,384]{1,0:T(8,128)(2,1)}, u32[]{:S(2)}, u32[]{:S(2)}) collective-permute-start(bf16[272,384]{1,0:T(8,128)(2,1)} %pad_maximum_fusion.11), channel_id=1, source_target_pairs={{8,0},{16,8},{24,16},{9,1},{17,9},{25,17},{10,2},{18,10},{26,18},{... | collective-permute-start | bytes 626696 | tf_op jit(solution)/shard_map/ppermute | solution.py:46
  489.8 32.0 %collective-permute-start.68 = (bf16[128,2048]{1,0:T(8,128)(2,1)}, bf16[128,2048]{1,0:T(8,128)(2,1)}, u32[]{:S(2)}, u32[]{:S(2)}) collective-permute-start(bf16[128,2048]{1,0:T(8,128)(2,1)} %get-tuple-element.290), channel_id=1, source_target_pairs={{0,4},{2,6},{4,0},{6,2},{1,5},{3,7},{5,1},{7,3},{8,12},{10,14},{12... | collective-permute-start | bytes 1572872 | tf_op jit(solution)/shard_map/ppermute | solution.py:35
  490.9 32.1 %collective-permute-start.69 = (bf16[128,2048]{1,0:T(8,128)(2,1)}, bf16[128,2048]{1,0:T(8,128)(2,1)}, u32[]{:S(2)}, u32[]{:S(2)}) collective-permute-start(bf16[128,2048]{1,0:T(8,128)(2,1)} %get-tuple-element.291), channel_id=1, source_target_pairs={{0,6},{2,4},{4,2},{6,0},{1,7},{3,5},{5,3},{7,1},{8,14},{10,12},{12... | collective-permute-start | bytes 1572872 | tf_op jit(solution)/shard_map/ppermute | solution.py:35
  494.3 30.1 %collective-permute-start.66 = (bf16[128,1024]{1,0:T(8,128)(2,1)S(1)}, bf16[128,1024]{1,0:T(8,128)(2,1)S(1)}, u32[]{:S(2)}, u32[]{:S(2)}) collective-permute-start(bf16[128,1024]{1,0:T(8,128)(2,1)S(1)} %get-tuple-element.463), channel_id=1, source_target_pairs={{0,6},{2,4},{4,2},{6,0},{1,7},{3,5},{5,3},{7,1},{8,14},{10,12},{12... | collective-permute-start | bytes 786440 | tf_op jit(solution)/shard_map/ppermute | solution.py:35
  496.0 30.1 %collective-permute-start.65 = (bf16[128,1024]{1,0:T(8,128)(2,1)S(1)}, bf16[128,1024]{1,0:T(8,128)(2,1)S(1)}, u32[]{:S(2)}, u32[]{:S(2)}) collective-permute-start(bf16[128,1024]{1,0:T(8,128)(2,1)S(1)} %get-tuple-element.464), channel_id=1, source_target_pairs={{0,4},{2,6},{4,0},{6,2},{1,5},{3,7},{5,1},{7,3},{8,12},{10,14},{12... | collective-permute-start | bytes 786440 | tf_op jit(solution)/shard_map/ppermute | solution.py:35
  599.4 44.8 %collective-permute-start.88 = (bf16[512,512]{1,0:T(8,128)(2,1)}, bf16[512,512]{1,0:T(8,128)(2,1)}, u32[]{:S(2)}, u32[]{:S(2)}) collective-permute-start(bf16[512,512]{1,0:T(8,128)(2,1)} %get-tuple-element.445), channel_id=1, source_target_pairs={{0,24},{8,0},{16,8},{24,16},{1,25},{9,1},{17,9},{25,17},{2,26},{10... | collective-permute-start | bytes 1572872 | tf_op jit(solution)/shard_map/ppermute | solution.py:40
  600.1 56.6 %collective-permute-start.87 = (bf16[512,512]{1,0:T(8,128)(2,1)}, bf16[512,512]{1,0:T(8,128)(2,1)}, u32[]{:S(2)}, u32[]{:S(2)}) collective-permute-start(bf16[512,512]{1,0:T(8,128)(2,1)} %get-tuple-element.446), channel_id=1, source_target_pairs={{0,16},{8,24},{16,0},{24,8},{1,17},{9,25},{17,1},{25,9},{2,18},{10... | collective-permute-start | bytes 1572872 | tf_op jit(solution)/shard_map/ppermute | solution.py:40
  621.9 34.8 %collective-permute-start.86 = (bf16[512,512]{1,0:T(8,128)(2,1)}, bf16[512,512]{1,0:T(8,128)(2,1)}, u32[]{:S(2)}, u32[]{:S(2)}) collective-permute-start(bf16[512,512]{1,0:T(8,128)(2,1)} %get-tuple-element.447), channel_id=1, source_target_pairs={{0,8},{8,16},{16,24},{24,0},{1,9},{9,17},{17,25},{25,1},{2,10},{10... | collective-permute-start | bytes 1572872 | tf_op jit(solution)/shard_map/ppermute | solution.py:40
  636.2 37.5 %all-to-all-start.1 = ((f32[16,32,128]{2,1,0:T(8,128)}), f32[16,32,128]{2,1,0:T(8,128)S(1)}, u32[]{:S(2)}, u32[]{:S(2)}) async-start(f32[16,32,128]{2,1,0:T(8,128)} %bitcast.163), calls=%async_computation.2 | async-start | bytes 524288 | tf_op jit(solution)/shard_map/all_to_all | solution.py:96
  (271 other events, 2995.3 us)
Sparse Core Ops, SparseCore 0:
  93.8 84.3 all-gather.2
  179.8 127.8 all-gather.4
  357.8 101.1 reduce-scatter.2
  478.3 121.0 reduce-scatter.4

commit v4 on v3

--- a/solution.py
+++ b/solution.py
@@ -106,18 +106,31 @@
     return lax.dynamic_slice_in_dim(x, lax.axis_index("head") * half, half, 0)
 
 
-def tokens_kernel(gained, index, *refs):
+def normalized(value, gain):
+    value = value.astype(F32)
+    power = jnp.mean(value * value, 1, keepdims=True)
+    return (value * lax.rsqrt(power + EPS) * gain).astype(B16)
+
+
+def tokens_kernel(index, *refs):
     *refs, out = refs
-    gain = refs.pop()[...] if gained else None
     count = len(refs) // 2
     for k in range(count):
         for side in range(2):
-            value = refs[k + side * count][...]
-            if gained:
-                value = value.astype(F32)
-                power = jnp.mean(value * value, 1, keepdims=True)
-                value = (value * lax.rsqrt(power + EPS) * gain).astype(B16)
-            out[index[k], index[count + side]] = value
+            out[index[k], index[count + side]] = refs[k + side * count][...]
+
+
+def normed_kernel(index, *refs):
+    *refs, gain, out, halo = refs
+    count, rows = len(refs) // 2, out.shape[2]
+    for k in range(count):
+        for side in range(2):
+            value = refs[k + side * count][:rows]
+            out[index[k], index[count + side]] = normalized(value, gain[...])
+
+        @pl.when(index[k] == count - 1)
+        def _():
+            halo[...] = normalized(refs[k][rows:], gain[...])
 
 
 def sent_tokens(mine):
@@ -125,16 +138,25 @@
     return [*got, *map(swap_cores, got)]
 
 
-def placed_tokens(parts, gain=None):
-    core, places = lax.axis_index("head"), near_places()
+def tokens_index():
+    core = lax.axis_index("head")
+    return jnp.stack([*near_places(), core, 1 - core]).astype(jnp.int32)
+
+
+def placed_tokens(parts):
     rows, width = parts[0].shape
-    index = jnp.stack([*places, core, 1 - core]).astype(jnp.int32)
-    operands = [index, *parts]
-    if gain is not None:
-        operands.append(gain[None, :])
-    shape = jax.ShapeDtypeStruct((len(places), 2, rows, width), parts[0].dtype)
-    kernel = functools.partial(tokens_kernel, gain is not None)
-    return whole_call(kernel, shape, [], *operands).reshape(-1, width)
+    shape = jax.ShapeDtypeStruct((len(parts) // 2, 2, rows, width), parts[0].dtype)
+    return whole_call(tokens_kernel, shape, [], tokens_index(), *parts).reshape(-1, width)
+
+
+def normed_tokens(parts, gain, more):
+    rows, width = parts[0].shape[0] - more, parts[0].shape[1]
+    shapes = [
+        jax.ShapeDtypeStruct((len(parts) // 2, 2, rows, width), B16),
+        jax.ShapeDtypeStruct((more, width), B16),
+    ]
+    out, halo = whole_call(normed_kernel, shapes, [], tokens_index(), *parts, gain[None, :])
+    return out.reshape(-1, width), halo
 
 
 def gather_tokens(mine):
@@ -282,17 +304,23 @@
     return total
 
 
-def conv_back(grad, grad_edge, inputs, edge, weight, dim):
-    length = inputs.shape[dim]
-    padded = jnp.concatenate([edge, inputs], dim)
+def conv_back(grad, grad_edge, weight, dim):
+    length = grad.shape[dim]
     late = jnp.concatenate([grad, grad_edge], dim)
     total = 0.0
-    taps = []
     for tap in range(CONV):
         back = CONV - 1 - tap
         total = total + weight[tap] * lax.slice_in_dim(late, back, back + length, axis=dim)
+    return total
+
+
+def taps_back(grad, inputs, edge, dim):
+    length = inputs.shape[dim]
+    padded = jnp.concatenate([edge, inputs], dim)
+    taps = []
+    for tap in range(CONV):
         taps.append(jnp.sum(grad * lax.slice_in_dim(padded, tap, tap + length, axis=dim), dim))
-    return total, jnp.stack(taps), jnp.sum(grad, dim)
+    return jnp.stack(taps), jnp.sum(grad, dim)
 
 
 def silu_slope(v):
@@ -891,12 +919,15 @@
     extra = jnp.concatenate([extra, w_dt.T.reshape(near, n_dt)], 1)
     extra = jnp.pad(extra, ((0, 0), (0, -extra.shape[1] % (8 * pack1.shape[2]))))
     pack1 = jnp.concatenate([pack1, extra.reshape(near, -1, pack1.shape[2])], 1)
+    halo = step_group(tokens[rows - 16 :], 1)
+    pack1 = after(pack1, halo)
     full1 = jnp.broadcast_to(pack1, (groups, *pack1.shape)).reshape(devices, *pack1.shape[1:])
     full1 = trade_all(full1)
-    token_parts = sent_tokens(own_half(tokens))
+    token_parts = sent_tokens(jnp.concatenate([own_half(tokens), halo], 0))
     pack2 = [columns(w_z), columns(w_out.T), columns(w_q), columns(w_o.T)]
     pack2 = jnp.concatenate(pack2, 2)
     pack3 = jnp.concatenate([columns(w_gate), columns(w_up), columns(w_down.T)], 2)
+    pack2, *token_parts[:near] = lax.optimization_barrier((pack2, *token_parts[:near]))
     sent2 = sent_near(pack2)
     positions = (group * span + jnp.arange(span)).astype(F32)
     half = HEAD_DIM // 2
@@ -931,7 +962,9 @@
     bias_bc = smalls[:, -conv_bc_bias.shape[0] :].reshape(2, near, -1)[core, here][:, None]
     full1 = full1[:, :piece].reshape(width, -1)
     full_x, full_kvbc = full1[:, :inner], full1[:, inner:]
-    n1 = placed_tokens(token_parts, gain1)
+    n1, halo = normed_tokens(token_parts, gain1, 16)
+    edge = dot(halo, full1)[17 - CONV :]
+    x_edge, bc_edge = edge[:, :inner], edge[:, inner + 2 * key_cols :].T
     grad_parts = sent_tokens(after(own_half(cotangent), n1))
 
     kvbc = dot(full_kvbc, n1, ((0,), (1,)))
@@ -940,14 +973,12 @@
     kv = flat(kv)
     kv_parts = [kv] + [step_group(kv, r) for r in range(1, groups)]
     bc_proj = flat(kvbc[2 * key_cols :])
-    bc_edge = step_group(bc_proj[:, span - CONV + 1 :], 1)
     sent2, n1, kv = lax.optimization_barrier((sent2, n1, kv))
     full2 = placed(near_places(), sent2).reshape(near * piece, -1)
     n1_x, full2 = lax.optimization_barrier((n1, full2))
     full2 = lax.all_gather(full2, "group", axis=0, tiled=True)
 
     x_proj = dot(n1_x, full_x)
-    x_edge = step_group(x_proj[span - CONV + 1 :], 1)
     sent3 = sent_near(after(pack3, x_proj))
 
     bc_pre = conv(bc_proj, bc_edge, taps_bc, bias_bc, 1)
@@ -1108,10 +1139,8 @@
     grad_bcpre = grad_bc * silu_slope(bc_pre)
     next_x = step_group(grad_xpre[: CONV - 1], -1)
     next_bc = step_group(grad_bcpre[:, : CONV - 1], -1)
-    grad_x, grad_tapx, grad_biasx = conv_back(grad_xpre, next_x, x_proj, x_edge, taps_x, 0)
-    grad_bcp, grad_tapbc, grad_biasbc = conv_back(
-        grad_bcpre, next_bc, bc_proj, bc_edge, taps_bc, 1
-    )
+    grad_x = conv_back(grad_xpre, next_x, taps_x, 0)
+    grad_bcp = conv_back(grad_bcpre, next_bc, taps_bc, 1)
     grad_kv = added(after(grad_kv, grad_xpre))
     gk_first, gk_second = rotate_pair(
         grad_kv[:half_cols], grad_kv[half_cols:key_cols], cos_k, -sin_k
@@ -1136,10 +1165,17 @@
         (grad_dt_low.T, full_dt),
     ]
     partial1 = partial_tokens(width, pairs)
+    grad_xpre, grad_bcpre = after((grad_xpre, grad_bcpre), partial1)
+    grad_tapx, grad_biasx = taps_back(grad_xpre, x_proj, x_edge, 0)
+    grad_tapbc, grad_biasbc = taps_back(grad_bcpre, bc_proj, bc_edge, 1)
     output = (hidden + added(after(feed, partial1))).astype(B16)
     output = both_halves(output, swap_cores(output), 0)
     outs3 = homed(after(home3, partial1), (ff, True), (ff, True))
-    grad_n1, (sum_wgate, sum_wup, output) = scatter_tokens(partial1, alongside=(*outs3, output))
+    taps = grad_tapx, grad_biasx, grad_tapbc, grad_biasbc
+    grad_n1, (sum_wgate, sum_wup, output, taps) = scatter_tokens(
+        partial1, alongside=(*outs3, output, taps)
+    )
+    grad_tapx, grad_biasx, grad_tapbc, grad_biasbc = taps
     _, unit1, factor1 = normalize(my_tokens, gain1)
     grad_norm1, grad_g1 = norm_back(grad_n1, unit1, factor1, gain1)
     grad_tokens = grad_hidden + grad_norm1

time: 705 us -> 693 us (0.983)
  starting transfers between devices: 125 us -> 115 us
    ppermute x16 -> x15, waiting for transfers between devices: 59.2 us -> 44.9 us  [step_group(): return lax.ppermute(x, 'group', route)]
    ppermute x51, waiting for transfers between devices: 167 us -> 178 us  [to_near(): lax.ppermute(x, 'near', [(i, i ^ k) for i in range(lax.axis_size('near'))])]
    all_gather x1, waiting for transfers between devices: 3.92 us -> 15.1 us  [per_device(): full3 = lax.all_gather(full3, 'group', axis=0, tiled=True)]
    reduce_sum x2, other arithmetic: 9.05 us -> 1.65 us  [the longest x1 0.86 us: taps_back(): return (jnp.stack(taps), jnp.sum(grad, dim))]
    ppermute x16 -> x15, starting transfers between devices: 43.1 us -> 37.6 us  [step_group(): return lax.ppermute(x, 'group', route)]
    dot_general x14 -> x15, matrix products: 51 us -> 53.5 us  [dot(): lax.dot_general(left, right, (dims, ((), ())), preferred_element_type=F32)]
    unnamed x416 -> x370, local copies, waits for them, and re-layouts: 43.4 us -> 41.1 us
  transfers between devices with their start and end apart: 102 -> 101, of which waited for: 43 -> 40; matrix products, arithmetic and copies ran while one was open for 20% -> 20% of each run, Pallas kernels for 12% -> 12%
where the time goes in v4:
time: 693 us; the launch traced here: 683 us
  waiting for transfers between devices  260 us (38%)
  starting transfers between devices  115 us (17%)
  Pallas kernels  94.2 us (14%)
  local copies, waits for them, and re-layouts  79.3 us (11%)
  other arithmetic  59.8 us (9%)
  matrix products  57.5 us (8%)
  between operations  17.1 us (2%)
    ppermute x51, waiting for transfers between devices, to_near(): lax.ppermute(x, 'near', [(i, i ^ k) for i in range(lax.axis_size('near'))])  178 us
    ppermute x51, starting transfers between devices, to_near(): lax.ppermute(x, 'near', [(i, i ^ k) for i in range(lax.axis_size('near'))])  60.9 us
    dot_general x15, matrix products, dot(): lax.dot_general(left, right, (dims, ((), ())), preferred_element_type=F32)  53.5 us
    ppermute x15, waiting for transfers between devices, step_group(): return lax.ppermute(x, 'group', route)  44.9 us
    unnamed x370, local copies, waits for them, and re-layouts  41.1 us
    ppermute x15, starting transfers between devices, step_group(): return lax.ppermute(x, 'group', route)  37.6 us
    pallas_call x17, Pallas kernels, whole_call(): pl.pallas_call(kernel, grid=(1,), out_shape=out_shape, in_specs=[pl.Block...  37.3 us
    pallas_call x3, Pallas kernels, chunk_call(): pl.pallas_call(kernel, grid=(chunks,), in_specs=in_specs, out_specs=out_s...  29.1 us
  transfers between devices with their start and end apart: 101, of which 40 were waited for; matrix products, arithmetic and copies ran while one was open for 20% of the time, Pallas kernels for 12%

profile of v4, /device:TPU:0, one launch (start us, length us, event | category | flops | bytes accessed | tf_op | source)
XLA Modules:
  0.0 682.7 jit_solution(7969486585122241831)
XLA Ops:
  21.1 6.0 all-to-all-start
  42.1 29.9 %collective-permute-done.3.refs_3_ = bf16[144,2048]{1,0:T(8,128)(2,1)} collective-permute-done((bf16[144,2048]{1,0:T(8,128)(2,1)S(1)}, bf16[144,2048]{1,0:T(8,128)(2,1)}, u32[]{:S(2)}, u32[]{:S(2)}) %collective-permute-start.3) | collective-permute-done | bytes 589856 | tf_op jit(solution)/shard_map/ppermute | solution.py:35
  72.0 6.3 collective-permute-done.2.refs_2_
  78.3 7.0 %collective-permute-done.1.refs_1_ = bf16[144,2048]{1,0:T(8,128)(2,1)} collective-permute-done((bf16[144,2048]{1,0:T(8,128)(2,1)S(1)}, bf16[144,2048]{1,0:T(8,128)(2,1)}, u32[]{:S(2)}, u32[]{:S(2)}) %collective-permute-start.1) | collective-permute-done | bytes 589856 | tf_op jit(solution)/shard_map/ppermute | solution.py:35
  104.6 6.8 collective-permute-start.19
  123.4 5.8 collective-permute-done.23.refs_3_
  156.8 7.4 %collective-permute-done.16.refs_2_ = bf16[128,1536]{1,0:T(8,128)(2,1)S(1)} collective-permute-done((bf16[128,1536]{1,0:T(8,128)(2,1)}, bf16[128,1536]{1,0:T(8,128)(2,1)S(1)}, u32[]{:S(2)}, u32[]{:S(2)}) %collective-permute-start.16) | collective-permute-done | bytes 393248 | tf_op jit(solution)/shard_map/ppermute | solution.py:35
  180.4 7.9 %shard_map.402 = (f32[1024,384]{1,0:T(8,128)S(1)}, f32[4,256,384]{2,1,0:T(8,128)S(1)}) custom-call(f32[1024,384]{1,0:T(8,128)S(1)} %get-tuple-element.234.x, f32[8,1024]{1,0:T(8,128)S(1)} %get-tuple-element.534.dt, f32[1024,8]{1,0:T(8,128)S(1)} %copy.129.cum, f32[8,1024]{1,0:T(8,128)S(1)} %reshape_reshape.3.cum_t, ...), custom_call_target="tpu_custom_call" | custom-call | tf_op jit(solution)/shard_map/pallas_call | solution.py:586
  191.4 6.9 %collective-permute-start.30 = (bf16[272,384]{1,0:T(8,128)(2,1)}, bf16[272,384]{1,0:T(8,128)(2,1)}, u32[]{:S(2)}, u32[]{:S(2)}) collective-permute-start(bf16[272,384]{1,0:T(8,128)(2,1)} %pad_maximum_fusion.13), channel_id=1, source_target_pairs={{0,24},{1,25},{2,26},{3,27},{4,28},{5,29},{6,30},{7,31}} | collective-permute-start | bytes 626696 | tf_op jit(solution)/shard_map/ppermute | solution.py:46
  200.2 6.6 fusion.19
  217.2 7.0 %collective-permute-done.28 = bf16[272,384]{1,0:T(8,128)(2,1)} collective-permute-done((bf16[272,384]{1,0:T(8,128)(2,1)}, bf16[272,384]{1,0:T(8,128)(2,1)}, u32[]{:S(2)}, u32[]{:S(2)}) %collective-permute-start.28) | collective-permute-done | bytes 208928 | tf_op jit(solution)/shard_map/ppermute | solution.py:46
  246.6 9.0 %collective-permute-done.35 = bf16[128,2048]{1,0:T(8,128)(2,1)S(1)} collective-permute-done((bf16[128,2048]{1,0:T(8,128)(2,1)S(1)}, bf16[128,2048]{1,0:T(8,128)(2,1)S(1)}, u32[]{:S(2)}, u32[]{:S(2)}) %collective-permute-start.35) | collective-permute-done | bytes 524320 | tf_op jit(solution)/shard_map/ppermute | solution.py:35
  255.7 10.5 %collective-permute-done.36 = bf16[128,2048]{1,0:T(8,128)(2,1)S(1)} collective-permute-done((bf16[128,2048]{1,0:T(8,128)(2,1)S(1)}, bf16[128,2048]{1,0:T(8,128)(2,1)S(1)}, u32[]{:S(2)}, u32[]{:S(2)}) %collective-permute-start.36) | collective-permute-done | bytes 524320 | tf_op jit(solution)/shard_map/ppermute | solution.py:35
  271.0 12.3 %collective-permute-done.40.refs_3_ = bf16[128,2048]{1,0:T(8,128)(2,1)S(1)} collective-permute-done((bf16[128,2048]{1,0:T(8,128)(2,1)S(1)}, bf16[128,2048]{1,0:T(8,128)(2,1)S(1)}, u32[]{:S(2)}, u32[]{:S(2)}) %collective-permute-start.40) | collective-permute-done | bytes 524320 | tf_op jit(solution)/shard_map/ppermute | solution.py:35
  283.3 8.5 %collective-permute-done.39.refs_2_ = bf16[128,2048]{1,0:T(8,128)(2,1)S(1)} collective-permute-done((bf16[128,2048]{1,0:T(8,128)(2,1)S(1)}, bf16[128,2048]{1,0:T(8,128)(2,1)S(1)}, u32[]{:S(2)}, u32[]{:S(2)}) %collective-permute-start.39) | collective-permute-done | bytes 524320 | tf_op jit(solution)/shard_map/ppermute | solution.py:35
  297.5 15.1 %all-gather.5.cloned.1.call-done.refs_1_ = bf16[2048,1536]{1,0:T(8,128)(2,1)} async-done(((bf16[512,1536]{1,0:T(8,128)(2,1)}), bf16[2048,1536]{1,0:T(8,128)(2,1)}) %all-gather.5.cloned.1.call-update) | async-done | bytes 6291472 | tf_op jit(solution)/shard_map/all_gather | solution.py:1009
  312.7 8.1 %fusion = f32[1024,1024]{1,0:T(8,128)S(1)} fusion(bf16[1024,2048]{1,0:T(8,128)(2,1)} %bitcast.304, bf16[2048,1536]{1,0:T(8,128)(2,1)} %all-gather.5.cloned.1.call-done.refs_1_), kind=kOutput, calls=%fused_computation | convolution fusion | flops 4294967296 | bytes 12582912 | tf_op jit(solution)/shard_map/dot_general | solution.py:265
  339.3 6.4 convolution_convert_fusion
  350.8 11.4 %collective-permute-done.47 = bf16[128,2048]{1,0:T(8,128)(2,1)} collective-permute-done((bf16[128,2048]{1,0:T(8,128)(2,1)}, bf16[128,2048]{1,0:T(8,128)(2,1)}, u32[]{:S(2)}, u32[]{:S(2)}) %collective-permute-start.47) | collective-permute-done | bytes 524320 | tf_op jit(solution)/shard_map/ppermute | solution.py:35
  370.2 12.6 %collective-permute-done.51.refs_3_ = bf16[128,2048]{1,0:T(8,128)(2,1)} collective-permute-done((bf16[128,2048]{1,0:T(8,128)(2,1)}, bf16[128,2048]{1,0:T(8,128)(2,1)}, u32[]{:S(2)}, u32[]{:S(2)}) %collective-permute-start.51) | collective-permute-done | bytes 524320 | tf_op jit(solution)/shard_map/ppermute | solution.py:35
  382.9 9.1 %collective-permute-done.50.refs_2_ = bf16[128,2048]{1,0:T(8,128)(2,1)} collective-permute-done((bf16[128,2048]{1,0:T(8,128)(2,1)}, bf16[128,2048]{1,0:T(8,128)(2,1)}, u32[]{:S(2)}, u32[]{:S(2)}) %collective-permute-start.50) | collective-permute-done | bytes 524320 | tf_op jit(solution)/shard_map/ppermute | solution.py:35
  433.2 13.3 %collective-permute-done.57 = bf16[272,384]{1,0:T(8,128)(2,1)} collective-permute-done((bf16[272,384]{1,0:T(8,128)(2,1)}, bf16[272,384]{1,0:T(8,128)(2,1)}, u32[]{:S(2)}, u32[]{:S(2)}) %collective-permute-start.57) | collective-permute-done | bytes 208928 | tf_op jit(solution)/shard_map/ppermute | solution.py:46
  446.5 10.0 %collective-permute-done.56 = bf16[272,384]{1,0:T(8,128)(2,1)} collective-permute-done((bf16[272,384]{1,0:T(8,128)(2,1)}, bf16[272,384]{1,0:T(8,128)(2,1)}, u32[]{:S(2)}, u32[]{:S(2)}) %collective-permute-start.56) | collective-permute-done | bytes 208928 | tf_op jit(solution)/shard_map/ppermute | solution.py:46
  463.4 10.3 %shard_map.413 = bf16[2048,1536]{1,0:T(8,128)(2,1)} custom-call(bf16[1024,2048]{1,0:T(8,128)(2,1)S(1)} %bitcast.300, bf16[1024,2048]{1,0:T(8,128)(2,1)S(1)} %bitcast.294, bf16[1024,2048]{1,0:T(8,128)(2,1)} %bitcast.288, bf16[1024,512]{1,0:T(8,128)(2,1)S(1)} %copy-done.34, bf16[1024,512]{1,0:T(8,128)(2,1)S(1)} %copy-done.32, ...), custom_call_target="tpu_custom_call" | custom-call | tf_op jit(solution)/shard_map/pallas_call | solution.py:225
  495.8 6.6 collective-permute-done.66
  506.3 12.4 %shard_map.415 = (f32[1024,384]{1,0:T(8,128)S(1)}, f32[256,1024]{1,0:T(8,128)S(1)}, bf16[256,1024]{1,0:T(8,128)(2,1)S(1)}) custom-call(f32[1024,384]{1,0:T(8,128)S(1)} %get-tuple-element.234.x, f32[8,1024]{1,0:T(8,128)S(1)} %copy-done.53, f32[1024,8]{1,0:T(8,128)S(1)} %copy-done.29, f32[8,1024]{1,0:T(8,128)S(1)} %reshape_reshape.3.cum_t, ...), custom_call_target="tpu_custom_call" | custom-call | tf_op jit(solution)/shard_map/pallas_call | solution.py:586
  528.5 8.9 %shard_map.416 = (f32[1024,384]{1,0:T(8,128)S(1)}, bf16[256,1024]{1,0:T(8,128)(2,1)S(1)}, f32[8,1024]{1,0:T(8,128)S(1)}, f32[8,1024]{1,0:T(8,128)S(1)}, f32[1,384]{1,0:T(1,128)S(1)}) custom-call(f32[1024,384]{1,0:T(8,128)S(1)} %get-tuple-element.234.x, f32[1024,384]{1,0:T(8,128)S(1)} %copy-done.25, f32[8,1024]{1,0:T(8,128)S(1)} %copy-done.53, ...), custom_call_target="tpu_custom_call" | custom-call | tf_op jit(solution)/shard_map/pallas_call | solution.py:586
  558.8 10.9 %collective-permute-done.77 = f32[64,3]{1,0:T(8,128)S(1)} collective-permute-done((f32[64,3]{1,0:T(8,128)S(1)}, f32[64,3]{1,0:T(8,128)S(1)}, u32[]{:S(2)}, u32[]{:S(2)}) %collective-permute-start.77) | collective-permute-done | bytes 800 | tf_op jit(solution)/shard_map/ppermute | solution.py:46
  570.3 6.1 convolution_convert_fusion.1
  576.4 6.8 shard_map.417
  609.6 10.0 %collective-permute-done.80 = bf16[128,2048]{1,0:T(8,128)(2,1)S(1)} collective-permute-done((bf16[128,2048]{1,0:T(8,128)(2,1)S(1)}, bf16[128,2048]{1,0:T(8,128)(2,1)S(1)}, u32[]{:S(2)}, u32[]{:S(2)}) %collective-permute-start.80) | collective-permute-done | bytes 524320 | tf_op jit(solution)/shard_map/ppermute | solution.py:35
  637.1 10.5 %collective-permute-done.86 = bf16[512,512]{1,0:T(8,128)(2,1)} collective-permute-done((bf16[512,512]{1,0:T(8,128)(2,1)}, bf16[512,512]{1,0:T(8,128)(2,1)}, u32[]{:S(2)}, u32[]{:S(2)}) %collective-permute-start.86) | collective-permute-done | bytes 524320 | tf_op jit(solution)/shard_map/ppermute | solution.py:40
  (811 shorter events, 359.4 us)
Async XLA Ops:
  21.1 65.5 %all-to-all-start = ((bf16[16,136,512]{2,1,0:T(8,128)(2,1)}), bf16[16,136,512]{2,1,0:T(8,128)(2,1)}, u32[]{:S(2)}, u32[]{:S(2)}) async-start(bf16[16,136,512]{2,1,0:T(8,128)(2,1)} %bitcast.15), calls=%async_computation | async-start | bytes 4456448 | tf_op jit(solution)/shard_map/all_to_all | solution.py:96
  27.2 173.1 %all-gather.3.cloned.1.call-start = ((), (), s32[]{:S(2)}) async-start(), calls=%async_computation.4 | async-start | bytes 5242880 | tf_op jit(solution)/shard_map/all_gather | solution.py:979
  35.7 36.3 %collective-permute-start.3 = (bf16[144,2048]{1,0:T(8,128)(2,1)S(1)}, bf16[144,2048]{1,0:T(8,128)(2,1)}, u32[]{:S(2)}, u32[]{:S(2)}) collective-permute-start(bf16[144,2048]{1,0:T(8,128)(2,1)S(1)} %pad_maximum_fusion.9.refs_0_), channel_id=1, source_target_pairs={{0,6},{2,4},{4,2},{6,0},{1,7},{3,5},{5,3},{7,1},{8,14},{10,12},{12... | collective-permute-start | bytes 1769480 | tf_op jit(solution)/shard_map/ppermute | solution.py:35
  38.5 39.8 %collective-permute-start.2 = (bf16[144,2048]{1,0:T(8,128)(2,1)S(1)}, bf16[144,2048]{1,0:T(8,128)(2,1)}, u32[]{:S(2)}, u32[]{:S(2)}) collective-permute-start(bf16[144,2048]{1,0:T(8,128)(2,1)S(1)} %pad_maximum_fusion.9.refs_0_), channel_id=1, source_target_pairs={{0,4},{2,6},{4,0},{6,2},{1,5},{3,7},{5,1},{7,3},{8,12},{10,14},{12... | collective-permute-start | bytes 1769480 | tf_op jit(solution)/shard_map/ppermute | solution.py:35
  39.1 46.3 %collective-permute-start.1 = (bf16[144,2048]{1,0:T(8,128)(2,1)S(1)}, bf16[144,2048]{1,0:T(8,128)(2,1)}, u32[]{:S(2)}, u32[]{:S(2)}) collective-permute-start(bf16[144,2048]{1,0:T(8,128)(2,1)S(1)} %pad_maximum_fusion.9.refs_0_), channel_id=1, source_target_pairs={{0,2},{2,0},{4,6},{6,4},{1,3},{3,1},{5,7},{7,5},{8,10},{10,8},{12,... | collective-permute-start | bytes 1769480 | tf_op jit(solution)/shard_map/ppermute | solution.py:35
  42.1 48.1 %collective-permute-start.4 = (bf16[144,2048]{1,0:T(8,128)(2,1)S(1)}, bf16[144,2048]{1,0:T(8,128)(2,1)}, u32[]{:S(2)}, u32[]{:S(2)}) collective-permute-start(bf16[144,2048]{1,0:T(8,128)(2,1)S(1)} %pad_maximum_fusion.9.refs_0_), channel_id=1, source_target_pairs={{0,1},{1,0},{2,3},{3,2},{4,5},{5,4},{6,7},{7,6},{8,9},{9,8},{10,11... | collective-permute-start | bytes 1769480 | tf_op jit(solution)/shard_map/ppermute | solution.py:31
  103.4 209.3 %all-gather.5.cloned.1.call-start = ((), (), s32[]{:S(2)}) async-start(), calls=%async_computation.5 | async-start | bytes 7864320 | tf_op jit(solution)/shard_map/all_gather | solution.py:1009
  113.4 30.3 %collective-permute-start.24 = (bf16[128,2048]{1,0:T(8,128)(2,1)S(1)}, bf16[128,2048]{1,0:T(8,128)(2,1)S(1)}, u32[]{:S(2)}, u32[]{:S(2)}) collective-permute-start(bf16[128,2048]{1,0:T(8,128)(2,1)S(1)} %constant_dynamic-slice_fusion.4.refs_0_), channel_id=1, source_target_pairs={{0,1},{1,0},{2,3},{3,2},{4,5},{5,4},{6,7},{7,6},{8,9},{9,8},{10,11... | collective-permute-start | bytes 1572872 | tf_op jit(solution)/shard_map/ppermute | solution.py:31
  114.4 25.4 %collective-permute-start.22 = (bf16[128,2048]{1,0:T(8,128)(2,1)S(1)}, bf16[128,2048]{1,0:T(8,128)(2,1)}, u32[]{:S(2)}, u32[]{:S(2)}) collective-permute-start(bf16[128,2048]{1,0:T(8,128)(2,1)S(1)} %constant_dynamic-slice_fusion.4.refs_0_), channel_id=1, source_target_pairs={{0,4},{2,6},{4,0},{6,2},{1,5},{3,7},{5,1},{7,3},{8,12},{10,14},{12... | collective-permute-start | bytes 1572872 | tf_op jit(solution)/shard_map/ppermute | solution.py:35
  166.7 324.0 %reduce-scatter.3.cloned.1.call-start = ((), (), s32[]{:S(2)}) async-start(), calls=%async_computation.6 | async-start | bytes 5242880 | tf_op jit(solution)/shard_map/reduce_scatter | solution.py:1062
  175.8 33.6 %collective-permute-start.33 = (bf16[256,1024]{1,0:T(8,128)(2,1)}, bf16[256,1024]{1,0:T(8,128)(2,1)}, u32[]{:S(2)}, u32[]{:S(2)}) collective-permute-start(bf16[256,1024]{1,0:T(8,128)(2,1)} %pad_maximum_fusion.11.refs_0_), channel_id=1, source_target_pairs={{0,6},{2,4},{4,2},{6,0},{1,7},{3,5},{5,3},{7,1},{8,14},{10,12},{12... | collective-permute-start | bytes 1572872 | tf_op jit(solution)/shard_map/ppermute | solution.py:35
  176.9 36.2 %collective-permute-start.32 = (bf16[256,1024]{1,0:T(8,128)(2,1)}, bf16[256,1024]{1,0:T(8,128)(2,1)}, u32[]{:S(2)}, u32[]{:S(2)}) collective-permute-start(bf16[256,1024]{1,0:T(8,128)(2,1)} %pad_maximum_fusion.11.refs_0_), channel_id=1, source_target_pairs={{0,4},{2,6},{4,0},{6,2},{1,5},{3,7},{5,1},{7,3},{8,12},{10,14},{12... | collective-permute-start | bytes 1572872 | tf_op jit(solution)/shard_map/ppermute | solution.py:35
  178.3 34.8 %collective-permute-start.31 = (bf16[256,1024]{1,0:T(8,128)(2,1)}, bf16[256,1024]{1,0:T(8,128)(2,1)}, u32[]{:S(2)}, u32[]{:S(2)}) collective-permute-start(bf16[256,1024]{1,0:T(8,128)(2,1)} %pad_maximum_fusion.11.refs_0_), channel_id=1, source_target_pairs={{0,2},{2,0},{4,6},{6,4},{1,3},{3,1},{5,7},{7,5},{8,10},{10,8},{12,... | collective-permute-start | bytes 1572872 | tf_op jit(solution)/shard_map/ppermute | solution.py:35
  191.4 25.8 %collective-permute-start.30 = (bf16[272,384]{1,0:T(8,128)(2,1)}, bf16[272,384]{1,0:T(8,128)(2,1)}, u32[]{:S(2)}, u32[]{:S(2)}) collective-permute-start(bf16[272,384]{1,0:T(8,128)(2,1)} %pad_maximum_fusion.13), channel_id=1, source_target_pairs={{0,24},{1,25},{2,26},{3,27},{4,28},{5,29},{6,30},{7,31}} | collective-permute-start | bytes 626696 | tf_op jit(solution)/shard_map/ppermute | solution.py:46
  241.3 24.9 %collective-permute-start.36 = (bf16[128,2048]{1,0:T(8,128)(2,1)S(1)}, bf16[128,2048]{1,0:T(8,128)(2,1)S(1)}, u32[]{:S(2)}, u32[]{:S(2)}) collective-permute-start(bf16[128,2048]{1,0:T(8,128)(2,1)S(1)} %get-tuple-element.253), channel_id=1, source_target_pairs={{0,4},{2,6},{4,0},{6,2},{1,5},{3,7},{5,1},{7,3},{8,12},{10,14},{12... | collective-permute-start | bytes 1572872 | tf_op jit(solution)/shard_map/ppermute | solution.py:35
  241.3 24.9 %collective-permute-start.37 = (bf16[128,2048]{1,0:T(8,128)(2,1)S(1)}, bf16[128,2048]{1,0:T(8,128)(2,1)S(1)}, u32[]{:S(2)}, u32[]{:S(2)}) collective-permute-start(bf16[128,2048]{1,0:T(8,128)(2,1)S(1)} %get-tuple-element.254), channel_id=1, source_target_pairs={{0,6},{2,4},{4,2},{6,0},{1,7},{3,5},{5,3},{7,1},{8,14},{10,12},{12... | collective-permute-start | bytes 1572872 | tf_op jit(solution)/shard_map/ppermute | solution.py:35
  336.8 25.5 %collective-permute-start.47 = (bf16[128,2048]{1,0:T(8,128)(2,1)}, bf16[128,2048]{1,0:T(8,128)(2,1)}, u32[]{:S(2)}, u32[]{:S(2)}) collective-permute-start(bf16[128,2048]{1,0:T(8,128)(2,1)} %get-tuple-element.273), channel_id=1, source_target_pairs={{0,4},{2,6},{4,0},{6,2},{1,5},{3,7},{5,1},{7,3},{8,12},{10,14},{12... | collective-permute-start | bytes 1572872 | tf_op jit(solution)/shard_map/ppermute | solution.py:35
  362.3 267.4 %reduce-scatter.5.cloned.1.call-start = ((), (), s32[]{:S(2)}) async-start(), calls=%async_computation.7 | async-start | bytes 7864320 | tf_op jit(solution)/shard_map/reduce_scatter | solution.py:1062
  370.2 25.4 %collective-permute-start.52 = (bf16[128,2048]{1,0:T(8,128)(2,1)}, bf16[128,2048]{1,0:T(8,128)(2,1)}, u32[]{:S(2)}, u32[]{:S(2)}) collective-permute-start(bf16[128,2048]{1,0:T(8,128)(2,1)} %fusion.82.refs_0_), channel_id=1, source_target_pairs={{0,1},{1,0},{2,3},{3,2},{4,5},{5,4},{6,7},{7,6},{8,9},{9,8},{10,11... | collective-permute-start | bytes 1572872 | tf_op jit(solution)/shard_map/ppermute | solution.py:31
  408.5 38.1 %collective-permute-start.57 = (bf16[272,384]{1,0:T(8,128)(2,1)}, bf16[272,384]{1,0:T(8,128)(2,1)}, u32[]{:S(2)}, u32[]{:S(2)}) collective-permute-start(bf16[272,384]{1,0:T(8,128)(2,1)} %pad_maximum_fusion.12), channel_id=1, source_target_pairs={{16,0},{24,8},{17,1},{25,9},{18,2},{26,10},{19,3},{27,11},{20,4},{... | collective-permute-start | bytes 626696 | tf_op jit(solution)/shard_map/ppermute | solution.py:46
  425.7 47.9 %collective-permute-start.59 = (bf16[256,1024]{1,0:T(8,128)(2,1)}, bf16[256,1024]{1,0:T(8,128)(2,1)}, u32[]{:S(2)}, u32[]{:S(2)}) collective-permute-start(bf16[256,1024]{1,0:T(8,128)(2,1)} %copy-done.73), channel_id=1, source_target_pairs={{0,2},{2,0},{4,6},{6,4},{1,3},{3,1},{5,7},{7,5},{8,10},{10,8},{12,... | collective-permute-start | bytes 1572872 | tf_op jit(solution)/shard_map/ppermute | solution.py:35
  426.9 46.8 %collective-permute-start.60 = (bf16[256,1024]{1,0:T(8,128)(2,1)}, bf16[256,1024]{1,0:T(8,128)(2,1)}, u32[]{:S(2)}, u32[]{:S(2)}) collective-permute-start(bf16[256,1024]{1,0:T(8,128)(2,1)} %copy-done.72), channel_id=1, source_target_pairs={{0,4},{2,6},{4,0},{6,2},{1,5},{3,7},{5,1},{7,3},{8,12},{10,14},{12... | collective-permute-start | bytes 1572872 | tf_op jit(solution)/shard_map/ppermute | solution.py:35
  428.1 45.6 %collective-permute-start.61 = (bf16[256,1024]{1,0:T(8,128)(2,1)}, bf16[256,1024]{1,0:T(8,128)(2,1)}, u32[]{:S(2)}, u32[]{:S(2)}) collective-permute-start(bf16[256,1024]{1,0:T(8,128)(2,1)} %copy-done.71), channel_id=1, source_target_pairs={{0,6},{2,4},{4,2},{6,0},{1,7},{3,5},{5,3},{7,1},{8,14},{10,12},{12... | collective-permute-start | bytes 1572872 | tf_op jit(solution)/shard_map/ppermute | solution.py:35
  429.4 27.1 %collective-permute-start.56 = (bf16[272,384]{1,0:T(8,128)(2,1)}, bf16[272,384]{1,0:T(8,128)(2,1)}, u32[]{:S(2)}, u32[]{:S(2)}) collective-permute-start(bf16[272,384]{1,0:T(8,128)(2,1)} %pad_maximum_fusion.12), channel_id=1, source_target_pairs={{8,0},{16,8},{24,16},{9,1},{17,9},{25,17},{10,2},{18,10},{26,18},{... | collective-permute-start | bytes 626696 | tf_op jit(solution)/shard_map/ppermute | solution.py:46
  488.7 32.0 %collective-permute-start.67 = (bf16[128,2048]{1,0:T(8,128)(2,1)}, bf16[128,2048]{1,0:T(8,128)(2,1)}, u32[]{:S(2)}, u32[]{:S(2)}) collective-permute-start(bf16[128,2048]{1,0:T(8,128)(2,1)} %get-tuple-element.312), channel_id=1, source_target_pairs={{0,4},{2,6},{4,0},{6,2},{1,5},{3,7},{5,1},{7,3},{8,12},{10,14},{12... | collective-permute-start | bytes 1572872 | tf_op jit(solution)/shard_map/ppermute | solution.py:35
  490.2 31.8 %collective-permute-start.68 = (bf16[128,2048]{1,0:T(8,128)(2,1)}, bf16[128,2048]{1,0:T(8,128)(2,1)}, u32[]{:S(2)}, u32[]{:S(2)}) collective-permute-start(bf16[128,2048]{1,0:T(8,128)(2,1)} %get-tuple-element.313), channel_id=1, source_target_pairs={{0,6},{2,4},{4,2},{6,0},{1,7},{3,5},{5,3},{7,1},{8,14},{10,12},{12... | collective-permute-start | bytes 1572872 | tf_op jit(solution)/shard_map/ppermute | solution.py:35
  492.9 30.4 %collective-permute-start.65 = (bf16[128,1024]{1,0:T(8,128)(2,1)S(1)}, bf16[128,1024]{1,0:T(8,128)(2,1)S(1)}, u32[]{:S(2)}, u32[]{:S(2)}) collective-permute-start(bf16[128,1024]{1,0:T(8,128)(2,1)S(1)} %get-tuple-element.492), channel_id=1, source_target_pairs={{0,6},{2,4},{4,2},{6,0},{1,7},{3,5},{5,3},{7,1},{8,14},{10,12},{12... | collective-permute-start | bytes 786440 | tf_op jit(solution)/shard_map/ppermute | solution.py:35
  495.2 29.8 %collective-permute-start.64 = (bf16[128,1024]{1,0:T(8,128)(2,1)S(1)}, bf16[128,1024]{1,0:T(8,128)(2,1)S(1)}, u32[]{:S(2)}, u32[]{:S(2)}) collective-permute-start(bf16[128,1024]{1,0:T(8,128)(2,1)S(1)} %get-tuple-element.493), channel_id=1, source_target_pairs={{0,4},{2,6},{4,0},{6,2},{1,5},{3,7},{5,1},{7,3},{8,12},{10,14},{12... | collective-permute-start | bytes 786440 | tf_op jit(solution)/shard_map/ppermute | solution.py:35
  589.0 45.1 %collective-permute-start.87 = (bf16[512,512]{1,0:T(8,128)(2,1)}, bf16[512,512]{1,0:T(8,128)(2,1)}, u32[]{:S(2)}, u32[]{:S(2)}) collective-permute-start(bf16[512,512]{1,0:T(8,128)(2,1)} %get-tuple-element.475), channel_id=1, source_target_pairs={{0,24},{8,0},{16,8},{24,16},{1,25},{9,1},{17,9},{25,17},{2,26},{10... | collective-permute-start | bytes 1572872 | tf_op jit(solution)/shard_map/ppermute | solution.py:40
  589.0 58.6 %collective-permute-start.86 = (bf16[512,512]{1,0:T(8,128)(2,1)}, bf16[512,512]{1,0:T(8,128)(2,1)}, u32[]{:S(2)}, u32[]{:S(2)}) collective-permute-start(bf16[512,512]{1,0:T(8,128)(2,1)} %get-tuple-element.476), channel_id=1, source_target_pairs={{0,16},{8,24},{16,0},{24,8},{1,17},{9,25},{17,1},{25,9},{2,18},{10... | collective-permute-start | bytes 1572872 | tf_op jit(solution)/shard_map/ppermute | solution.py:40
  608.4 39.1 %collective-permute-start.85 = (bf16[512,512]{1,0:T(8,128)(2,1)}, bf16[512,512]{1,0:T(8,128)(2,1)}, u32[]{:S(2)}, u32[]{:S(2)}) collective-permute-start(bf16[512,512]{1,0:T(8,128)(2,1)} %get-tuple-element.477), channel_id=1, source_target_pairs={{0,8},{8,16},{16,24},{24,0},{1,9},{9,17},{17,25},{25,1},{2,10},{10... | collective-permute-start | bytes 1572872 | tf_op jit(solution)/shard_map/ppermute | solution.py:40
  625.2 37.5 %all-to-all-start.1 = ((f32[16,32,128]{2,1,0:T(8,128)}), f32[16,32,128]{2,1,0:T(8,128)S(1)}, u32[]{:S(2)}, u32[]{:S(2)}) async-start(f32[16,32,128]{2,1,0:T(8,128)} %bitcast.164), calls=%async_computation.2 | async-start | bytes 524288 | tf_op jit(solution)/shard_map/all_to_all | solution.py:96
  (246 other events, 2967.3 us)
Sparse Core Ops, SparseCore 0:
  103.5 83.8 all-gather.2
  188.9 123.6 all-gather.4
  362.4 95.0 reduce-scatter.2
  476.9 122.4 reduce-scatter.4

commit v5 on v4

--- a/solution.py
+++ b/solution.py
@@ -19,7 +19,7 @@
 F32 = jnp.float32
 B16 = jnp.bfloat16
 ATTEND_ROWS = 256
-ATTEND_KEYS = 512
+ATTEND_KEYS = 1024
 VMEM_LIMIT = 40 << 20
 
 

time: 693 us -> 693 us (level)
  transfers between devices with their start and end apart: 101 -> 101, of which waited for: 40 -> 41; matrix products, arithmetic and copies ran while one was open for 20% -> 20% of each run, Pallas kernels for 12% -> 12%
where the time goes in v5:
time: 693 us; the launch traced here: 682 us
  waiting for transfers between devices  259 us (37%)
  starting transfers between devices  116 us (17%)
  Pallas kernels  93.7 us (14%)
  local copies, waits for them, and re-layouts  79.5 us (11%)
  other arithmetic  59.8 us (9%)
  matrix products  57.5 us (8%)
  between operations  17.3 us (2%)
    ppermute x51, waiting for transfers between devices, to_near(): lax.ppermute(x, 'near', [(i, i ^ k) for i in range(lax.axis_size('near'))])  178 us
    ppermute x51, starting transfers between devices, to_near(): lax.ppermute(x, 'near', [(i, i ^ k) for i in range(lax.axis_size('near'))])  60.9 us
    dot_general x15, matrix products, dot(): lax.dot_general(left, right, (dims, ((), ())), preferred_element_type=F32)  53.6 us
    ppermute x15, waiting for transfers between devices, step_group(): return lax.ppermute(x, 'group', route)  44.1 us
    unnamed x370, local copies, waits for them, and re-layouts  41.4 us
    ppermute x15, starting transfers between devices, step_group(): return lax.ppermute(x, 'group', route)  38 us
    pallas_call x17, Pallas kernels, whole_call(): pl.pallas_call(kernel, grid=(1,), out_shape=out_shape, in_specs=[pl.Block...  36.8 us
    pallas_call x3, Pallas kernels, chunk_call(): pl.pallas_call(kernel, grid=(chunks,), in_specs=in_specs, out_specs=out_s...  29.1 us
  transfers between devices with their start and end apart: 101, of which 41 were waited for; matrix products, arithmetic and copies ran while one was open for 20% of the time, Pallas kernels for 12%

profile of v5, /device:TPU:0, one launch (start us, length us, event | category | flops | bytes accessed | tf_op | source)
XLA Modules:
  0.0 682.1 jit_solution(17710255771427605535)
XLA Ops:
  21.1 6.0 all-to-all-start
  42.1 29.9 %collective-permute-done.3.refs_3_ = bf16[144,2048]{1,0:T(8,128)(2,1)} collective-permute-done((bf16[144,2048]{1,0:T(8,128)(2,1)S(1)}, bf16[144,2048]{1,0:T(8,128)(2,1)}, u32[]{:S(2)}, u32[]{:S(2)}) %collective-permute-start.3) | collective-permute-done | bytes 589856 | tf_op jit(solution)/shard_map/ppermute | solution.py:35
  72.0 6.3 collective-permute-done.2.refs_2_
  78.3 7.0 %collective-permute-done.1.refs_1_ = bf16[144,2048]{1,0:T(8,128)(2,1)} collective-permute-done((bf16[144,2048]{1,0:T(8,128)(2,1)S(1)}, bf16[144,2048]{1,0:T(8,128)(2,1)}, u32[]{:S(2)}, u32[]{:S(2)}) %collective-permute-start.1) | collective-permute-done | bytes 589856 | tf_op jit(solution)/shard_map/ppermute | solution.py:35
  104.6 6.8 collective-permute-start.19
  156.8 7.4 %collective-permute-done.16.refs_2_ = bf16[128,1536]{1,0:T(8,128)(2,1)S(1)} collective-permute-done((bf16[128,1536]{1,0:T(8,128)(2,1)}, bf16[128,1536]{1,0:T(8,128)(2,1)S(1)}, u32[]{:S(2)}, u32[]{:S(2)}) %collective-permute-start.16) | collective-permute-done | bytes 393248 | tf_op jit(solution)/shard_map/ppermute | solution.py:35
  180.4 7.9 %shard_map.402 = (f32[1024,384]{1,0:T(8,128)S(1)}, f32[4,256,384]{2,1,0:T(8,128)S(1)}) custom-call(f32[1024,384]{1,0:T(8,128)S(1)} %get-tuple-element.234.x, f32[8,1024]{1,0:T(8,128)S(1)} %get-tuple-element.534.dt, f32[1024,8]{1,0:T(8,128)S(1)} %copy.129.cum, f32[8,1024]{1,0:T(8,128)S(1)} %reshape_reshape.3.cum_t, ...), custom_call_target="tpu_custom_call" | custom-call | tf_op jit(solution)/shard_map/pallas_call | solution.py:586
  191.4 6.9 %collective-permute-start.30 = (bf16[272,384]{1,0:T(8,128)(2,1)}, bf16[272,384]{1,0:T(8,128)(2,1)}, u32[]{:S(2)}, u32[]{:S(2)}) collective-permute-start(bf16[272,384]{1,0:T(8,128)(2,1)} %pad_maximum_fusion.13), channel_id=1, source_target_pairs={{0,24},{1,25},{2,26},{3,27},{4,28},{5,29},{6,30},{7,31}} | collective-permute-start | bytes 626696 | tf_op jit(solution)/shard_map/ppermute | solution.py:46
  200.2 6.6 fusion.19
  217.1 7.0 %collective-permute-done.28 = bf16[272,384]{1,0:T(8,128)(2,1)} collective-permute-done((bf16[272,384]{1,0:T(8,128)(2,1)}, bf16[272,384]{1,0:T(8,128)(2,1)}, u32[]{:S(2)}, u32[]{:S(2)}) %collective-permute-start.28) | collective-permute-done | bytes 208928 | tf_op jit(solution)/shard_map/ppermute | solution.py:46
  246.7 9.0 %collective-permute-done.35 = bf16[128,2048]{1,0:T(8,128)(2,1)S(1)} collective-permute-done((bf16[128,2048]{1,0:T(8,128)(2,1)S(1)}, bf16[128,2048]{1,0:T(8,128)(2,1)S(1)}, u32[]{:S(2)}, u32[]{:S(2)}) %collective-permute-start.35) | collective-permute-done | bytes 524320 | tf_op jit(solution)/shard_map/ppermute | solution.py:35
  255.7 10.5 %collective-permute-done.36 = bf16[128,2048]{1,0:T(8,128)(2,1)S(1)} collective-permute-done((bf16[128,2048]{1,0:T(8,128)(2,1)S(1)}, bf16[128,2048]{1,0:T(8,128)(2,1)S(1)}, u32[]{:S(2)}, u32[]{:S(2)}) %collective-permute-start.36) | collective-permute-done | bytes 524320 | tf_op jit(solution)/shard_map/ppermute | solution.py:35
  271.0 12.3 %collective-permute-done.40.refs_3_ = bf16[128,2048]{1,0:T(8,128)(2,1)S(1)} collective-permute-done((bf16[128,2048]{1,0:T(8,128)(2,1)S(1)}, bf16[128,2048]{1,0:T(8,128)(2,1)S(1)}, u32[]{:S(2)}, u32[]{:S(2)}) %collective-permute-start.40) | collective-permute-done | bytes 524320 | tf_op jit(solution)/shard_map/ppermute | solution.py:35
  283.3 8.5 %collective-permute-done.39.refs_2_ = bf16[128,2048]{1,0:T(8,128)(2,1)S(1)} collective-permute-done((bf16[128,2048]{1,0:T(8,128)(2,1)S(1)}, bf16[128,2048]{1,0:T(8,128)(2,1)S(1)}, u32[]{:S(2)}, u32[]{:S(2)}) %collective-permute-start.39) | collective-permute-done | bytes 524320 | tf_op jit(solution)/shard_map/ppermute | solution.py:35
  297.6 15.1 %all-gather.5.cloned.1.call-done.refs_1_ = bf16[2048,1536]{1,0:T(8,128)(2,1)} async-done(((bf16[512,1536]{1,0:T(8,128)(2,1)}), bf16[2048,1536]{1,0:T(8,128)(2,1)}) %all-gather.5.cloned.1.call-update) | async-done | bytes 6291472 | tf_op jit(solution)/shard_map/all_gather | solution.py:1009
  312.7 7.9 %fusion = f32[1024,1024]{1,0:T(8,128)S(1)} fusion(bf16[1024,2048]{1,0:T(8,128)(2,1)} %bitcast.304, bf16[2048,1536]{1,0:T(8,128)(2,1)} %all-gather.5.cloned.1.call-done.refs_1_), kind=kOutput, calls=%fused_computation | convolution fusion | flops 4294967296 | bytes 12582912 | tf_op jit(solution)/shard_map/dot_general | solution.py:265
  339.1 6.6 convolution_convert_fusion
  350.6 11.4 %collective-permute-done.47 = bf16[128,2048]{1,0:T(8,128)(2,1)} collective-permute-done((bf16[128,2048]{1,0:T(8,128)(2,1)}, bf16[128,2048]{1,0:T(8,128)(2,1)}, u32[]{:S(2)}, u32[]{:S(2)}) %collective-permute-start.47) | collective-permute-done | bytes 524320 | tf_op jit(solution)/shard_map/ppermute | solution.py:35
  370.0 12.6 %collective-permute-done.51.refs_3_ = bf16[128,2048]{1,0:T(8,128)(2,1)} collective-permute-done((bf16[128,2048]{1,0:T(8,128)(2,1)}, bf16[128,2048]{1,0:T(8,128)(2,1)}, u32[]{:S(2)}, u32[]{:S(2)}) %collective-permute-start.51) | collective-permute-done | bytes 524320 | tf_op jit(solution)/shard_map/ppermute | solution.py:35
  382.6 9.1 %collective-permute-done.50.refs_2_ = bf16[128,2048]{1,0:T(8,128)(2,1)} collective-permute-done((bf16[128,2048]{1,0:T(8,128)(2,1)}, bf16[128,2048]{1,0:T(8,128)(2,1)}, u32[]{:S(2)}, u32[]{:S(2)}) %collective-permute-start.50) | collective-permute-done | bytes 524320 | tf_op jit(solution)/shard_map/ppermute | solution.py:35
  432.9 13.4 %collective-permute-done.57 = bf16[272,384]{1,0:T(8,128)(2,1)} collective-permute-done((bf16[272,384]{1,0:T(8,128)(2,1)}, bf16[272,384]{1,0:T(8,128)(2,1)}, u32[]{:S(2)}, u32[]{:S(2)}) %collective-permute-start.57) | collective-permute-done | bytes 208928 | tf_op jit(solution)/shard_map/ppermute | solution.py:46
  446.3 10.0 %collective-permute-done.56 = bf16[272,384]{1,0:T(8,128)(2,1)} collective-permute-done((bf16[272,384]{1,0:T(8,128)(2,1)}, bf16[272,384]{1,0:T(8,128)(2,1)}, u32[]{:S(2)}, u32[]{:S(2)}) %collective-permute-start.56) | collective-permute-done | bytes 208928 | tf_op jit(solution)/shard_map/ppermute | solution.py:46
  463.2 10.3 %shard_map.413 = bf16[2048,1536]{1,0:T(8,128)(2,1)} custom-call(bf16[1024,2048]{1,0:T(8,128)(2,1)S(1)} %bitcast.300, bf16[1024,2048]{1,0:T(8,128)(2,1)S(1)} %bitcast.294, bf16[1024,2048]{1,0:T(8,128)(2,1)} %bitcast.288, bf16[1024,512]{1,0:T(8,128)(2,1)S(1)} %copy-done.34, bf16[1024,512]{1,0:T(8,128)(2,1)S(1)} %copy-done.32, ...), custom_call_target="tpu_custom_call" | custom-call | tf_op jit(solution)/shard_map/pallas_call | solution.py:225
  495.5 6.6 collective-permute-done.66
  506.0 12.4 %shard_map.415 = (f32[1024,384]{1,0:T(8,128)S(1)}, f32[256,1024]{1,0:T(8,128)S(1)}, bf16[256,1024]{1,0:T(8,128)(2,1)S(1)}) custom-call(f32[1024,384]{1,0:T(8,128)S(1)} %get-tuple-element.234.x, f32[8,1024]{1,0:T(8,128)S(1)} %copy-done.53, f32[1024,8]{1,0:T(8,128)S(1)} %copy-done.29, f32[8,1024]{1,0:T(8,128)S(1)} %reshape_reshape.3.cum_t, ...), custom_call_target="tpu_custom_call" | custom-call | tf_op jit(solution)/shard_map/pallas_call | solution.py:586
  528.3 8.9 %shard_map.416 = (f32[1024,384]{1,0:T(8,128)S(1)}, bf16[256,1024]{1,0:T(8,128)(2,1)S(1)}, f32[8,1024]{1,0:T(8,128)S(1)}, f32[8,1024]{1,0:T(8,128)S(1)}, f32[1,384]{1,0:T(1,128)S(1)}) custom-call(f32[1024,384]{1,0:T(8,128)S(1)} %get-tuple-element.234.x, f32[1024,384]{1,0:T(8,128)S(1)} %copy-done.25, f32[8,1024]{1,0:T(8,128)S(1)} %copy-done.53, ...), custom_call_target="tpu_custom_call" | custom-call | tf_op jit(solution)/shard_map/pallas_call | solution.py:586
  558.7 9.8 %collective-permute-done.77 = f32[64,3]{1,0:T(8,128)S(1)} collective-permute-done((f32[64,3]{1,0:T(8,128)S(1)}, f32[64,3]{1,0:T(8,128)S(1)}, u32[]{:S(2)}, u32[]{:S(2)}) %collective-permute-start.77) | collective-permute-done | bytes 800 | tf_op jit(solution)/shard_map/ppermute | solution.py:46
  569.2 6.1 convolution_convert_fusion.1
  575.3 6.8 shard_map.417
  609.0 9.8 %collective-permute-done.80 = bf16[128,2048]{1,0:T(8,128)(2,1)S(1)} collective-permute-done((bf16[128,2048]{1,0:T(8,128)(2,1)S(1)}, bf16[128,2048]{1,0:T(8,128)(2,1)S(1)}, u32[]{:S(2)}, u32[]{:S(2)}) %collective-permute-start.80) | collective-permute-done | bytes 524320 | tf_op jit(solution)/shard_map/ppermute | solution.py:35
  636.2 10.2 %collective-permute-done.86 = bf16[512,512]{1,0:T(8,128)(2,1)} collective-permute-done((bf16[512,512]{1,0:T(8,128)(2,1)}, bf16[512,512]{1,0:T(8,128)(2,1)}, u32[]{:S(2)}, u32[]{:S(2)}) %collective-permute-start.86) | collective-permute-done | bytes 524320 | tf_op jit(solution)/shard_map/ppermute | solution.py:40
  646.4 6.1 collective-permute-done.89.refs_2_
  (811 shorter events, 359.7 us)
Async XLA Ops:
  21.1 65.5 %all-to-all-start = ((bf16[16,136,512]{2,1,0:T(8,128)(2,1)}), bf16[16,136,512]{2,1,0:T(8,128)(2,1)}, u32[]{:S(2)}, u32[]{:S(2)}) async-start(bf16[16,136,512]{2,1,0:T(8,128)(2,1)} %bitcast.15), calls=%async_computation | async-start | bytes 4456448 | tf_op jit(solution)/shard_map/all_to_all | solution.py:96
  27.2 173.1 %all-gather.3.cloned.1.call-start = ((), (), s32[]{:S(2)}) async-start(), calls=%async_computation.4 | async-start | bytes 5242880 | tf_op jit(solution)/shard_map/all_gather | solution.py:979
  35.7 36.3 %collective-permute-start.3 = (bf16[144,2048]{1,0:T(8,128)(2,1)S(1)}, bf16[144,2048]{1,0:T(8,128)(2,1)}, u32[]{:S(2)}, u32[]{:S(2)}) collective-permute-start(bf16[144,2048]{1,0:T(8,128)(2,1)S(1)} %pad_maximum_fusion.9.refs_0_), channel_id=1, source_target_pairs={{0,6},{2,4},{4,2},{6,0},{1,7},{3,5},{5,3},{7,1},{8,14},{10,12},{12... | collective-permute-start | bytes 1769480 | tf_op jit(solution)/shard_map/ppermute | solution.py:35
  38.5 39.8 %collective-permute-start.2 = (bf16[144,2048]{1,0:T(8,128)(2,1)S(1)}, bf16[144,2048]{1,0:T(8,128)(2,1)}, u32[]{:S(2)}, u32[]{:S(2)}) collective-permute-start(bf16[144,2048]{1,0:T(8,128)(2,1)S(1)} %pad_maximum_fusion.9.refs_0_), channel_id=1, source_target_pairs={{0,4},{2,6},{4,0},{6,2},{1,5},{3,7},{5,1},{7,3},{8,12},{10,14},{12... | collective-permute-start | bytes 1769480 | tf_op jit(solution)/shard_map/ppermute | solution.py:35
  39.1 46.3 %collective-permute-start.1 = (bf16[144,2048]{1,0:T(8,128)(2,1)S(1)}, bf16[144,2048]{1,0:T(8,128)(2,1)}, u32[]{:S(2)}, u32[]{:S(2)}) collective-permute-start(bf16[144,2048]{1,0:T(8,128)(2,1)S(1)} %pad_maximum_fusion.9.refs_0_), channel_id=1, source_target_pairs={{0,2},{2,0},{4,6},{6,4},{1,3},{3,1},{5,7},{7,5},{8,10},{10,8},{12,... | collective-permute-start | bytes 1769480 | tf_op jit(solution)/shard_map/ppermute | solution.py:35
  42.1 48.1 %collective-permute-start.4 = (bf16[144,2048]{1,0:T(8,128)(2,1)S(1)}, bf16[144,2048]{1,0:T(8,128)(2,1)}, u32[]{:S(2)}, u32[]{:S(2)}) collective-permute-start(bf16[144,2048]{1,0:T(8,128)(2,1)S(1)} %pad_maximum_fusion.9.refs_0_), channel_id=1, source_target_pairs={{0,1},{1,0},{2,3},{3,2},{4,5},{5,4},{6,7},{7,6},{8,9},{9,8},{10,11... | collective-permute-start | bytes 1769480 | tf_op jit(solution)/shard_map/ppermute | solution.py:31
  103.4 209.3 %all-gather.5.cloned.1.call-start = ((), (), s32[]{:S(2)}) async-start(), calls=%async_computation.5 | async-start | bytes 7864320 | tf_op jit(solution)/shard_map/all_gather | solution.py:1009
  113.4 30.3 %collective-permute-start.24 = (bf16[128,2048]{1,0:T(8,128)(2,1)S(1)}, bf16[128,2048]{1,0:T(8,128)(2,1)S(1)}, u32[]{:S(2)}, u32[]{:S(2)}) collective-permute-start(bf16[128,2048]{1,0:T(8,128)(2,1)S(1)} %constant_dynamic-slice_fusion.4.refs_0_), channel_id=1, source_target_pairs={{0,1},{1,0},{2,3},{3,2},{4,5},{5,4},{6,7},{7,6},{8,9},{9,8},{10,11... | collective-permute-start | bytes 1572872 | tf_op jit(solution)/shard_map/ppermute | solution.py:31
  114.4 25.4 %collective-permute-start.22 = (bf16[128,2048]{1,0:T(8,128)(2,1)S(1)}, bf16[128,2048]{1,0:T(8,128)(2,1)}, u32[]{:S(2)}, u32[]{:S(2)}) collective-permute-start(bf16[128,2048]{1,0:T(8,128)(2,1)S(1)} %constant_dynamic-slice_fusion.4.refs_0_), channel_id=1, source_target_pairs={{0,4},{2,6},{4,0},{6,2},{1,5},{3,7},{5,1},{7,3},{8,12},{10,14},{12... | collective-permute-start | bytes 1572872 | tf_op jit(solution)/shard_map/ppermute | solution.py:35
  166.7 323.8 %reduce-scatter.3.cloned.1.call-start = ((), (), s32[]{:S(2)}) async-start(), calls=%async_computation.6 | async-start | bytes 5242880 | tf_op jit(solution)/shard_map/reduce_scatter | solution.py:1062
  175.8 33.6 %collective-permute-start.33 = (bf16[256,1024]{1,0:T(8,128)(2,1)}, bf16[256,1024]{1,0:T(8,128)(2,1)}, u32[]{:S(2)}, u32[]{:S(2)}) collective-permute-start(bf16[256,1024]{1,0:T(8,128)(2,1)} %pad_maximum_fusion.11.refs_0_), channel_id=1, source_target_pairs={{0,6},{2,4},{4,2},{6,0},{1,7},{3,5},{5,3},{7,1},{8,14},{10,12},{12... | collective-permute-start | bytes 1572872 | tf_op jit(solution)/shard_map/ppermute | solution.py:35
  176.9 36.2 %collective-permute-start.32 = (bf16[256,1024]{1,0:T(8,128)(2,1)}, bf16[256,1024]{1,0:T(8,128)(2,1)}, u32[]{:S(2)}, u32[]{:S(2)}) collective-permute-start(bf16[256,1024]{1,0:T(8,128)(2,1)} %pad_maximum_fusion.11.refs_0_), channel_id=1, source_target_pairs={{0,4},{2,6},{4,0},{6,2},{1,5},{3,7},{5,1},{7,3},{8,12},{10,14},{12... | collective-permute-start | bytes 1572872 | tf_op jit(solution)/shard_map/ppermute | solution.py:35
  178.3 34.9 %collective-permute-start.31 = (bf16[256,1024]{1,0:T(8,128)(2,1)}, bf16[256,1024]{1,0:T(8,128)(2,1)}, u32[]{:S(2)}, u32[]{:S(2)}) collective-permute-start(bf16[256,1024]{1,0:T(8,128)(2,1)} %pad_maximum_fusion.11.refs_0_), channel_id=1, source_target_pairs={{0,2},{2,0},{4,6},{6,4},{1,3},{3,1},{5,7},{7,5},{8,10},{10,8},{12,... | collective-permute-start | bytes 1572872 | tf_op jit(solution)/shard_map/ppermute | solution.py:35
  191.4 25.8 %collective-permute-start.30 = (bf16[272,384]{1,0:T(8,128)(2,1)}, bf16[272,384]{1,0:T(8,128)(2,1)}, u32[]{:S(2)}, u32[]{:S(2)}) collective-permute-start(bf16[272,384]{1,0:T(8,128)(2,1)} %pad_maximum_fusion.13), channel_id=1, source_target_pairs={{0,24},{1,25},{2,26},{3,27},{4,28},{5,29},{6,30},{7,31}} | collective-permute-start | bytes 626696 | tf_op jit(solution)/shard_map/ppermute | solution.py:46
  241.3 24.9 %collective-permute-start.36 = (bf16[128,2048]{1,0:T(8,128)(2,1)S(1)}, bf16[128,2048]{1,0:T(8,128)(2,1)S(1)}, u32[]{:S(2)}, u32[]{:S(2)}) collective-permute-start(bf16[128,2048]{1,0:T(8,128)(2,1)S(1)} %get-tuple-element.253), channel_id=1, source_target_pairs={{0,4},{2,6},{4,0},{6,2},{1,5},{3,7},{5,1},{7,3},{8,12},{10,14},{12... | collective-permute-start | bytes 1572872 | tf_op jit(solution)/shard_map/ppermute | solution.py:35
  241.3 24.9 %collective-permute-start.37 = (bf16[128,2048]{1,0:T(8,128)(2,1)S(1)}, bf16[128,2048]{1,0:T(8,128)(2,1)S(1)}, u32[]{:S(2)}, u32[]{:S(2)}) collective-permute-start(bf16[128,2048]{1,0:T(8,128)(2,1)S(1)} %get-tuple-element.254), channel_id=1, source_target_pairs={{0,6},{2,4},{4,2},{6,0},{1,7},{3,5},{5,3},{7,1},{8,14},{10,12},{12... | collective-permute-start | bytes 1572872 | tf_op jit(solution)/shard_map/ppermute | solution.py:35
  336.6 25.5 %collective-permute-start.47 = (bf16[128,2048]{1,0:T(8,128)(2,1)}, bf16[128,2048]{1,0:T(8,128)(2,1)}, u32[]{:S(2)}, u32[]{:S(2)}) collective-permute-start(bf16[128,2048]{1,0:T(8,128)(2,1)} %get-tuple-element.273), channel_id=1, source_target_pairs={{0,4},{2,6},{4,0},{6,2},{1,5},{3,7},{5,1},{7,3},{8,12},{10,14},{12... | collective-permute-start | bytes 1572872 | tf_op jit(solution)/shard_map/ppermute | solution.py:35
  362.1 266.7 %reduce-scatter.5.cloned.1.call-start = ((), (), s32[]{:S(2)}) async-start(), calls=%async_computation.7 | async-start | bytes 7864320 | tf_op jit(solution)/shard_map/reduce_scatter | solution.py:1062
  370.0 25.4 %collective-permute-start.52 = (bf16[128,2048]{1,0:T(8,128)(2,1)}, bf16[128,2048]{1,0:T(8,128)(2,1)}, u32[]{:S(2)}, u32[]{:S(2)}) collective-permute-start(bf16[128,2048]{1,0:T(8,128)(2,1)} %fusion.82.refs_0_), channel_id=1, source_target_pairs={{0,1},{1,0},{2,3},{3,2},{4,5},{5,4},{6,7},{7,6},{8,9},{9,8},{10,11... | collective-permute-start | bytes 1572872 | tf_op jit(solution)/shard_map/ppermute | solution.py:31
  408.3 38.1 %collective-permute-start.57 = (bf16[272,384]{1,0:T(8,128)(2,1)}, bf16[272,384]{1,0:T(8,128)(2,1)}, u32[]{:S(2)}, u32[]{:S(2)}) collective-permute-start(bf16[272,384]{1,0:T(8,128)(2,1)} %pad_maximum_fusion.12), channel_id=1, source_target_pairs={{16,0},{24,8},{17,1},{25,9},{18,2},{26,10},{19,3},{27,11},{20,4},{... | collective-permute-start | bytes 626696 | tf_op jit(solution)/shard_map/ppermute | solution.py:46
  425.4 48.1 %collective-permute-start.59 = (bf16[256,1024]{1,0:T(8,128)(2,1)}, bf16[256,1024]{1,0:T(8,128)(2,1)}, u32[]{:S(2)}, u32[]{:S(2)}) collective-permute-start(bf16[256,1024]{1,0:T(8,128)(2,1)} %copy-done.73), channel_id=1, source_target_pairs={{0,2},{2,0},{4,6},{6,4},{1,3},{3,1},{5,7},{7,5},{8,10},{10,8},{12,... | collective-permute-start | bytes 1572872 | tf_op jit(solution)/shard_map/ppermute | solution.py:35
  426.5 47.0 %collective-permute-start.60 = (bf16[256,1024]{1,0:T(8,128)(2,1)}, bf16[256,1024]{1,0:T(8,128)(2,1)}, u32[]{:S(2)}, u32[]{:S(2)}) collective-permute-start(bf16[256,1024]{1,0:T(8,128)(2,1)} %copy-done.72), channel_id=1, source_target_pairs={{0,4},{2,6},{4,0},{6,2},{1,5},{3,7},{5,1},{7,3},{8,12},{10,14},{12... | collective-permute-start | bytes 1572872 | tf_op jit(solution)/shard_map/ppermute | solution.py:35
  427.8 45.7 %collective-permute-start.61 = (bf16[256,1024]{1,0:T(8,128)(2,1)}, bf16[256,1024]{1,0:T(8,128)(2,1)}, u32[]{:S(2)}, u32[]{:S(2)}) collective-permute-start(bf16[256,1024]{1,0:T(8,128)(2,1)} %copy-done.71), channel_id=1, source_target_pairs={{0,6},{2,4},{4,2},{6,0},{1,7},{3,5},{5,3},{7,1},{8,14},{10,12},{12... | collective-permute-start | bytes 1572872 | tf_op jit(solution)/shard_map/ppermute | solution.py:35
  429.0 27.3 %collective-permute-start.56 = (bf16[272,384]{1,0:T(8,128)(2,1)}, bf16[272,384]{1,0:T(8,128)(2,1)}, u32[]{:S(2)}, u32[]{:S(2)}) collective-permute-start(bf16[272,384]{1,0:T(8,128)(2,1)} %pad_maximum_fusion.12), channel_id=1, source_target_pairs={{8,0},{16,8},{24,16},{9,1},{17,9},{25,17},{10,2},{18,10},{26,18},{... | collective-permute-start | bytes 626696 | tf_op jit(solution)/shard_map/ppermute | solution.py:46
  488.5 32.0 %collective-permute-start.67 = (bf16[128,2048]{1,0:T(8,128)(2,1)}, bf16[128,2048]{1,0:T(8,128)(2,1)}, u32[]{:S(2)}, u32[]{:S(2)}) collective-permute-start(bf16[128,2048]{1,0:T(8,128)(2,1)} %get-tuple-element.312), channel_id=1, source_target_pairs={{0,4},{2,6},{4,0},{6,2},{1,5},{3,7},{5,1},{7,3},{8,12},{10,14},{12... | collective-permute-start | bytes 1572872 | tf_op jit(solution)/shard_map/ppermute | solution.py:35
  489.9 31.9 %collective-permute-start.68 = (bf16[128,2048]{1,0:T(8,128)(2,1)}, bf16[128,2048]{1,0:T(8,128)(2,1)}, u32[]{:S(2)}, u32[]{:S(2)}) collective-permute-start(bf16[128,2048]{1,0:T(8,128)(2,1)} %get-tuple-element.313), channel_id=1, source_target_pairs={{0,6},{2,4},{4,2},{6,0},{1,7},{3,5},{5,3},{7,1},{8,14},{10,12},{12... | collective-permute-start | bytes 1572872 | tf_op jit(solution)/shard_map/ppermute | solution.py:35
  492.7 30.4 %collective-permute-start.65 = (bf16[128,1024]{1,0:T(8,128)(2,1)S(1)}, bf16[128,1024]{1,0:T(8,128)(2,1)S(1)}, u32[]{:S(2)}, u32[]{:S(2)}) collective-permute-start(bf16[128,1024]{1,0:T(8,128)(2,1)S(1)} %get-tuple-element.492), channel_id=1, source_target_pairs={{0,6},{2,4},{4,2},{6,0},{1,7},{3,5},{5,3},{7,1},{8,14},{10,12},{12... | collective-permute-start | bytes 786440 | tf_op jit(solution)/shard_map/ppermute | solution.py:35
  494.9 29.9 %collective-permute-start.64 = (bf16[128,1024]{1,0:T(8,128)(2,1)S(1)}, bf16[128,1024]{1,0:T(8,128)(2,1)S(1)}, u32[]{:S(2)}, u32[]{:S(2)}) collective-permute-start(bf16[128,1024]{1,0:T(8,128)(2,1)S(1)} %get-tuple-element.493), channel_id=1, source_target_pairs={{0,4},{2,6},{4,0},{6,2},{1,5},{3,7},{5,1},{7,3},{8,12},{10,14},{12... | collective-permute-start | bytes 786440 | tf_op jit(solution)/shard_map/ppermute | solution.py:35
  587.8 45.3 %collective-permute-start.87 = (bf16[512,512]{1,0:T(8,128)(2,1)}, bf16[512,512]{1,0:T(8,128)(2,1)}, u32[]{:S(2)}, u32[]{:S(2)}) collective-permute-start(bf16[512,512]{1,0:T(8,128)(2,1)} %get-tuple-element.475), channel_id=1, source_target_pairs={{0,24},{8,0},{16,8},{24,16},{1,25},{9,1},{17,9},{25,17},{2,26},{10... | collective-permute-start | bytes 1572872 | tf_op jit(solution)/shard_map/ppermute | solution.py:40
  588.9 57.5 %collective-permute-start.86 = (bf16[512,512]{1,0:T(8,128)(2,1)}, bf16[512,512]{1,0:T(8,128)(2,1)}, u32[]{:S(2)}, u32[]{:S(2)}) collective-permute-start(bf16[512,512]{1,0:T(8,128)(2,1)} %get-tuple-element.476), channel_id=1, source_target_pairs={{0,16},{8,24},{16,0},{24,8},{1,17},{9,25},{17,1},{25,9},{2,18},{10... | collective-permute-start | bytes 1572872 | tf_op jit(solution)/shard_map/ppermute | solution.py:40
  608.2 38.2 %collective-permute-start.85 = (bf16[512,512]{1,0:T(8,128)(2,1)}, bf16[512,512]{1,0:T(8,128)(2,1)}, u32[]{:S(2)}, u32[]{:S(2)}) collective-permute-start(bf16[512,512]{1,0:T(8,128)(2,1)} %get-tuple-element.477), channel_id=1, source_target_pairs={{0,8},{8,16},{16,24},{24,0},{1,9},{9,17},{17,25},{25,1},{2,10},{10... | collective-permute-start | bytes 1572872 | tf_op jit(solution)/shard_map/ppermute | solution.py:40
  624.4 37.4 %all-to-all-start.1 = ((f32[16,32,128]{2,1,0:T(8,128)}), f32[16,32,128]{2,1,0:T(8,128)S(1)}, u32[]{:S(2)}, u32[]{:S(2)}) async-start(f32[16,32,128]{2,1,0:T(8,128)} %bitcast.164), calls=%async_computation.2 | async-start | bytes 524288 | tf_op jit(solution)/shard_map/all_to_all | solution.py:96
  (246 other events, 2960.1 us)
Sparse Core Ops, SparseCore 0:
  103.5 83.8 all-gather.2
  188.9 123.6 all-gather.4
  362.2 95.1 reduce-scatter.2
  476.7 121.5 reduce-scatter.4
